TPU v7x, 32 devices: a whole 2x2x4 slice. The times are simulated.
32 devices in a mesh: frame: 8 (over z, y), patch: 4 (over x, core).
Axes of the slice: x: 2, y: 2, z: 4, core: 2. Of those that a mesh axis runs over, the one named last changes fastest.
Arguments:
- hidden_states: bfloat16 [8, 1024, 1152], P('frame', 'patch'), may hold values from -6 to 6
- mod_spatial: float32 [3, 1152], replicated, may hold values from -4 to 4
- w_spatial_qkv: bfloat16 [1152, 3456], P(None, 'patch'), may hold values from -2.5 to 2.5
- w_spatial_out: bfloat16 [1152, 1152], P('patch'), may hold values from -0.1875 to 0.1875
- mod_temporal: float32 [3, 1152], replicated, may hold values from -4 to 4
- w_temporal_qkv: bfloat16 [1152, 3456], P(None, 'frame'), may hold values from -2.5 to 2.5
- w_temporal_out: bfloat16 [1152, 1152], P('frame'), may hold values from -0.1875 to 0.1875
Outputs:
- block_out: bfloat16 [8, 1024, 1152], P('frame', 'patch')
All inputs are finite; a program needn't handle non-finite values.
Results may differ from a plain program's by a relative error of at most 0.017.
Values may be sent and summed in bfloat16 or wider, within the bound.
No kernel may reach another device: no remote copies, remote signals or barrier semaphores. Data moves between devices by JAX's collectives and lax.ppermute only.
A program may use at most 64 MiB of HBM per device.

v0:
```python
import math

import jax
import jax.numpy as jnp
from jax import lax
from jax.sharding import PartitionSpec as P

HEADS = 16
HEAD_DIM = 72


EPS = 1e-06


def modulate(tokens, mod):
    values = tokens.astype(jnp.float32)
    mean = jnp.mean(values, axis=-1, keepdims=True)
    centred = values - mean
    var = jnp.mean(centred * centred, axis=-1, keepdims=True)
    normed = centred * lax.rsqrt(var + EPS)
    return (normed * (1.0 + mod[1]) + mod[0]).astype(jnp.bfloat16)


def attend_rows(query, keys, values):
    scores = jnp.einsum(
        "qhd,khd->hqk", query, keys, preferred_element_type=jnp.float32
    ) / math.sqrt(HEAD_DIM)
    probs = jax.nn.softmax(scores, axis=-1).astype(jnp.bfloat16)
    return jnp.einsum("hqk,khd->qhd", probs, values, preferred_element_type=jnp.float32).astype(
        jnp.bfloat16
    )


def spatial_block(packed):
    frames, seq_len, heads_here, _ = packed.shape
    qkv = packed.reshape(frames, seq_len, heads_here, 3, HEAD_DIM)
    block = math.gcd(seq_len, 512)

    def one_frame(frame_qkv):
        query = frame_qkv[:, :, 0].reshape(seq_len // block, block, heads_here, HEAD_DIM)
        keys = frame_qkv[:, :, 1]
        values = frame_qkv[:, :, 2]
        result = lax.map(lambda rows: attend_rows(rows, keys, values), query)
        return result.reshape(seq_len, heads_here, HEAD_DIM)

    return lax.map(one_frame, qkv)


def temporal_block(packed):
    frames, positions, heads_here, _ = packed.shape
    qkv = packed.reshape(frames, positions, heads_here, 3, HEAD_DIM)
    scores = jnp.einsum(
        "fphd,gphd->phfg", qkv[:, :, :, 0], qkv[:, :, :, 1], preferred_element_type=jnp.float32
    ) / math.sqrt(HEAD_DIM)
    probs = jax.nn.softmax(scores, axis=-1).astype(jnp.bfloat16)
    return jnp.einsum(
        "phfg,gphd->fphd", probs, qkv[:, :, :, 2], preferred_element_type=jnp.float32
    ).astype(jnp.bfloat16)


def residual_update(tokens, update, mod):
    return (tokens.astype(jnp.float32) + mod[2] * update.reshape(tokens.shape)).astype(jnp.bfloat16)


def shards(
    hidden_states,
    mod_spatial,
    w_spatial_qkv,
    w_spatial_out,
    mod_temporal,
    w_temporal_qkv,
    w_temporal_out,
):
    frames, patches, width = hidden_states.shape
    moved = modulate(hidden_states, mod_spatial)
    flat = moved.reshape(frames * patches, width)
    qkv = jnp.dot(
        flat,
        lax.all_gather(w_spatial_qkv, "patch", axis=1, tiled=True),
        preferred_element_type=jnp.float32,
    ).astype(jnp.bfloat16)
    qkv = qkv.reshape(frames, patches, HEADS, 3 * HEAD_DIM)
    heads = spatial_block(lax.all_to_all(qkv, "patch", split_axis=2, concat_axis=1, tiled=True))
    heads = lax.all_to_all(heads, "patch", split_axis=1, concat_axis=2, tiled=True)
    head_flat = heads.reshape(frames * patches, width)
    cols = head_flat
    update = jnp.dot(
        cols,
        lax.all_gather(w_spatial_out, "patch", axis=0, tiled=True),
        preferred_element_type=jnp.float32,
    )
    after_spatial = residual_update(hidden_states, update, mod_spatial)
    moved = modulate(after_spatial, mod_temporal)
    flat = moved.reshape(frames * patches, width)
    qkv = jnp.dot(
        flat,
        lax.all_gather(w_temporal_qkv, "frame", axis=1, tiled=True),
        preferred_element_type=jnp.float32,
    ).astype(jnp.bfloat16)
    qkv = qkv.reshape(frames, patches, HEADS, 3 * HEAD_DIM)
    heads = temporal_block(lax.all_to_all(qkv, "frame", split_axis=2, concat_axis=0, tiled=True))
    heads = lax.all_to_all(heads, "frame", split_axis=0, concat_axis=2, tiled=True)
    head_flat = heads.reshape(frames * patches, width)
    cols = head_flat
    update = jnp.dot(
        cols,
        lax.all_gather(w_temporal_out, "frame", axis=0, tiled=True),
        preferred_element_type=jnp.float32,
    )
    return residual_update(after_spatial, update, mod_temporal)


def solution(mesh):
    in_specs = (
        P("frame", "patch", None),
        P(),
        P(None, "patch"),
        P("patch", None),
        P(),
        P(None, "frame"),
        P("frame", None),
    )
    out_specs = P("frame", "patch", None)
    return jax.shard_map(shards, mesh=mesh, in_specs=in_specs, out_specs=out_specs, check_vma=False)
```

profile of v0, /device:TPU:0, one launch (start us, length us, event | category | flops | bytes accessed | tf_op | source)
XLA Modules:
  0.0 338.6 jit_solution(6642813857051733817)
XLA Ops:
  6.5 0.0 all-gather.5.cloned.1.call-start
  6.5 0.0 copy-start.5
  6.5 0.0 copy-start
  6.5 0.7 all-gather.5.cloned.1.call-update
  7.3 0.0 all-gather.7.cloned.1.call-start
  7.3 0.7 all-gather.7.cloned.1.call-update
  8.0 0.0 all-gather.9.cloned.1.call-start
  8.1 0.7 all-gather.9.cloned.1.call-update
  8.7 0.0 copy-done.5
  8.8 0.0 copy-done
  8.8 0.2 convert_reduce_fusion
  9.0 0.3 fusion.39
  9.3 58.2 %all-gather.5.cloned.1.call-done = bf16[1152,3456]{0,1:T(8,128)(2,1)} async-done(((bf16[1152,864]{0,1:T(8,128)(2,1)}), bf16[1152,3456]{0,1:T(8,128)(2,1)}) %all-gather.5.cloned.1.call-update) | async-done | bytes 7962640 | tf_op jit(solution)/shard_map/all_gather | solution.py:79
  67.5 5.9 %convolution_convert_fusion.1 = bf16[256,3456]{1,0:T(8,128)(2,1)S(1)} fusion(bf16[1152,3456]{0,1:T(8,128)(2,1)} %all-gather.5.cloned.1.call-done, bf16[1,256,1152]{2,1,0:T(8,128)(2,1)S(1)} %copy-done, f32[1152]{0:T(1024)S(1)} %get-tuple-element.61, f32[1152]{0:T(1024)S(1)} %get-tuple-element.62, f32[256]{0:T(256)S(1)} %add_rsqrt_fusion.1, ...), kind=kOutput, calls=%fused_computation.21 | convolution fusion | flops 2041085952 | bytes 10333184 | tf_op jit(solution)/shard_map/dot_general | solution.py:77
  73.4 2.3 copy.33
  75.7 3.6 %all-to-all-start = ((bf16[1,256,16,216]{1,3,0,2:T(8,128)(2,1)}), bf16[1,256,16,216]{1,3,0,2:T(8,128)(2,1)S(1)}, u32[]{:S(2)}, u32[]{:S(2)}) async-start(bf16[1,256,16,216]{1,3,0,2:T(8,128)(2,1)} %bitcast.5), calls=%async_computation | async-start | bytes 3538944 | tf_op jit(solution)/shard_map/all_to_all | solution.py:83
  79.3 33.0 %all-to-all-done = bf16[1,256,16,216]{1,3,0,2:T(8,128)(2,1)S(1)} async-done(((bf16[1,256,16,216]{1,3,0,2:T(8,128)(2,1)}), bf16[1,256,16,216]{1,3,0,2:T(8,128)(2,1)S(1)}, u32[]{:S(2)}, u32[]{:S(2)}) %all-to-all-start) | async-done | bytes 1769504 | tf_op jit(solution)/shard_map/all_to_all | solution.py:83
  112.3 1.4 copy.35
  113.6 1.3 squeeze.32
  114.9 0.2 slice_bitcast_fusion
  115.1 0.0 copy-start.4
  115.1 0.4 squeeze.33
  115.5 0.1 copy.36
  115.6 0.6 copy-done.4
  116.2 19.7 %while.17 = (s32[]{:T(128)}, bf16[2,512,4,72]{1,3,2,0:T(8,128)(2,1)S(1)}, bf16[2,512,4,72]{1,3,2,0:T(8,128)(2,1)S(1)}, bf16[1024,4,72]{0,2,1:T(8,128)(2,1)S(1)}, bf16[1024,4,72]{0,2,1:T(8,128)(2,1)S(1)}, /*index=5*/s32[]{:T(128)}) while((s32[]{:T(128)}, bf16[2,512,4,72]{1,3,2,0:T(8,128)(2,1)S(1)}, bf16[2,512,4,72]{1,3,2,0:T(8,128)(2,1)S(1)}, ...), condition=%wide.region_5.0_spmd, body=%wide.region_2.5_spmd.sunk | while | flops 614614016 | bytes 18563148 | solution.py:43
  116.2 4.9 %fusion.103 = (f32[4,512]{1,0:T(4,128)S(1)}, f32[4,512,1024]{2,1,0:T(8,128)}) fusion(bf16[1024,4,72]{0,2,1:T(8,128)(2,1)S(1)} %get-tuple-element.135, bf16[2,512,4,72]{1,3,2,0:T(8,128)(2,1)S(1)} %get-tuple-element.134, s32[]{:T(128)} %get-tuple-element.126), kind=kOutput, calls=%fused_computation.76.clone.1 | convolution fusion | flops 308282368 | bytes 9281540 | tf_op jit(solution)/shard_map/while/body/eval_jaxpr/while/body/eval_jaxpr/sub | solution.py:28
  121.2 4.9 %fusion.104 = bf16[2,512,4,72]{1,3,2,0:T(8,128)(2,1)S(1)} fusion(bf16[2,512,4,72]{1,3,2,0:T(8,128)(2,1)S(1)} %get-tuple-element.127, s32[]{:T(128)} %get-tuple-element.126, bf16[1024,4,72]{0,2,1:T(8,128)(2,1)S(1)} %get-tuple-element.136, f32[4,512,1024]{2,1,0:T(8,128)} %get-tuple-element.118, f32[4,512]{1,0:T(4,128)S(1)} %get-tuple-element.119), kind=kOutput, calls=%fused_computation.9.clone.1 | convolution fusion | flops 306331648 | bytes 9281540 | tf_op jit(solution)/shard_map/while/body/eval_jaxpr/while/body/eval_jaxpr/hqk,khd->qhd/dot_general | solution.py:29
  126.0 5.0 %fusion.103 = (f32[4,512]{1,0:T(4,128)S(1)}, f32[4,512,1024]{2,1,0:T(8,128)}) fusion(bf16[1024,4,72]{0,2,1:T(8,128)(2,1)S(1)} %get-tuple-element.135, bf16[2,512,4,72]{1,3,2,0:T(8,128)(2,1)S(1)} %get-tuple-element.134, s32[]{:T(128)} %get-tuple-element.126), kind=kOutput, calls=%fused_computation.76.clone.1 | convolution fusion | flops 308282368 | bytes 9281540 | tf_op jit(solution)/shard_map/while/body/eval_jaxpr/while/body/eval_jaxpr/sub | solution.py:28
  131.0 4.9 %fusion.104 = bf16[2,512,4,72]{1,3,2,0:T(8,128)(2,1)S(1)} fusion(bf16[2,512,4,72]{1,3,2,0:T(8,128)(2,1)S(1)} %get-tuple-element.127, s32[]{:T(128)} %get-tuple-element.126, bf16[1024,4,72]{0,2,1:T(8,128)(2,1)S(1)} %get-tuple-element.136, f32[4,512,1024]{2,1,0:T(8,128)} %get-tuple-element.118, f32[4,512]{1,0:T(4,128)S(1)} %get-tuple-element.119), kind=kOutput, calls=%fused_computation.9.clone.1 | convolution fusion | flops 306331648 | bytes 9281540 | tf_op jit(solution)/shard_map/while/body/eval_jaxpr/while/body/eval_jaxpr/hqk,khd->qhd/dot_general | solution.py:29
  135.9 0.0 copy-start.6
  135.9 1.4 copy.49
  137.3 3.7 %all-to-all-start.1 = ((bf16[1,1024,4,72]{3,2,0,1:T(4,128)(2,1)}), bf16[1,1024,4,72]{3,2,0,1:T(4,128)(2,1)S(1)}, u32[]{:S(2)}, u32[]{:S(2)}) async-start(bf16[1,1024,4,72]{3,2,0,1:T(4,128)(2,1)} %bitcast.10), calls=%async_computation.1 | async-start | bytes 2097152 | tf_op jit(solution)/shard_map/all_to_all | solution.py:84
  141.0 0.0 copy-done.6
  141.1 0.0 copy-start.1
  141.1 14.2 %all-to-all-done.1 = bf16[1,1024,4,72]{3,2,0,1:T(4,128)(2,1)S(1)} async-done(((bf16[1,1024,4,72]{3,2,0,1:T(4,128)(2,1)}), bf16[1,1024,4,72]{3,2,0,1:T(4,128)(2,1)S(1)}, u32[]{:S(2)}, u32[]{:S(2)}) %all-to-all-start.1) | async-done | bytes 589856 | tf_op jit(solution)/shard_map/all_to_all | solution.py:84
  155.3 0.8 copy.50
  156.1 0.1 copy.40
  156.2 0.0 all-gather.7.cloned.1.call-done
  156.2 0.0 copy-done.1
  156.2 3.1 fusion.80
  159.3 0.0 copy-start.2
  159.3 0.3 multiply_reduce_fusion.2
  159.6 68.2 %all-gather.9.cloned.1.call-done = bf16[1152,3456]{0,1:T(8,128)(2,1)} async-done(((bf16[1152,432]{0,1:T(8,128)(2,1)}), bf16[1152,3456]{0,1:T(8,128)(2,1)}) %all-gather.9.cloned.1.call-update) | async-done | bytes 7962640 | tf_op jit(solution)/shard_map/all_gather | solution.py:97
  227.9 5.9 %convolution_convert_fusion = bf16[256,3456]{1,0:T(8,128)(2,1)S(1)} fusion(bf16[1152,3456]{0,1:T(8,128)(2,1)} %all-gather.9.cloned.1.call-done, f32[1,256,1152]{2,1,0:T(8,128)S(1)} %get-tuple-element.82, f32[1152]{0:T(1024)S(1)} %get-tuple-element.58, f32[1152]{0:T(1024)S(1)} %get-tuple-element.59, f32[256]{0:T(256)S(1)} %add_rsqrt_fusion, ...), kind=kOutput, calls=%fused_computation.20 | convolution fusion | flops 2040791040 | bytes 10923008 | tf_op jit(solution)/shard_map/dot_general | solution.py:95
  233.8 0.0 copy-done.2
  233.8 2.2 copy.41
  236.0 3.6 %all-to-all-start.2 = ((bf16[1,256,16,216]{1,3,0,2:T(8,128)(2,1)}), bf16[1,256,16,216]{1,3,0,2:T(8,128)(2,1)S(1)}, u32[]{:S(2)}, u32[]{:S(2)}) async-start(bf16[1,256,16,216]{1,3,0,2:T(8,128)(2,1)} %bitcast.17), calls=%async_computation.2 | async-start | bytes 3538944 | tf_op jit(solution)/shard_map/all_to_all | solution.py:101
  239.6 0.0 all-gather.11.cloned.1.call-start
  239.6 0.5 all-gather.11.cloned.1.call-update
  240.2 51.1 %all-to-all-done.2 = bf16[1,256,16,216]{1,3,0,2:T(8,128)(2,1)S(1)} async-done(((bf16[1,256,16,216]{1,3,0,2:T(8,128)(2,1)}), bf16[1,256,16,216]{1,3,0,2:T(8,128)(2,1)S(1)}, u32[]{:S(2)}, u32[]{:S(2)}) %all-to-all-start.2) | async-done | bytes 1769504 | tf_op jit(solution)/shard_map/all_to_all | solution.py:101
  291.3 0.1 fusion.79
  291.4 1.0 copy.53
  292.4 1.7 copy.54
  294.2 1.0 copy.52
  295.2 5.0 %fusion.81 = (f32[256,2,8]{2,1,0:T(2,128)}, f32[256,2,8,8]{2,3,1,0:T(8,128)}) fusion(bf16[8,256,2,1,72]{4,0,2,1,3:T(8,128)(2,1)} %copy.54, bf16[8,256,2,1,72]{4,0,2,1,3:T(8,128)(2,1)S(1)} %copy.53), kind=kOutput, calls=%fused_computation.79 | convolution fusion | flops 4816903 | bytes 1327104 | tf_op jit(solution)/shard_map/sub | solution.py:55
  300.2 2.4 fusion.38
  302.6 0.0 copy-start.3
  302.6 1.5 copy.47
  304.1 4.7 %all-to-all-start.3 = ((bf16[8,256,2,72]{1,3,2,0:T(8,128)(2,1)}), bf16[8,256,2,72]{1,3,2,0:T(8,128)(2,1)S(1)}, u32[]{:S(2)}, u32[]{:S(2)}) async-start(bf16[8,256,2,72]{1,3,2,0:T(8,128)(2,1)} %copy.47), calls=%async_computation.3 | async-start | bytes 1179648 | tf_op jit(solution)/shard_map/all_to_all | solution.py:102
  308.7 10.6 %all-gather.11.cloned.1.call-done = bf16[1152,1152]{1,0:T(8,128)(2,1)} async-done(((bf16[144,1152]{1,0:T(8,128)(2,1)}), bf16[1152,1152]{1,0:T(8,128)(2,1)}) %all-gather.11.cloned.1.call-update) | async-done | bytes 2654224 | tf_op jit(solution)/shard_map/all_gather | solution.py:107
  319.3 9.1 %all-to-all-done.3 = bf16[8,256,2,72]{1,3,2,0:T(8,128)(2,1)S(1)} async-done(((bf16[8,256,2,72]{1,3,2,0:T(8,128)(2,1)}), bf16[8,256,2,72]{1,3,2,0:T(8,128)(2,1)S(1)}, u32[]{:S(2)}, u32[]{:S(2)}) %all-to-all-start.3) | async-done | bytes 589856 | tf_op jit(solution)/shard_map/all_to_all | solution.py:102
  328.5 0.0 copy-done.3
  328.5 3.6 %fusion.32 = bf16[1,256,1152]{2,1,0:T(8,128)(2,1)} fusion(f32[1,256,1152]{2,1,0:T(8,128)S(1)} %copy-done.3, bf16[256,1152]{0,1:T(8,128)(2,1)S(1)} %bitcast.120, bf16[1152,1152]{1,0:T(8,128)(2,1)} %all-gather.11.cloned.1.call-done, f32[1152]{0:T(1024)S(1)} %get-tuple-element.57), kind=kOutput, calls=%fused_computation.28 | convolution fusion | flops 680361984 | bytes 5018112 | tf_op jit(solution)/shard_map/dot_general | solution.py:105
  (7 shorter events, 0.1 us)
Async XLA Ops:
  6.5 61.0 %all-gather.5.cloned.1.call-start = ((), (), s32[]{:S(2)}) async-start(), calls=%async_computation.4 | async-start | bytes 9953280 | tf_op jit(solution)/shard_map/all_gather | solution.py:79
  6.5 2.2 copy-start.5
  6.5 2.3 copy-start
  7.3 149.0 %all-gather.7.cloned.1.call-start = ((), (), s32[]{:S(2)}) async-start(), calls=%async_computation.5 | async-start | bytes 3317760 | tf_op jit(solution)/shard_map/all_gather | solution.py:89
  8.0 219.8 %all-gather.9.cloned.1.call-start = ((), (), s32[]{:S(2)}) async-start(), calls=%async_computation.6 | async-start | bytes 8957952 | tf_op jit(solution)/shard_map/all_gather | solution.py:97
  75.7 36.6 %all-to-all-start = ((bf16[1,256,16,216]{1,3,0,2:T(8,128)(2,1)}), bf16[1,256,16,216]{1,3,0,2:T(8,128)(2,1)S(1)}, u32[]{:S(2)}, u32[]{:S(2)}) async-start(bf16[1,256,16,216]{1,3,0,2:T(8,128)(2,1)} %bitcast.5), calls=%async_computation | async-start | bytes 3538944 | tf_op jit(solution)/shard_map/all_to_all | solution.py:83
  115.1 1.1 copy-start.4
  135.9 5.2 %copy-start.6 = (f32[3,1152]{1,0:T(4,128)S(1)}, f32[3,1152]{1,0:T(4,128)}, u32[]{:S(2)}) copy-start(f32[3,1152]{1,0:T(4,128)} %param.13) | copy-start | bytes 41476
  137.3 18.0 %all-to-all-start.1 = ((bf16[1,1024,4,72]{3,2,0,1:T(4,128)(2,1)}), bf16[1,1024,4,72]{3,2,0,1:T(4,128)(2,1)S(1)}, u32[]{:S(2)}, u32[]{:S(2)}) async-start(bf16[1,1024,4,72]{3,2,0,1:T(4,128)(2,1)} %bitcast.10), calls=%async_computation.1 | async-start | bytes 2097152 | tf_op jit(solution)/shard_map/all_to_all | solution.py:84
  141.1 15.2 %copy-start.1 = (bf16[1,256,1152]{2,1,0:T(8,128)(2,1)S(1)}, bf16[1,256,1152]{2,1,0:T(8,128)(2,1)}, u32[]{:S(2)}) copy-start(bf16[1,256,1152]{2,1,0:T(8,128)(2,1)} %param.9) | copy-start | bytes 1769476
  159.3 74.4 %copy-start.2 = (f32[1,256,1152]{2,1,0:T(8,128)}, f32[1,256,1152]{2,1,0:T(8,128)S(1)}, u32[]{:S(2)}) copy-start(f32[1,256,1152]{2,1,0:T(8,128)S(1)} %get-tuple-element.82) | copy-start | bytes 3538948
  236.0 55.3 %all-to-all-start.2 = ((bf16[1,256,16,216]{1,3,0,2:T(8,128)(2,1)}), bf16[1,256,16,216]{1,3,0,2:T(8,128)(2,1)S(1)}, u32[]{:S(2)}, u32[]{:S(2)}) async-start(bf16[1,256,16,216]{1,3,0,2:T(8,128)(2,1)} %bitcast.17), calls=%async_computation.2 | async-start | bytes 3538944 | tf_op jit(solution)/shard_map/all_to_all | solution.py:101
  239.6 79.7 %all-gather.11.cloned.1.call-start = ((), (), s32[]{:S(2)}) async-start(), calls=%async_computation.7 | async-start | bytes 2985984 | tf_op jit(solution)/shard_map/all_gather | solution.py:107
  302.6 25.9 %copy-start.3 = (f32[1,256,1152]{2,1,0:T(8,128)S(1)}, f32[1,256,1152]{2,1,0:T(8,128)}, u32[]{:S(2)}) copy-start(f32[1,256,1152]{2,1,0:T(8,128)} %copy-done.2) | copy-start | bytes 3538948
  304.1 24.4 %all-to-all-start.3 = ((bf16[8,256,2,72]{1,3,2,0:T(8,128)(2,1)}), bf16[8,256,2,72]{1,3,2,0:T(8,128)(2,1)S(1)}, u32[]{:S(2)}, u32[]{:S(2)}) async-start(bf16[8,256,2,72]{1,3,2,0:T(8,128)(2,1)} %copy.47), calls=%async_computation.3 | async-start | bytes 1179648 | tf_op jit(solution)/shard_map/all_to_all | solution.py:102
Sparse Core Ops, SparseCore 0:
  8.9 58.5 all-gather.4
  69.1 36.6 all-gather.6
  107.9 119.8 all-gather.8
  242.3 76.9 all-gather.10
where the time goes:
time: 339 us
  waiting for transfers between devices  247 us (73%)
  matrix products  45.5 us (13%)
  local copies, waits for them, and re-layouts  16.1 us (5%)
  starting transfers between devices  15.6 us (5%)
  between operations  13.4 us (4%)
    all_gather x1, waiting for transfers between devices, shards(): lax.all_gather(w_temporal_qkv, 'frame', axis=1, tiled=True)  68.2 us
    all_gather x1, waiting for transfers between devices, shards(): lax.all_gather(w_spatial_qkv, 'patch', axis=1, tiled=True)  58.2 us
    all_to_all x1, waiting for transfers between devices, shards(): lax.all_to_all(qkv, 'frame', split_axis=2, concat_axis=0, tiled=True)  51.1 us
    all_to_all x1, waiting for transfers between devices, shards(): lax.all_to_all(qkv, 'patch', split_axis=2, concat_axis=1, tiled=True)  33 us
    all_to_all x1, waiting for transfers between devices, shards(): lax.all_to_all(heads, 'patch', split_axis=1, concat_axis=2, tiled=True)  14.2 us
    all_gather x1, waiting for transfers between devices, shards(): lax.all_gather(w_temporal_out, 'frame', axis=0, tiled=True)  10.6 us
    sub x2, matrix products, attend_rows(): probs = jax.nn.softmax(scores, axis=-1).astype(jnp.bfloat16)  9.9 us
    dot_general x2, matrix products, attend_rows(): jnp.einsum('hqk,khd->qhd', probs, values, preferred_element_type=jnp.floa...  9.72 us
  transfers between devices with their start and end apart: 8, of which 7 were waited for; matrix products, arithmetic and copies ran while one was open for 15% of the time, Pallas kernels for 0%

commit v1 on v0

v1 whole, which is shorter than its diff:
```python
import math

import jax
import jax.numpy as jnp
from jax import lax
from jax.experimental import pallas as pl
from jax.experimental.pallas import tpu as pltpu
from jax.sharding import PartitionSpec as P

HEADS = 16
HEAD_DIM = 72
PAD_DIM = 80
EPS = 1e-06
QUERY_SCALE = math.log2(math.e) / math.sqrt(HEAD_DIM)
QKV_ROWS = 224
VMEM_LIMIT = 24 * 1024 * 1024
LARGE_VMEM_LIMIT = 51 * 1024 * 1024
MEDIUM = pl.CostEstimate(flops=3 << 29, bytes_accessed=1, transcendentals=0)
SMALL = pl.CostEstimate(flops=1, bytes_accessed=1, transcendentals=0)

TRANSPOSED_RHS = (((1,), (1,)), ((), ()))
PLAIN = (((1,), (0,)), ((), ()))


def dot(lhs, rhs, dims=PLAIN):
    return lax.dot_general(lhs, rhs, dims, preferred_element_type=jnp.float32)


def normalise(tokens, mod_ref):
    values = tokens.astype(jnp.float32)
    mean = jnp.mean(values, axis=-1, keepdims=True)
    centred = values - mean
    var = jnp.mean(centred * centred, axis=-1, keepdims=True)
    normed = centred * lax.rsqrt(var + EPS)
    return (normed * (1.0 + mod_ref[1:2, :]) + mod_ref[0:1, :]).astype(jnp.bfloat16)


def split_head(columns):
    count = columns.shape[1]
    zeros = jnp.zeros((PAD_DIM - HEAD_DIM, count), jnp.float32)
    row = lax.broadcasted_iota(jnp.int32, (PAD_DIM - HEAD_DIM, count), 0)
    ones = jnp.where(row == 0, 1.0, 0.0).astype(jnp.float32)
    query = jnp.concatenate([columns[:HEAD_DIM] * QUERY_SCALE, zeros], axis=0)
    keys = jnp.concatenate([columns[HEAD_DIM : 2 * HEAD_DIM], zeros], axis=0)
    values = jnp.concatenate([columns[2 * HEAD_DIM :], ones], axis=0)
    return (
        query.astype(jnp.bfloat16),
        keys.T.astype(jnp.bfloat16),
        values.astype(jnp.bfloat16),
    )


def qkv_kernel(tokens_ref, mod_ref, weight_ref, qv_ref, keys_ref):
    moved = normalise(tokens_ref[...], mod_ref)
    columns = dot(weight_ref[...], moved, TRANSPOSED_RHS)
    for head in range(keys_ref.shape[0]):
        query, keys, values = split_head(
            columns[head * 3 * HEAD_DIM : (head + 1) * 3 * HEAD_DIM]
        )
        qv_ref[2 * head] = query
        qv_ref[2 * head + 1] = values
        keys_ref[head] = keys


def spatial_qkv(tokens, mod, weight, cost=SMALL):
    count, width = tokens.shape
    heads_here = weight.shape[0] // (3 * HEAD_DIM)
    return pl.pallas_call(
        qkv_kernel,
        out_shape=(
            jax.ShapeDtypeStruct((2 * heads_here, PAD_DIM, count), jnp.bfloat16),
            jax.ShapeDtypeStruct((heads_here, count, PAD_DIM), jnp.bfloat16),
        ),
        compiler_params=pltpu.CompilerParams(vmem_limit_bytes=VMEM_LIMIT),
        cost_estimate=cost,
        name="spatial_qkv",
    )(tokens, mod, weight)


def attention_kernel(parts, query_ref, *refs):
    qv_refs, keys_refs, out_ref, scratch = refs[:parts], refs[parts : 2 * parts], refs[-2], refs[-1]
    count = query_ref.shape[2]
    for head in range(keys_refs[0].shape[0]):
        query = query_ref[2 * head]
        scores = [dot(keys[head], query) for keys in keys_refs]
        top = jnp.max(scores[0], axis=0, keepdims=True)
        for block in scores[1:]:
            top = jnp.maximum(top, jnp.max(block, axis=0, keepdims=True))
        total = jnp.zeros((PAD_DIM, count), jnp.float32)
        for block, qv in zip(scores, qv_refs):
            probs = jnp.exp2(block - top).astype(jnp.bfloat16)
            total = total + dot(qv[2 * head + 1], probs)
        scratch[pl.ds(head * HEAD_DIM, HEAD_DIM), :] = (
            total[:HEAD_DIM] / total[HEAD_DIM : HEAD_DIM + 1]
        )
    out_ref[...] = scratch[...].T.astype(jnp.bfloat16)


def spatial_attention(query, qv_parts, keys_parts):
    heads_here, count, _ = keys_parts[0].shape
    parts = len(qv_parts)
    width = heads_here * HEAD_DIM
    return pl.pallas_call(
        lambda *refs: attention_kernel(parts, *refs),
        out_shape=jax.ShapeDtypeStruct((count, width), jnp.bfloat16),
        scratch_shapes=[pltpu.VMEM((width, count), jnp.float32)],
        compiler_params=pltpu.CompilerParams(vmem_limit_bytes=VMEM_LIMIT),
        cost_estimate=SMALL,
        name="spatial_attention",
    )(query, *qv_parts, *keys_parts)


def partial_kernel(heads_ref, other_ref, weight_ref, other_weight_ref, result_ref):
    total = dot(heads_ref[...], weight_ref[...]) + dot(other_ref[...], other_weight_ref[...])
    result_ref[...] = total.astype(jnp.bfloat16)


def chip_partial(heads, other, weight, other_weight):
    return pl.pallas_call(
        partial_kernel,
        out_shape=jax.ShapeDtypeStruct((heads.shape[0], weight.shape[1]), jnp.bfloat16),
        compiler_params=pltpu.CompilerParams(vmem_limit_bytes=VMEM_LIMIT),
        cost_estimate=SMALL,
        name="chip_partial",
    )(heads, other, weight, other_weight)


def base_kernel(tokens_ref, mod_ref, heads_ref, other_ref, weight_ref, other_weight_ref, base_ref):
    total = dot(heads_ref[...], weight_ref[...]) + dot(other_ref[...], other_weight_ref[...])
    base_ref[...] = tokens_ref[...].astype(jnp.float32) + mod_ref[2:3, :] * total


def spatial_base(tokens, mod, heads, other, weight, other_weight):
    return pl.pallas_call(
        base_kernel,
        out_shape=jax.ShapeDtypeStruct(tokens.shape, jnp.float32),
        compiler_params=pltpu.CompilerParams(vmem_limit_bytes=VMEM_LIMIT),
        cost_estimate=SMALL,
        name="spatial_base",
    )(tokens, mod, heads, other, weight, other_weight)


def add_kernel(base_ref, mod_ref, *refs):
    total = refs[0][...].astype(jnp.float32)
    for partial_ref in refs[1:-1]:
        total = total + partial_ref[...].astype(jnp.float32)
    refs[-1][...] = (base_ref[...] + mod_ref[2:3, :] * total).astype(jnp.bfloat16)


def spatial_add(base, mod, partials):
    return pl.pallas_call(
        add_kernel,
        out_shape=jax.ShapeDtypeStruct(base.shape, jnp.bfloat16),
        compiler_params=pltpu.CompilerParams(vmem_limit_bytes=VMEM_LIMIT),
        cost_estimate=MEDIUM,
        name="spatial_add",
    )(base, mod, *partials)


def pack_kernel(place_ref, qkv_ref, out_ref, *head_refs):
    count = len(head_refs)
    zeros = jnp.zeros((PAD_DIM - HEAD_DIM, qkv_ref.shape[1]), jnp.bfloat16)
    for first in range(count):

        @pl.when(place_ref[0] == first)
        def _():
            for index, head_ref in enumerate(head_refs):
                head = first ^ index
                head_ref[...] = jnp.concatenate(
                    [
                        qkv_ref[head * 3 * HEAD_DIM : (head + 1) * 3 * HEAD_DIM],
                        zeros,
                        out_ref[head * HEAD_DIM : (head + 1) * HEAD_DIM],
                        zeros,
                    ],
                    axis=0,
                )


def pack(place, qkv, out):
    count = out.shape[0] // HEAD_DIM
    if count == 1:
        place = jnp.zeros((1,), jnp.int32)
    return pl.pallas_call(
        pack_kernel,
        out_shape=(jax.ShapeDtypeStruct((QKV_ROWS + PAD_DIM, out.shape[1]), jnp.bfloat16),) * count,
        in_specs=[pl.BlockSpec(memory_space=pltpu.SMEM)]
        + [pl.BlockSpec(memory_space=pltpu.VMEM)] * 2,
        compiler_params=pltpu.CompilerParams(vmem_limit_bytes=VMEM_LIMIT),
        cost_estimate=SMALL,
        name="pack",
    )(place, qkv, out)


def temporal_kernel(positions, group, tokens_ref, moved_ref, mod_ref, *refs):
    head_refs = refs[:HEADS]
    result_ref, heads_scratch, qkv_scratch, out_scratch, sems = refs[HEADS:]
    copies = []
    for index, ref in enumerate(head_refs):
        copies.append(
            pltpu.make_async_copy(
                ref.at[pl.ds(0, QKV_ROWS)],
                qkv_scratch.at[pl.ds(index * QKV_ROWS, QKV_ROWS)],
                sems.at[index],
            )
        )
    for index, ref in enumerate(head_refs):
        copies.append(
            pltpu.make_async_copy(
                ref.at[pl.ds(QKV_ROWS, PAD_DIM)],
                out_scratch.at[pl.ds(index * PAD_DIM, PAD_DIM)],
                sems.at[HEADS + index],
            )
        )
    for copy in copies[: 2 * group]:
        copy.start()

    tokens = tokens_ref[...]
    count = tokens.shape[0]
    moved = moved_ref[...]
    key_pos = lax.broadcasted_iota(jnp.int32, (count, count), 0) % positions
    query_pos = lax.broadcasted_iota(jnp.int32, (count, count), 1) % positions
    same = key_pos == query_pos
    zeros = jnp.zeros((PAD_DIM - HEAD_DIM, count), jnp.float32)

    def project(first):
        for copy in copies[first + 2 * group : first + 3 * group]:
            copy.start()
        for index in range(first, first + group):
            copies[index].wait()
        rows = qkv_scratch[pl.ds(first * QKV_ROWS, group * QKV_ROWS), :]
        return dot(rows, moved, TRANSPOSED_RHS)

    columns = project(0)
    for first in range(0, HEADS, group):
        here = columns
        if first + group < HEADS:
            columns = project(first + group)
        split = [
            split_head(here[QKV_ROWS * k : QKV_ROWS * k + 3 * HEAD_DIM]) for k in range(group)
        ]
        scores = [jnp.where(same, dot(keys, query), -jnp.inf) for query, keys, _ in split]
        probs = [
            jnp.exp2(block - jnp.max(block, axis=0, keepdims=True)).astype(jnp.bfloat16)
            for block in scores
        ]
        mixed = [dot(values, block) for (_, _, values), block in zip(split, probs)]
        for index, block in enumerate(mixed):
            heads_scratch[pl.ds((first + index) * PAD_DIM, PAD_DIM), :] = jnp.concatenate(
                [block[:HEAD_DIM] / block[HEAD_DIM : HEAD_DIM + 1], zeros], axis=0
            )
    for copy in copies[HEADS + 2 * group :]:
        copy.start()
    for copy in copies[HEADS:]:
        copy.wait()
    total = dot(heads_scratch[...].T.astype(jnp.bfloat16), out_scratch[...])
    result_ref[...] = (tokens.astype(jnp.float32) + mod_ref[2:3, :] * total).astype(jnp.bfloat16)


def norm_kernel(tokens_ref, mod_ref, moved_ref):
    moved_ref[...] = normalise(tokens_ref[...], mod_ref)


def temporal_norm(tokens, mod):
    return pl.pallas_call(
        norm_kernel,
        out_shape=jax.ShapeDtypeStruct(tokens.shape, jnp.bfloat16),
        compiler_params=pltpu.CompilerParams(vmem_limit_bytes=VMEM_LIMIT),
        cost_estimate=SMALL,
        name="temporal_norm",
    )(tokens, mod)


def temporal_block(tokens, moved, mod, weights, positions):
    count, width = tokens.shape
    return pl.pallas_call(
        lambda *refs: temporal_kernel(positions, 2, *refs),
        out_shape=jax.ShapeDtypeStruct((count, width), jnp.bfloat16),
        in_specs=[pl.BlockSpec(memory_space=pltpu.VMEM)] * 3
        + [pl.BlockSpec(memory_space=pl.ANY)] * HEADS,
        scratch_shapes=[
            pltpu.VMEM((HEADS * PAD_DIM, count), jnp.float32),
            pltpu.VMEM((HEADS * QKV_ROWS, width), jnp.bfloat16),
            pltpu.VMEM((HEADS * PAD_DIM, width), jnp.bfloat16),
            pltpu.SemaphoreType.DMA((2 * HEADS,)),
        ],
        compiler_params=pltpu.CompilerParams(vmem_limit_bytes=LARGE_VMEM_LIMIT),
        cost_estimate=SMALL,
        name="temporal_block",
    )(tokens, moved, mod, *weights)


def swap(array, offset, count):
    return lax.ppermute(array, "patch", [(rank, rank ^ offset) for rank in range(count)])


def ring_step(array, frame_count, patch_count):
    order = list(range(0, frame_count, 2)) + list(range(1, frame_count, 2))[::-1]
    pairs = []
    for place, frame in enumerate(order):
        right, left = order[(place + 1) % frame_count], order[place - 1]
        for patch in range(patch_count):
            target = left if patch % 2 else right
            pairs.append((frame * patch_count + patch, target * patch_count + patch))
    return lax.ppermute(array, ("frame", "patch"), pairs)


def make_shards(frame_count, patch_count):
    def hop(array):
        return ring_step(array, frame_count, patch_count)

    def over_cores(array):
        return swap(array, 1, patch_count)

    def exchange(tokens):
        pieces = tokens.reshape(frame_count, -1, tokens.shape[-1])
        pieces = lax.all_to_all(pieces, "frame", 0, 0, tiled=True)
        return pieces.reshape(tokens.shape)

    def shards(
        hidden_states,
        mod_spatial,
        w_spatial_qkv,
        w_spatial_out,
        mod_temporal,
        w_temporal_qkv,
        w_temporal_out,
    ):
        _, patches, width = hidden_states.shape
        barrier = lax.optimization_barrier
        near = range(2, patch_count, 2)
        steps = frame_count // 2
        patch = lax.axis_index("patch").astype(jnp.int32)
        place = ((patch ^ (patch >> 1)) & 1).reshape(1)
        place, hidden_states = barrier((place, hidden_states))
        tokens = hidden_states.reshape(patches, width)
        w_qkv = w_spatial_qkv.T

        gathered = [tokens] * patch_count
        for offset in near:
            gathered[offset] = swap(tokens, offset, patch_count)
        gathered[1] = swap(tokens, 1, patch_count)
        weights = list(pack(place, w_temporal_qkv.T, w_temporal_out))
        first = [hop(array) for array in weights]
        other_out = over_cores(w_spatial_out)
        qkv = [None] * patch_count
        for offset in range(2):
            qkv[offset] = spatial_qkv(gathered[offset], mod_spatial, w_qkv)
        qkv[:2] = barrier(qkv[:2])
        gathered, qkv[:2] = barrier((gathered, qkv[:2]))

        for offset in near:
            gathered[offset + 1] = over_cores(gathered[offset])
        qkv[2] = spatial_qkv(gathered[2], mod_spatial, w_qkv, MEDIUM)
        qkv[2], first[0] = barrier((qkv[2], first[0]))

        second = [hop(first[0])]
        for offset in range(3, patch_count):
            qkv[offset] = spatial_qkv(gathered[offset], mod_spatial, w_qkv)
        qkv, other_out = barrier((qkv, other_out))

        qv, keys = zip(*qkv)
        heads = [None] * patch_count
        for offset in near:
            heads[offset + 1] = spatial_attention(qv[offset + 1], qv, keys)
        heads, qv, keys, first = barrier((heads, qv, keys, first))

        for offset in near:
            heads[offset + 1] = over_cores(heads[offset + 1])
            heads[offset] = spatial_attention(qv[offset], qv, keys)
        partials = [
            chip_partial(heads[offset], heads[offset + 1], w_spatial_out, other_out)
            for offset in near
        ]
        partials, qv, keys = barrier((partials, qv, keys))

        partials = [swap(partial, offset, patch_count) for partial, offset in zip(partials, near)]
        heads[1] = spatial_attention(qv[1], qv, keys)
        heads[1], qv, keys, second[0], first = barrier((heads[1], qv, keys, second[0], first))

        third = hop(second[0])
        second += [hop(array) for array in first[1:]]
        heads[0] = spatial_attention(qv[0], qv, keys)
        heads[:2] = barrier(heads[:2])

        heads[1] = over_cores(heads[1])
        base = spatial_base(tokens, mod_spatial, heads[0], heads[1], w_spatial_out, other_out)
        base, first, second[0] = barrier((base, first, second[0]))

        after_spatial = spatial_add(base, mod_spatial, partials)
        after_spatial, third = barrier((after_spatial, third))

        fourth = hop(third)
        if len(first) == 2:
            third_far = swap(third, 2, patch_count)
        arrived = exchange(after_spatial)
        moved = temporal_norm(arrived, mod_temporal)
        rest = first + second + [third]
        if len(first) == 2:
            rest += [third_far, fourth]
        else:
            for _ in range(4, steps):
                rest.append(fourth)
                fourth = hop(fourth)
            weights.append(fourth)
        for array in rest:
            weights += [array, over_cores(array)]
        result = temporal_block(arrived, moved, mod_temporal, weights, patches // frame_count)
        return exchange(result).reshape(1, patches, width)

    return shards


def solution(mesh):
    in_specs = (
        P("frame", "patch", None),
        P(),
        P(None, "patch"),
        P("patch", None),
        P(),
        P(None, "frame"),
        P("frame", None),
    )
    out_specs = P("frame", "patch", None)
    shards = make_shards(mesh.shape["frame"], mesh.shape["patch"])
    return jax.shard_map(shards, mesh=mesh, in_specs=in_specs, out_specs=out_specs, check_vma=False)
```

time: 339 us -> 104 us (0.31)
  waiting for transfers between devices: 247 us -> 25 us
  matrix products: 45.5 us -> 0 us
  Pallas kernels: 0 us -> 27.4 us
  blocking collectives: 0 us -> 21.8 us
  between operations: 13.4 us -> 0.29 us
  local copies, waits for them, and re-layouts: 16.1 us -> 7.56 us
  starting transfers between devices: 15.6 us -> 21.6 us
    all_gather x4 -> x0, waiting for transfers between devices: 137 us -> none  [the longest x1 68.2 us: shards(): lax.all_gather(w_temporal_qkv, 'frame', axis=1, tiled=True)]
    all_to_all x4 -> x1, waiting for transfers between devices: 107 us -> 6.66 us  [exchange(): pieces = lax.all_to_all(pieces, 'frame', 0, 0, tiled=True)]
    dot_general x7 -> x0, matrix products: 30.6 us -> none  [the longest x2 9.72 us: attend_rows(): jnp.einsum('hqk,khd->qhd', probs, values, preferred_element_type=jnp.floa...]
    pallas_call x0 -> x14, Pallas kernels: none -> 27.4 us  [the longest x1 10.5 us: temporal_block(): pl.pallas_call(lambda *refs: temporal_kernel(positions, 2, *refs), out_sh...]
    all_to_all x0 -> x1, blocking collectives: none -> 21.8 us  [exchange(): pieces = lax.all_to_all(pieces, 'frame', 0, 0, tiled=True)]
    ppermute x0 -> x21, waiting for transfers between devices: none -> 18.4 us  [the longest x6 10.1 us: ring_step(): return lax.ppermute(array, ('frame', 'patch'), pairs)]
    ppermute x0 -> x21, starting transfers between devices: none -> 17.2 us  [the longest x6 9.85 us: ring_step(): return lax.ppermute(array, ('frame', 'patch'), pairs)]
    sub x3 -> x0, matrix products: 14.9 us -> none  [the longest x2 9.9 us: attend_rows(): probs = jax.nn.softmax(scores, axis=-1).astype(jnp.bfloat16)]
  transfers between devices with their start and end apart: 8 -> 22, of which waited for: 7 -> 7; matrix products, arithmetic and copies ran while one was open for 15% -> 0% of each run, Pallas kernels for 0% -> 16%
where the time goes in v1:
time: 104 us
  Pallas kernels  27.4 us (26%)
  waiting for transfers between devices  25 us (24%)
  blocking collectives  21.8 us (21%)
  starting transfers between devices  21.6 us (21%)
  local copies, waits for them, and re-layouts  7.56 us (7%)
    all_to_all x1, blocking collectives, exchange(): pieces = lax.all_to_all(pieces, 'frame', 0, 0, tiled=True)  21.8 us
    pallas_call x1, Pallas kernels, temporal_block(): pl.pallas_call(lambda *refs: temporal_kernel(positions, 2, *refs), out_sh...  10.5 us
    ppermute x6, waiting for transfers between devices, ring_step(): return lax.ppermute(array, ('frame', 'patch'), pairs)  10.1 us
    ppermute x6, starting transfers between devices, ring_step(): return lax.ppermute(array, ('frame', 'patch'), pairs)  9.85 us
    pallas_call x4, Pallas kernels, spatial_attention(): pl.pallas_call(lambda *refs: attention_kernel(parts, *refs), out_shape=ja...  9.1 us
    ppermute x15, waiting for transfers between devices, swap(): lax.ppermute(array, 'patch', [(rank, rank ^ offset) for rank in range(cou...  8.29 us
    unnamed x31, local copies, waits for them, and re-layouts  7.56 us
    ppermute x15, starting transfers between devices, swap(): lax.ppermute(array, 'patch', [(rank, rank ^ offset) for rank in range(cou...  7.31 us
  transfers between devices with their start and end apart: 22, of which 7 were waited for; matrix products, arithmetic and copies ran while one was open for 0% of the time, Pallas kernels for 16%

profile of v1, /device:TPU:0, one launch (start us, length us, event | category | flops | bytes accessed | tf_op | source)
XLA Modules:
  0.0 103.7 jit_solution(13902500067265280534)
XLA Ops:
  0.0 0.5 collective-permute-start
  0.5 2.5 %collective-permute-start.1 = (bf16[256,1152]{1,0:T(8,128)(2,1)}, bf16[256,1152]{1,0:T(8,128)(2,1)S(1)}, u32[]{:S(2)}, u32[]{:S(2)}) collective-permute-start(bf16[256,1152]{1,0:T(8,128)(2,1)} %bitcast.15), channel_id=1, source_target_pairs={{0,2},{1,3},{2,0},{3,1},{4,6},{5,7},{6,4},{7,5},{8,10},{9,11},{10,... | collective-permute-start | bytes 1769480 | tf_op jit(solution)/shard_map/ppermute | solution.py:294
  2.9 1.2 %copy-done.5 = bf16[1152,432]{0,1:T(8,128)(2,1)S(1)} copy-done((bf16[1152,432]{0,1:T(8,128)(2,1)S(1)}, bf16[1152,432]{0,1:T(8,128)(2,1)}, u32[]{:S(2)}) %copy-start.5) | copy-done | bytes 995352
  4.2 1.0 copy-done.7
  5.1 0.1 pack.1
  5.2 1.6 %collective-permute-start.2 = (bf16[304,1152]{1,0:T(8,128)(2,1)S(1)}, bf16[304,1152]{1,0:T(8,128)(2,1)S(1)}, u32[]{:S(2)}, u32[]{:S(2)}) collective-permute-start(bf16[304,1152]{1,0:T(8,128)(2,1)S(1)} %get-tuple-element.95.refs_3_), channel_id=1, source_target_pairs={{0,8},{1,5},{2,10},{3,7},{8,16},{9,1},{10,18},{11,3},{16,24},{17,9... | collective-permute-start | bytes 2101256 | tf_op jit(solution)/shard_map/ppermute | solution.py:305
  6.9 1.6 %collective-permute-start.5 = (bf16[304,1152]{1,0:T(8,128)(2,1)S(1)}, bf16[304,1152]{1,0:T(8,128)(2,1)S(1)}, u32[]{:S(2)}, u32[]{:S(2)}) collective-permute-start(bf16[304,1152]{1,0:T(8,128)(2,1)S(1)} %get-tuple-element.109.refs_4_), channel_id=1, source_target_pairs={{0,8},{1,5},{2,10},{3,7},{8,16},{9,1},{10,18},{11,3},{16,24},{17,9... | collective-permute-start | bytes 2101256 | tf_op jit(solution)/shard_map/ppermute | solution.py:305
  8.5 0.0 collective-permute-start.4
  8.5 1.6 %copy-done = bf16[1152,864]{0,1:T(8,128)(2,1)S(1)} copy-done((bf16[1152,864]{0,1:T(8,128)(2,1)S(1)}, bf16[1152,864]{0,1:T(8,128)(2,1)}, u32[]{:S(2)}) %copy-start) | copy-done | bytes 1990680
  10.0 1.1 %copy-done.3 = bf16[1,256,1152]{2,1,0:T(8,128)(2,1)S(1)} copy-done((bf16[1,256,1152]{2,1,0:T(8,128)(2,1)S(1)}, bf16[1,256,1152]{2,1,0:T(8,128)(2,1)}, u32[]{:S(2)}) %copy-start.3) | copy-done | bytes 589848
  11.1 0.7 copy-done.8
  11.8 1.2 %spatial_qkv.4 = (bf16[8,80,256]{2,1,0:T(8,128)(2,1)S(1)}, bf16[4,256,80]{2,1,0:T(8,128)(2,1)S(1)}) custom-call(bf16[256,1152]{1,0:T(8,128)(2,1)S(1)} %bitcast.16, f32[3,1152]{1,0:T(4,128)S(1)} %copy-done.8, bf16[864,1152]{1,0:T(8,128)(2,1)S(1)} %bitcast.8), custom_call_target="tpu_custom_call" | custom-call | flops 1 | bytes 1 | tf_op jit(solution)/shard_map/spatial_qkv/pallas_call | solution.py:68
  13.0 0.0 collective-permute-done.tokens_ref
  13.0 0.4 copy-done.1
  13.4 1.2 %spatial_qkv.5 = (bf16[8,80,256]{2,1,0:T(8,128)(2,1)S(1)}, bf16[4,256,80]{2,1,0:T(8,128)(2,1)S(1)}) custom-call(bf16[256,1152]{1,0:T(8,128)(2,1)S(1)} %collective-permute-done.tokens_ref, f32[3,1152]{1,0:T(4,128)S(1)} %copy-done.8, bf16[864,1152]{1,0:T(8,128)(2,1)S(1)} %bitcast.9), custom_call_target="tpu_custom_call" | custom-call | flops 1 | bytes 1 | tf_op jit(solution)/shard_map/spatial_qkv/pallas_call | solution.py:68
  14.5 2.6 %collective-permute-done.1.tokens_ref = bf16[256,1152]{1,0:T(8,128)(2,1)S(1)} collective-permute-done((bf16[256,1152]{1,0:T(8,128)(2,1)}, bf16[256,1152]{1,0:T(8,128)(2,1)S(1)}, u32[]{:S(2)}, u32[]{:S(2)}) %collective-permute-start.1) | collective-permute-done | bytes 589856 | tf_op jit(solution)/shard_map/ppermute | solution.py:294
  17.2 0.0 collective-permute-start.3
  17.2 1.2 %spatial_qkv.6 = (bf16[8,80,256]{2,1,0:T(8,128)(2,1)S(1)}, bf16[4,256,80]{2,1,0:T(8,128)(2,1)S(1)}) custom-call(bf16[256,1152]{1,0:T(8,128)(2,1)S(1)} %collective-permute-done.1.tokens_ref, f32[3,1152]{1,0:T(4,128)S(1)} %copy-done.9, bf16[864,1152]{1,0:T(8,128)(2,1)S(1)} %bitcast.10), custom_call_target="tpu_custom_call" | custom-call | flops 1610612736 | bytes 1 | tf_op jit(solution)/shard_map/spatial_qkv/pallas_call | solution.py:68
  18.3 0.0 collective-permute-done.2.refs_5_
  18.4 1.9 %collective-permute-start.7 = (bf16[304,1152]{1,0:T(8,128)(2,1)S(1)}, bf16[304,1152]{1,0:T(8,128)(2,1)S(1)}, u32[]{:S(2)}, u32[]{:S(2)}) collective-permute-start(bf16[304,1152]{1,0:T(8,128)(2,1)S(1)} %collective-permute-done.2.refs_5_), channel_id=1, source_target_pairs={{0,8},{1,5},{2,10},{3,7},{8,16},{9,1},{10,18},{11,3},{16,24},{17,9... | collective-permute-start | bytes 2101256 | tf_op jit(solution)/shard_map/ppermute | solution.py:305
  20.2 0.0 collective-permute-done.3.tokens_ref
  20.2 1.2 %spatial_qkv.7 = (bf16[8,80,256]{2,1,0:T(8,128)(2,1)S(1)}, bf16[4,256,80]{2,1,0:T(8,128)(2,1)S(1)}) custom-call(bf16[256,1152]{1,0:T(8,128)(2,1)S(1)} %collective-permute-done.3.tokens_ref, f32[3,1152]{1,0:T(4,128)S(1)} %copy-done.9, bf16[864,1152]{1,0:T(8,128)(2,1)S(1)} %bitcast.11), custom_call_target="tpu_custom_call" | custom-call | flops 1 | bytes 1 | tf_op jit(solution)/shard_map/spatial_qkv/pallas_call | solution.py:68
  21.4 2.3 %spatial_attention.4 = bf16[256,288]{1,0:T(8,128)(2,1)S(1)} custom-call(bf16[8,80,256]{2,1,0:T(8,128)(2,1)S(1)} %get-tuple-element.133.refs_0_.refs_4_, bf16[8,80,256]{2,1,0:T(8,128)(2,1)S(1)} %get-tuple-element.130.refs_1_.refs_0_, bf16[8,80,256]{2,1,0:T(8,128)(2,1)S(1)} %get-tuple-element.131.refs_2_.refs_0_, ...), custom_call_target="tpu_custom_call" | custom-call | flops 1 | bytes 1 | tf_op jit(solution)/shard_map/spatial_attention/pallas_call | solution.py:103
  23.7 0.0 copy-start.2
  23.7 0.2 collective-permute-done.5.refs_7_
  23.9 0.1 collective-permute-start.6
  24.0 2.3 %spatial_attention.5.heads_ref = bf16[256,288]{1,0:T(8,128)(2,1)S(1)} custom-call(bf16[8,80,256]{2,1,0:T(8,128)(2,1)S(1)} %get-tuple-element.132.refs_3_.refs_0_, bf16[8,80,256]{2,1,0:T(8,128)(2,1)S(1)} %get-tuple-element.130.refs_1_.refs_0_, bf16[8,80,256]{2,1,0:T(8,128)(2,1)S(1)} %get-tuple-element.131.refs_2_.refs_0_, ...), custom_call_target="tpu_custom_call" | custom-call | flops 1 | bytes 1 | tf_op jit(solution)/shard_map/spatial_attention/pallas_call | solution.py:103
  26.2 0.0 collective-permute-done.6.other_ref
  26.3 0.8 chip_partial.1
  27.1 1.6 %collective-permute-start.9 = (bf16[256,1152]{1,0:T(8,128)(2,1)S(1)}, bf16[256,1152]{1,0:T(8,128)(2,1)S(1)}, u32[]{:S(2)}, u32[]{:S(2)}) collective-permute-start(bf16[256,1152]{1,0:T(8,128)(2,1)S(1)} %chip_partial.1), channel_id=1, source_target_pairs={{0,2},{1,3},{2,0},{3,1},{4,6},{5,7},{6,4},{7,5},{8,10},{9,11},{10,... | collective-permute-start | bytes 1769480 | tf_op jit(solution)/shard_map/ppermute | solution.py:294
  28.7 2.3 %spatial_attention.6 = bf16[256,288]{1,0:T(8,128)(2,1)S(1)} custom-call(bf16[8,80,256]{2,1,0:T(8,128)(2,1)S(1)} %get-tuple-element.131.refs_2_.refs_0_, bf16[8,80,256]{2,1,0:T(8,128)(2,1)S(1)} %get-tuple-element.130.refs_1_.refs_0_, bf16[8,80,256]{2,1,0:T(8,128)(2,1)S(1)} %get-tuple-element.131.refs_2_.refs_0_, ...), custom_call_target="tpu_custom_call" | custom-call | flops 1 | bytes 1 | tf_op jit(solution)/shard_map/spatial_attention/pallas_call | solution.py:103
  30.9 0.0 copy-start.4
  30.9 0.4 collective-permute-done.7.refs_9_
  31.4 1.6 %collective-permute-start.10 = (bf16[304,1152]{1,0:T(8,128)(2,1)S(1)}, bf16[304,1152]{1,0:T(8,128)(2,1)}, u32[]{:S(2)}, u32[]{:S(2)}) collective-permute-start(bf16[304,1152]{1,0:T(8,128)(2,1)S(1)} %collective-permute-done.7.refs_9_), channel_id=1, source_target_pairs={{0,8},{1,5},{2,10},{3,7},{8,16},{9,1},{10,18},{11,3},{16,24},{17,9... | collective-permute-start | bytes 2101256 | tf_op jit(solution)/shard_map/ppermute | solution.py:305
  33.0 2.3 %spatial_attention.7.heads_ref = bf16[256,288]{1,0:T(8,128)(2,1)S(1)} custom-call(bf16[8,80,256]{2,1,0:T(8,128)(2,1)S(1)} %get-tuple-element.130.refs_1_.refs_0_, bf16[8,80,256]{2,1,0:T(8,128)(2,1)S(1)} %get-tuple-element.130.refs_1_.refs_0_, bf16[8,80,256]{2,1,0:T(8,128)(2,1)S(1)} %get-tuple-element.131.refs_2_.refs_0_, ...), custom_call_target="tpu_custom_call" | custom-call | flops 1 | bytes 1 | tf_op jit(solution)/shard_map/spatial_attention/pallas_call | solution.py:103
  35.2 0.1 collective-permute-start.8
  35.3 1.6 %collective-permute-start.14 = (bf16[304,1152]{1,0:T(8,128)(2,1)S(1)}, bf16[304,1152]{1,0:T(8,128)(2,1)}, u32[]{:S(2)}, u32[]{:S(2)}) collective-permute-start(bf16[304,1152]{1,0:T(8,128)(2,1)S(1)} %collective-permute-done.5.refs_7_), channel_id=1, source_target_pairs={{0,8},{1,5},{2,10},{3,7},{8,16},{9,1},{10,18},{11,3},{16,24},{17,9... | collective-permute-start | bytes 2101256 | tf_op jit(solution)/shard_map/ppermute | solution.py:305
  37.0 0.8 spatial_base.1.base_ref
  37.8 0.0 copy-start.10
  37.8 0.1 collective-permute-start.11
  37.9 0.5 collective-permute-start.12
  38.4 4.4 %collective-permute-done.9.refs_0_ = bf16[256,1152]{1,0:T(8,128)(2,1)S(1)} collective-permute-done((bf16[256,1152]{1,0:T(8,128)(2,1)S(1)}, bf16[256,1152]{1,0:T(8,128)(2,1)S(1)}, u32[]{:S(2)}, u32[]{:S(2)}) %collective-permute-start.9) | collective-permute-done | bytes 589856 | tf_op jit(solution)/shard_map/ppermute | solution.py:294
  42.8 1.0 spatial_add.1
  43.8 1.6 %collective-permute-start.19 = (bf16[304,1152]{1,0:T(8,128)(2,1)}, bf16[304,1152]{1,0:T(8,128)(2,1)}, u32[]{:S(2)}, u32[]{:S(2)}) collective-permute-start(bf16[304,1152]{1,0:T(8,128)(2,1)} %collective-permute-done.10.refs_13_), channel_id=1, source_target_pairs={{0,8},{1,5},{2,10},{3,7},{8,16},{9,1},{10,18},{11,3},{16,24},{17,9... | collective-permute-start | bytes 2101256 | tf_op jit(solution)/shard_map/ppermute | solution.py:305
  45.4 1.4 %collective-permute-start.17 = (bf16[304,1152]{1,0:T(8,128)(2,1)}, bf16[304,1152]{1,0:T(8,128)(2,1)}, u32[]{:S(2)}, u32[]{:S(2)}) collective-permute-start(bf16[304,1152]{1,0:T(8,128)(2,1)} %collective-permute-done.10.refs_13_), channel_id=1, source_target_pairs={{0,2},{1,3},{2,0},{3,1},{4,6},{5,7},{6,4},{7,5},{8,10},{9,11},{10,... | collective-permute-start | bytes 2101256 | tf_op jit(solution)/shard_map/ppermute | solution.py:294
  46.8 4.4 %all-to-all-start = ((bf16[8,32,1152]{2,1,0:T(8,128)(2,1)}), bf16[8,32,1152]{2,1,0:T(8,128)(2,1)S(1)}, u32[]{:S(2)}, u32[]{:S(2)}) async-start(bf16[8,32,1152]{2,1,0:T(8,128)(2,1)} %bitcast.4), calls=%async_computation | async-start | bytes 1179648 | tf_op jit(solution)/shard_map/all_to_all | solution.py:317
  51.2 0.0 collective-permute-done.14.refs_11_
  51.2 0.1 collective-permute-start.13
  51.3 0.5 collective-permute-start.16
  51.8 0.1 collective-permute-start.15
  51.9 9.5 %collective-permute-done.19.refs_17_ = bf16[304,1152]{1,0:T(8,128)(2,1)} collective-permute-done((bf16[304,1152]{1,0:T(8,128)(2,1)}, bf16[304,1152]{1,0:T(8,128)(2,1)}, u32[]{:S(2)}, u32[]{:S(2)}) %collective-permute-start.19) | collective-permute-done | bytes 700448 | tf_op jit(solution)/shard_map/ppermute | solution.py:305
  61.4 0.0 collective-permute-start.20
  61.4 1.2 %collective-permute-done.17.refs_15_ = bf16[304,1152]{1,0:T(8,128)(2,1)} collective-permute-done((bf16[304,1152]{1,0:T(8,128)(2,1)}, bf16[304,1152]{1,0:T(8,128)(2,1)}, u32[]{:S(2)}, u32[]{:S(2)}) %collective-permute-start.17) | collective-permute-done | bytes 700448 | tf_op jit(solution)/shard_map/ppermute | solution.py:294
  62.6 0.0 collective-permute-start.18
  62.6 6.7 %all-to-all-done = bf16[8,32,1152]{2,1,0:T(8,128)(2,1)S(1)} async-done(((bf16[8,32,1152]{2,1,0:T(8,128)(2,1)}), bf16[8,32,1152]{2,1,0:T(8,128)(2,1)S(1)}, u32[]{:S(2)}, u32[]{:S(2)}) %all-to-all-start) | async-done | bytes 589856 | tf_op jit(solution)/shard_map/all_to_all | solution.py:317
  69.3 0.4 temporal_norm.1.refs_1_
  69.7 0.0 collective-permute-done.13.refs_10_
  69.7 0.0 collective-permute-done.15.refs_12_
  69.8 0.0 collective-permute-done.20.refs_18_
  69.8 0.8 copy-done.14
  70.6 0.0 collective-permute-done.18.refs_16_
  70.6 10.5 %temporal_block.1 = bf16[256,1152]{1,0:T(8,128)(2,1)S(1)} custom-call(bf16[256,1152]{1,0:T(8,128)(2,1)S(1)} %bitcast.13, bf16[256,1152]{1,0:T(8,128)(2,1)S(1)} %temporal_norm.1.refs_1_, f32[3,1152]{1,0:T(4,128)S(1)} %copy-done.10, bf16[304,1152]{1,0:T(8,128)(2,1)S(1)} %get-tuple-element.95.refs_3_, bf16[304,1152]{1,0:T(8,128)(2,1)} %copy-done.6, ...), custom_call_target="tpu_custom_call" | custom-call | flops 1 | bytes 1 | tf_op jit(solution)/shard_map/temporal_block/pallas_call | solution.py:276
  81.1 21.8 %all_to_all.10 = bf16[8,32,1152]{2,1,0:T(8,128)(2,1)S(1)} all-to-all(bf16[8,32,1152]{2,1,0:T(8,128)(2,1)S(1)} %bitcast.18), channel_id=1, replica_groups=mesh['frame'=8,'patch'=4] {'frame'}, dimensions={0} | all-to-all | bytes 1179648 | tf_op jit(solution)/shard_map/all_to_all | solution.py:317
  102.9 0.8 copy.9
  (26 shorter events, 0.1 us)
Async XLA Ops:
  0.0 13.0 %collective-permute-start = (bf16[256,1152]{1,0:T(8,128)(2,1)}, bf16[256,1152]{1,0:T(8,128)(2,1)S(1)}, u32[]{:S(2)}, u32[]{:S(2)}) collective-permute-start(bf16[256,1152]{1,0:T(8,128)(2,1)} %bitcast.14), channel_id=1, source_target_pairs={{0,1},{1,0},{2,3},{3,2},{4,5},{5,4},{6,7},{7,6},{8,9},{9,8},{10,11... | collective-permute-start | bytes 1769480 | tf_op jit(solution)/shard_map/ppermute | solution.py:294
  0.5 16.7 %collective-permute-start.1 = (bf16[256,1152]{1,0:T(8,128)(2,1)}, bf16[256,1152]{1,0:T(8,128)(2,1)S(1)}, u32[]{:S(2)}, u32[]{:S(2)}) collective-permute-start(bf16[256,1152]{1,0:T(8,128)(2,1)} %bitcast.15), channel_id=1, source_target_pairs={{0,2},{1,3},{2,0},{3,1},{4,6},{5,7},{6,4},{7,5},{8,10},{9,11},{10,... | collective-permute-start | bytes 1769480 | tf_op jit(solution)/shard_map/ppermute | solution.py:294
  2.9 1.2 %copy-start.5 = (bf16[1152,432]{0,1:T(8,128)(2,1)S(1)}, bf16[1152,432]{0,1:T(8,128)(2,1)}, u32[]{:S(2)}) copy-start(bf16[1152,432]{0,1:T(8,128)(2,1)} %param.12) | copy-start | bytes 2985988
  4.1 1.0 copy-start.7
  5.2 9.3 %copy-start.6 = (bf16[304,1152]{1,0:T(8,128)(2,1)}, bf16[304,1152]{1,0:T(8,128)(2,1)S(1)}, u32[]{:S(2)}) copy-start(bf16[304,1152]{1,0:T(8,128)(2,1)S(1)} %get-tuple-element.109.refs_4_) | copy-start | bytes 2101252
  5.2 13.1 %collective-permute-start.2 = (bf16[304,1152]{1,0:T(8,128)(2,1)S(1)}, bf16[304,1152]{1,0:T(8,128)(2,1)S(1)}, u32[]{:S(2)}, u32[]{:S(2)}) collective-permute-start(bf16[304,1152]{1,0:T(8,128)(2,1)S(1)} %get-tuple-element.95.refs_3_), channel_id=1, source_target_pairs={{0,8},{1,5},{2,10},{3,7},{8,16},{9,1},{10,18},{11,3},{16,24},{17,9... | collective-permute-start | bytes 2101256 | tf_op jit(solution)/shard_map/ppermute | solution.py:305
  6.9 17.0 %collective-permute-start.5 = (bf16[304,1152]{1,0:T(8,128)(2,1)S(1)}, bf16[304,1152]{1,0:T(8,128)(2,1)S(1)}, u32[]{:S(2)}, u32[]{:S(2)}) collective-permute-start(bf16[304,1152]{1,0:T(8,128)(2,1)S(1)} %get-tuple-element.109.refs_4_), channel_id=1, source_target_pairs={{0,8},{1,5},{2,10},{3,7},{8,16},{9,1},{10,18},{11,3},{16,24},{17,9... | collective-permute-start | bytes 2101256 | tf_op jit(solution)/shard_map/ppermute | solution.py:305
  8.5 13.0 %collective-permute-start.4 = (bf16[288,1152]{1,0:T(8,128)(2,1)}, bf16[288,1152]{1,0:T(8,128)(2,1)S(1)}, u32[]{:S(2)}, u32[]{:S(2)}) collective-permute-start(bf16[288,1152]{1,0:T(8,128)(2,1)} %weight_ref.3), channel_id=1, source_target_pairs={{0,1},{1,0},{2,3},{3,2},{4,5},{5,4},{6,7},{7,6},{8,9},{9,8},{10,11... | collective-permute-start | bytes 1990664 | tf_op jit(solution)/shard_map/ppermute | solution.py:294
  8.5 1.6 %copy-start = (bf16[1152,864]{0,1:T(8,128)(2,1)S(1)}, bf16[1152,864]{0,1:T(8,128)(2,1)}, u32[]{:S(2)}) copy-start(bf16[1152,864]{0,1:T(8,128)(2,1)} %param.9) | copy-start | bytes 5971972
  10.0 1.1 %copy-start.3 = (bf16[1,256,1152]{2,1,0:T(8,128)(2,1)S(1)}, bf16[1,256,1152]{2,1,0:T(8,128)(2,1)}, u32[]{:S(2)}) copy-start(bf16[1,256,1152]{2,1,0:T(8,128)(2,1)} %param.7) | copy-start | bytes 1769476
  11.1 0.7 copy-start.8
  11.8 1.6 %copy-start.1 = (bf16[1152,864]{0,1:T(8,128)(2,1)S(1)}, bf16[1152,864]{0,1:T(8,128)(2,1)}, u32[]{:S(2)}) copy-start(bf16[1152,864]{0,1:T(8,128)(2,1)} %param.9) | copy-start | bytes 5971972
  11.8 5.4 %copy-start.9 = (f32[3,1152]{1,0:T(4,128)S(1)}, f32[3,1152]{1,0:T(4,128)}, u32[]{:S(2)}) copy-start(f32[3,1152]{1,0:T(4,128)} %mod_ref.12) | copy-start | bytes 41476
  17.2 3.1 %collective-permute-start.3 = (bf16[256,1152]{1,0:T(8,128)(2,1)S(1)}, bf16[256,1152]{1,0:T(8,128)(2,1)S(1)}, u32[]{:S(2)}, u32[]{:S(2)}) collective-permute-start(bf16[256,1152]{1,0:T(8,128)(2,1)S(1)} %collective-permute-done.1.tokens_ref), channel_id=1, source_target_pairs={{0,1},{1,0},{2,3},{3,2},{4,5},{5,4},{6,7},{7,6},{8,9},{9,8},{10,11... | collective-permute-start | bytes 1769480 | tf_op jit(solution)/shard_map/ppermute | solution.py:294
  18.3 19.4 %copy-start.11 = (bf16[304,1152]{1,0:T(8,128)(2,1)}, bf16[304,1152]{1,0:T(8,128)(2,1)S(1)}, u32[]{:S(2)}) copy-start(bf16[304,1152]{1,0:T(8,128)(2,1)S(1)} %collective-permute-done.2.refs_5_) | copy-start | bytes 2101252
  18.4 13.0 %collective-permute-start.7 = (bf16[304,1152]{1,0:T(8,128)(2,1)S(1)}, bf16[304,1152]{1,0:T(8,128)(2,1)S(1)}, u32[]{:S(2)}, u32[]{:S(2)}) collective-permute-start(bf16[304,1152]{1,0:T(8,128)(2,1)S(1)} %collective-permute-done.2.refs_5_), channel_id=1, source_target_pairs={{0,8},{1,5},{2,10},{3,7},{8,16},{9,1},{10,18},{11,3},{16,24},{17,9... | collective-permute-start | bytes 2101256 | tf_op jit(solution)/shard_map/ppermute | solution.py:305
  23.7 2.6 %copy-start.2 = (bf16[288,1152]{1,0:T(8,128)(2,1)S(1)}, bf16[288,1152]{1,0:T(8,128)(2,1)}, u32[]{:S(2)}) copy-start(bf16[288,1152]{1,0:T(8,128)(2,1)} %weight_ref.3) | copy-start | bytes 1990660
  23.9 14.0 %copy-start.12 = (bf16[304,1152]{1,0:T(8,128)(2,1)}, bf16[304,1152]{1,0:T(8,128)(2,1)S(1)}, u32[]{:S(2)}) copy-start(bf16[304,1152]{1,0:T(8,128)(2,1)S(1)} %collective-permute-done.5.refs_7_) | copy-start | bytes 2101252
  23.9 2.4 %collective-permute-start.6 = (bf16[256,288]{1,0:T(8,128)(2,1)S(1)}, bf16[256,288]{1,0:T(8,128)(2,1)S(1)}, u32[]{:S(2)}, u32[]{:S(2)}) collective-permute-start(bf16[256,288]{1,0:T(8,128)(2,1)S(1)} %spatial_attention.4), channel_id=1, source_target_pairs={{0,1},{1,0},{2,3},{3,2},{4,5},{5,4},{6,7},{7,6},{8,9},{9,8},{10,11... | collective-permute-start | bytes 442376 | tf_op jit(solution)/shard_map/ppermute | solution.py:294
  27.1 15.7 %collective-permute-start.9 = (bf16[256,1152]{1,0:T(8,128)(2,1)S(1)}, bf16[256,1152]{1,0:T(8,128)(2,1)S(1)}, u32[]{:S(2)}, u32[]{:S(2)}) collective-permute-start(bf16[256,1152]{1,0:T(8,128)(2,1)S(1)} %chip_partial.1), channel_id=1, source_target_pairs={{0,2},{1,3},{2,0},{3,1},{4,6},{5,7},{6,4},{7,5},{8,10},{9,11},{10,... | collective-permute-start | bytes 1769480 | tf_op jit(solution)/shard_map/ppermute | solution.py:294
  30.9 6.0 %copy-start.4 = (bf16[1,256,1152]{2,1,0:T(8,128)(2,1)S(1)}, bf16[1,256,1152]{2,1,0:T(8,128)(2,1)}, u32[]{:S(2)}) copy-start(bf16[1,256,1152]{2,1,0:T(8,128)(2,1)} %param.7) | copy-start | bytes 1769476
  31.4 19.8 %copy-start.13 = (bf16[304,1152]{1,0:T(8,128)(2,1)}, bf16[304,1152]{1,0:T(8,128)(2,1)S(1)}, u32[]{:S(2)}) copy-start(bf16[304,1152]{1,0:T(8,128)(2,1)S(1)} %collective-permute-done.7.refs_9_) | copy-start | bytes 2101252
  31.4 12.4 %collective-permute-start.10 = (bf16[304,1152]{1,0:T(8,128)(2,1)S(1)}, bf16[304,1152]{1,0:T(8,128)(2,1)}, u32[]{:S(2)}, u32[]{:S(2)}) collective-permute-start(bf16[304,1152]{1,0:T(8,128)(2,1)S(1)} %collective-permute-done.7.refs_9_), channel_id=1, source_target_pairs={{0,8},{1,5},{2,10},{3,7},{8,16},{9,1},{10,18},{11,3},{16,24},{17,9... | collective-permute-start | bytes 2101256 | tf_op jit(solution)/shard_map/ppermute | solution.py:305
  35.2 1.7 %collective-permute-start.8 = (bf16[256,288]{1,0:T(8,128)(2,1)S(1)}, bf16[256,288]{1,0:T(8,128)(2,1)S(1)}, u32[]{:S(2)}, u32[]{:S(2)}) collective-permute-start(bf16[256,288]{1,0:T(8,128)(2,1)S(1)} %spatial_attention.6), channel_id=1, source_target_pairs={{0,1},{1,0},{2,3},{3,2},{4,5},{5,4},{6,7},{7,6},{8,9},{9,8},{10,11... | collective-permute-start | bytes 442376 | tf_op jit(solution)/shard_map/ppermute | solution.py:294
  35.3 15.9 %collective-permute-start.14 = (bf16[304,1152]{1,0:T(8,128)(2,1)S(1)}, bf16[304,1152]{1,0:T(8,128)(2,1)}, u32[]{:S(2)}, u32[]{:S(2)}) collective-permute-start(bf16[304,1152]{1,0:T(8,128)(2,1)S(1)} %collective-permute-done.5.refs_7_), channel_id=1, source_target_pairs={{0,8},{1,5},{2,10},{3,7},{8,16},{9,1},{10,18},{11,3},{16,24},{17,9... | collective-permute-start | bytes 2101256 | tf_op jit(solution)/shard_map/ppermute | solution.py:305
  37.8 31.5 %copy-start.10 = (f32[3,1152]{1,0:T(4,128)S(1)}, f32[3,1152]{1,0:T(4,128)}, u32[]{:S(2)}) copy-start(f32[3,1152]{1,0:T(4,128)} %refs_2_.1) | copy-start | bytes 41476
  37.8 13.5 %collective-permute-start.11 = (bf16[304,1152]{1,0:T(8,128)(2,1)S(1)}, bf16[304,1152]{1,0:T(8,128)(2,1)}, u32[]{:S(2)}, u32[]{:S(2)}) collective-permute-start(bf16[304,1152]{1,0:T(8,128)(2,1)S(1)} %collective-permute-done.2.refs_5_), channel_id=1, source_target_pairs={{0,1},{1,0},{2,3},{3,2},{4,5},{5,4},{6,7},{7,6},{8,9},{9,8},{10,11... | collective-permute-start | bytes 2101256 | tf_op jit(solution)/shard_map/ppermute | solution.py:294
  37.9 13.9 %collective-permute-start.12 = (bf16[304,1152]{1,0:T(8,128)(2,1)S(1)}, bf16[304,1152]{1,0:T(8,128)(2,1)}, u32[]{:S(2)}, u32[]{:S(2)}) collective-permute-start(bf16[304,1152]{1,0:T(8,128)(2,1)S(1)} %collective-permute-done.5.refs_7_), channel_id=1, source_target_pairs={{0,1},{1,0},{2,3},{3,2},{4,5},{5,4},{6,7},{7,6},{8,9},{9,8},{10,11... | collective-permute-start | bytes 2101256 | tf_op jit(solution)/shard_map/ppermute | solution.py:294
  43.8 17.6 %collective-permute-start.19 = (bf16[304,1152]{1,0:T(8,128)(2,1)}, bf16[304,1152]{1,0:T(8,128)(2,1)}, u32[]{:S(2)}, u32[]{:S(2)}) collective-permute-start(bf16[304,1152]{1,0:T(8,128)(2,1)} %collective-permute-done.10.refs_13_), channel_id=1, source_target_pairs={{0,8},{1,5},{2,10},{3,7},{8,16},{9,1},{10,18},{11,3},{16,24},{17,9... | collective-permute-start | bytes 2101256 | tf_op jit(solution)/shard_map/ppermute | solution.py:305
  45.4 17.2 %collective-permute-start.17 = (bf16[304,1152]{1,0:T(8,128)(2,1)}, bf16[304,1152]{1,0:T(8,128)(2,1)}, u32[]{:S(2)}, u32[]{:S(2)}) collective-permute-start(bf16[304,1152]{1,0:T(8,128)(2,1)} %collective-permute-done.10.refs_13_), channel_id=1, source_target_pairs={{0,2},{1,3},{2,0},{3,1},{4,6},{5,7},{6,4},{7,5},{8,10},{9,11},{10,... | collective-permute-start | bytes 2101256 | tf_op jit(solution)/shard_map/ppermute | solution.py:294
  46.8 22.5 %all-to-all-start = ((bf16[8,32,1152]{2,1,0:T(8,128)(2,1)}), bf16[8,32,1152]{2,1,0:T(8,128)(2,1)S(1)}, u32[]{:S(2)}, u32[]{:S(2)}) async-start(bf16[8,32,1152]{2,1,0:T(8,128)(2,1)} %bitcast.4), calls=%async_computation | async-start | bytes 1179648 | tf_op jit(solution)/shard_map/all_to_all | solution.py:317
  51.2 18.5 %collective-permute-start.13 = (bf16[304,1152]{1,0:T(8,128)(2,1)S(1)}, bf16[304,1152]{1,0:T(8,128)(2,1)}, u32[]{:S(2)}, u32[]{:S(2)}) collective-permute-start(bf16[304,1152]{1,0:T(8,128)(2,1)S(1)} %collective-permute-done.7.refs_9_), channel_id=1, source_target_pairs={{0,1},{1,0},{2,3},{3,2},{4,5},{5,4},{6,7},{7,6},{8,9},{9,8},{10,11... | collective-permute-start | bytes 2101256 | tf_op jit(solution)/shard_map/ppermute | solution.py:294
  51.3 18.4 %collective-permute-start.16 = (bf16[304,1152]{1,0:T(8,128)(2,1)}, bf16[304,1152]{1,0:T(8,128)(2,1)}, u32[]{:S(2)}, u32[]{:S(2)}) collective-permute-start(bf16[304,1152]{1,0:T(8,128)(2,1)} %collective-permute-done.10.refs_13_), channel_id=1, source_target_pairs={{0,1},{1,0},{2,3},{3,2},{4,5},{5,4},{6,7},{7,6},{8,9},{9,8},{10,11... | collective-permute-start | bytes 2101256 | tf_op jit(solution)/shard_map/ppermute | solution.py:294
  51.8 17.9 %collective-permute-start.15 = (bf16[304,1152]{1,0:T(8,128)(2,1)}, bf16[304,1152]{1,0:T(8,128)(2,1)S(1)}, u32[]{:S(2)}, u32[]{:S(2)}) collective-permute-start(bf16[304,1152]{1,0:T(8,128)(2,1)} %collective-permute-done.14.refs_11_), channel_id=1, source_target_pairs={{0,1},{1,0},{2,3},{3,2},{4,5},{5,4},{6,7},{7,6},{8,9},{9,8},{10,11... | collective-permute-start | bytes 2101256 | tf_op jit(solution)/shard_map/ppermute | solution.py:294
  61.4 8.4 %collective-permute-start.20 = (bf16[304,1152]{1,0:T(8,128)(2,1)}, bf16[304,1152]{1,0:T(8,128)(2,1)}, u32[]{:S(2)}, u32[]{:S(2)}) collective-permute-start(bf16[304,1152]{1,0:T(8,128)(2,1)} %collective-permute-done.19.refs_17_), channel_id=1, source_target_pairs={{0,1},{1,0},{2,3},{3,2},{4,5},{5,4},{6,7},{7,6},{8,9},{9,8},{10,11... | collective-permute-start | bytes 2101256 | tf_op jit(solution)/shard_map/ppermute | solution.py:294
  62.6 8.0 %collective-permute-start.18 = (bf16[304,1152]{1,0:T(8,128)(2,1)}, bf16[304,1152]{1,0:T(8,128)(2,1)}, u32[]{:S(2)}, u32[]{:S(2)}) collective-permute-start(bf16[304,1152]{1,0:T(8,128)(2,1)} %collective-permute-done.17.refs_15_), channel_id=1, source_target_pairs={{0,1},{1,0},{2,3},{3,2},{4,5},{5,4},{6,7},{7,6},{8,9},{9,8},{10,11... | collective-permute-start | bytes 2101256 | tf_op jit(solution)/shard_map/ppermute | solution.py:294
  69.7 0.9 copy-start.14

commit v2 on v1

--- a/solution.py
+++ b/solution.py
@@ -12,9 +12,11 @@
 PAD_DIM = 80
 EPS = 1e-06
 QUERY_SCALE = math.log2(math.e) / math.sqrt(HEAD_DIM)
+HEAD_ROWS = 4 * HEAD_DIM
+RESIDENT = 4
 QKV_ROWS = 224
 VMEM_LIMIT = 24 * 1024 * 1024
-LARGE_VMEM_LIMIT = 51 * 1024 * 1024
+LARGE_VMEM_LIMIT = 49 * 1024 * 1024
 MEDIUM = pl.CostEstimate(flops=3 << 29, bytes_accessed=1, transcendentals=0)
 SMALL = pl.CostEstimate(flops=1, bytes_accessed=1, transcendentals=0)
 
@@ -159,7 +161,6 @@
 
 def pack_kernel(place_ref, qkv_ref, out_ref, *head_refs):
     count = len(head_refs)
-    zeros = jnp.zeros((PAD_DIM - HEAD_DIM, qkv_ref.shape[1]), jnp.bfloat16)
     for first in range(count):
 
         @pl.when(place_ref[0] == first)
@@ -169,9 +170,7 @@
                 head_ref[...] = jnp.concatenate(
                     [
                         qkv_ref[head * 3 * HEAD_DIM : (head + 1) * 3 * HEAD_DIM],
-                        zeros,
                         out_ref[head * HEAD_DIM : (head + 1) * HEAD_DIM],
-                        zeros,
                     ],
                     axis=0,
                 )
@@ -183,7 +182,7 @@
         place = jnp.zeros((1,), jnp.int32)
     return pl.pallas_call(
         pack_kernel,
-        out_shape=(jax.ShapeDtypeStruct((QKV_ROWS + PAD_DIM, out.shape[1]), jnp.bfloat16),) * count,
+        out_shape=(jax.ShapeDtypeStruct((HEAD_ROWS, out.shape[1]), jnp.bfloat16),) * count,
         in_specs=[pl.BlockSpec(memory_space=pltpu.SMEM)]
         + [pl.BlockSpec(memory_space=pltpu.VMEM)] * 2,
         compiler_params=pltpu.CompilerParams(vmem_limit_bytes=VMEM_LIMIT),
@@ -193,10 +192,11 @@
 
 
 def temporal_kernel(positions, group, tokens_ref, moved_ref, mod_ref, *refs):
-    head_refs = refs[:HEADS]
+    resident_refs, streamed_refs = refs[:RESIDENT], refs[RESIDENT:HEADS]
     result_ref, heads_scratch, qkv_scratch, out_scratch, sems = refs[HEADS:]
+    streamed = len(streamed_refs)
     copies = []
-    for index, ref in enumerate(head_refs):
+    for index, ref in enumerate(streamed_refs):
         copies.append(
             pltpu.make_async_copy(
                 ref.at[pl.ds(0, QKV_ROWS)],
@@ -204,66 +204,105 @@
                 sems.at[index],
             )
         )
-    for index, ref in enumerate(head_refs):
+    for index, ref in enumerate(streamed_refs):
         copies.append(
             pltpu.make_async_copy(
-                ref.at[pl.ds(QKV_ROWS, PAD_DIM)],
-                out_scratch.at[pl.ds(index * PAD_DIM, PAD_DIM)],
-                sems.at[HEADS + index],
+                ref.at[pl.ds(HEAD_ROWS - PAD_DIM, PAD_DIM)],
+                out_scratch.at[pl.ds((RESIDENT + index) * PAD_DIM, PAD_DIM)],
+                sems.at[streamed + index],
             )
         )
-    for copy in copies[: 2 * group]:
+    for copy in copies:
         copy.start()
+    for index, ref in enumerate(resident_refs):
+        out_scratch[pl.ds(index * PAD_DIM, PAD_DIM), :] = ref[pl.ds(HEAD_ROWS - PAD_DIM, PAD_DIM), :]
 
     tokens = tokens_ref[...]
     count = tokens.shape[0]
     moved = moved_ref[...]
-    key_pos = lax.broadcasted_iota(jnp.int32, (count, count), 0) % positions
-    query_pos = lax.broadcasted_iota(jnp.int32, (count, count), 1) % positions
+    piece, places = by_half(count // positions, positions)
+    part = count // halves_of(positions)
+    key_pos = lax.broadcasted_iota(jnp.int32, (part, part), 0) % piece
+    query_pos = lax.broadcasted_iota(jnp.int32, (part, part), 1) % piece
     same = key_pos == query_pos
     zeros = jnp.zeros((PAD_DIM - HEAD_DIM, count), jnp.float32)
 
     def project(first):
-        for copy in copies[first + 2 * group : first + 3 * group]:
-            copy.start()
-        for index in range(first, first + group):
-            copies[index].wait()
-        rows = qkv_scratch[pl.ds(first * QKV_ROWS, group * QKV_ROWS), :]
-        return dot(rows, moved, TRANSPOSED_RHS)
+        if first < RESIDENT:
+            return [
+                dot(ref[pl.ds(0, QKV_ROWS), :], moved, TRANSPOSED_RHS)
+                for ref in resident_refs[first : first + group]
+            ]
+        for copy in copies[first - RESIDENT : first - RESIDENT + group]:
+            copy.wait()
+        rows = qkv_scratch[pl.ds((first - RESIDENT) * QKV_ROWS, group * QKV_ROWS), :]
+        columns = dot(rows, moved, TRANSPOSED_RHS)
+        return [columns[QKV_ROWS * k : QKV_ROWS * (k + 1)] for k in range(group)]
 
     columns = project(0)
     for first in range(0, HEADS, group):
         here = columns
         if first + group < HEADS:
             columns = project(first + group)
-        split = [
-            split_head(here[QKV_ROWS * k : QKV_ROWS * k + 3 * HEAD_DIM]) for k in range(group)
+        split = [split_head(block[: 3 * HEAD_DIM]) for block in here]
+        scores = [
+            jnp.where(
+                same,
+                dot(keys[start : start + part], query[:, start : start + part]),
+                -jnp.inf,
+            )
+            for query, keys, _ in split
+            for start in range(0, count, part)
         ]
-        scores = [jnp.where(same, dot(keys, query), -jnp.inf) for query, keys, _ in split]
         probs = [
             jnp.exp2(block - jnp.max(block, axis=0, keepdims=True)).astype(jnp.bfloat16)
             for block in scores
         ]
-        mixed = [dot(values, block) for (_, _, values), block in zip(split, probs)]
-        for index, block in enumerate(mixed):
+        for index, (_, _, values) in enumerate(split):
+            mixed = [
+                dot(values[:, start : start + part], block)
+                for start, block in zip(
+                    range(0, count, part), probs[index * count // part :]
+                )
+            ]
+            block = jnp.concatenate(mixed, axis=1)
             heads_scratch[pl.ds((first + index) * PAD_DIM, PAD_DIM), :] = jnp.concatenate(
-                [block[:HEAD_DIM] / block[HEAD_DIM : HEAD_DIM + 1], zeros], axis=0
+                [zeros, block[:HEAD_DIM] / block[HEAD_DIM : HEAD_DIM + 1]], axis=0
             )
-    for copy in copies[HEADS + 2 * group :]:
-        copy.start()
-    for copy in copies[HEADS:]:
+    for copy in copies[streamed:]:
         copy.wait()
     total = dot(heads_scratch[...].T.astype(jnp.bfloat16), out_scratch[...])
-    result_ref[...] = (tokens.astype(jnp.float32) + mod_ref[2:3, :] * total).astype(jnp.bfloat16)
-
-
-def norm_kernel(tokens_ref, mod_ref, moved_ref):
-    moved_ref[...] = normalise(tokens_ref[...], mod_ref)
-
-
-def temporal_norm(tokens, mod):
-    return pl.pallas_call(
-        norm_kernel,
+    for start, place in places:
+        result_ref[pl.ds(start, piece), :] = (
+            tokens[start : start + piece].astype(jnp.float32)
+            + mod_ref[2:3, :] * total[place : place + piece]
+        ).astype(jnp.bfloat16)
+
+
+def halves_of(positions):
+    return 1 if positions % 32 else 2
+
+
+def by_half(frames, positions):
+    halves = halves_of(positions)
+    rows = positions // halves
+    return rows, [
+        (frame * positions + half * rows, (half * frames + frame) * rows)
+        for half in range(halves)
+        for frame in range(frames)
+    ]
+
+
+def norm_kernel(positions, tokens_ref, mod_ref, moved_ref):
+    moved = normalise(tokens_ref[...], mod_ref)
+    rows, places = by_half(moved.shape[0] // positions, positions)
+    for start, place in places:
+        moved_ref[pl.ds(place, rows), :] = moved[start : start + rows]
+
+
+def temporal_norm(tokens, mod, positions):
+    return pl.pallas_call(
+        lambda *refs: norm_kernel(positions, *refs),
         out_shape=jax.ShapeDtypeStruct(tokens.shape, jnp.bfloat16),
         compiler_params=pltpu.CompilerParams(vmem_limit_bytes=VMEM_LIMIT),
         cost_estimate=SMALL,
@@ -274,15 +313,15 @@
 def temporal_block(tokens, moved, mod, weights, positions):
     count, width = tokens.shape
     return pl.pallas_call(
-        lambda *refs: temporal_kernel(positions, 2, *refs),
+        lambda *refs: temporal_kernel(positions, 4, *refs),
         out_shape=jax.ShapeDtypeStruct((count, width), jnp.bfloat16),
-        in_specs=[pl.BlockSpec(memory_space=pltpu.VMEM)] * 3
-        + [pl.BlockSpec(memory_space=pl.ANY)] * HEADS,
+        in_specs=[pl.BlockSpec(memory_space=pltpu.VMEM)] * (3 + RESIDENT)
+        + [pl.BlockSpec(memory_space=pl.ANY)] * (HEADS - RESIDENT),
         scratch_shapes=[
             pltpu.VMEM((HEADS * PAD_DIM, count), jnp.float32),
-            pltpu.VMEM((HEADS * QKV_ROWS, width), jnp.bfloat16),
+            pltpu.VMEM(((HEADS - RESIDENT) * QKV_ROWS, width), jnp.bfloat16),
             pltpu.VMEM((HEADS * PAD_DIM, width), jnp.bfloat16),
-            pltpu.SemaphoreType.DMA((2 * HEADS,)),
+            pltpu.SemaphoreType.DMA((2 * (HEADS - RESIDENT),)),
         ],
         compiler_params=pltpu.CompilerParams(vmem_limit_bytes=LARGE_VMEM_LIMIT),
         cost_estimate=SMALL,
@@ -394,8 +433,10 @@
         if len(first) == 2:
             third_far = swap(third, 2, patch_count)
         arrived = exchange(after_spatial)
-        moved = temporal_norm(arrived, mod_temporal)
-        rest = first + second + [third]
+        moved = temporal_norm(arrived, mod_temporal, patches // frame_count)
+        weights += first
+        others = [over_cores(array) for array in first]
+        rest = second + [third]
         if len(first) == 2:
             rest += [third_far, fourth]
         else:
@@ -404,7 +445,8 @@
                 fourth = hop(fourth)
             weights.append(fourth)
         for array in rest:
-            weights += [array, over_cores(array)]
+            others += [array, over_cores(array)]
+        weights += others
         result = temporal_block(arrived, moved, mod_temporal, weights, patches // frame_count)
         return exchange(result).reshape(1, patches, width)
 

time: 104 us -> 99.2 us (0.954)
  Pallas kernels: 27.4 us -> 23.7 us
    ppermute x6, waiting for transfers between devices: 10.1 us -> 7.09 us  [ring_step(): return lax.ppermute(array, ('frame', 'patch'), pairs)]
    pallas_call x3, Pallas kernels: 11 us -> 8.15 us  [the longest x1 7.62 us: temporal_block(): pl.pallas_call(lambda *refs: temporal_kernel(positions, 4, *refs), out_sh...]
    ppermute x15, waiting for transfers between devices: 8.29 us -> 9.51 us  [swap(): lax.ppermute(array, 'patch', [(rank, rank ^ offset) for rank in range(cou...]
    unnamed x31 -> x25, local copies, waits for them, and re-layouts: 7.56 us -> 7.53 us
  transfers between devices with their start and end apart: 22 -> 22, of which waited for: 7 -> 5; matrix products, arithmetic and copies ran while one was open for 0% -> 0% of each run, Pallas kernels for 16% -> 16%
where the time goes in v2:
time: 99.2 us; the launch traced here: 98.8 us
  waiting for transfers between devices  24.1 us (24%)
  Pallas kernels  23.7 us (24%)
  starting transfers between devices  21.9 us (22%)
  blocking collectives  21.3 us (21%)
  local copies, waits for them, and re-layouts  7.53 us (8%)
    all_to_all x1, blocking collectives, exchange(): pieces = lax.all_to_all(pieces, 'frame', 0, 0, tiled=True)  21.3 us
    ppermute x6, starting transfers between devices, ring_step(): return lax.ppermute(array, ('frame', 'patch'), pairs)  9.92 us
    ppermute x15, waiting for transfers between devices, swap(): lax.ppermute(array, 'patch', [(rank, rank ^ offset) for rank in range(cou...  9.51 us
    pallas_call x4, Pallas kernels, spatial_attention(): pl.pallas_call(lambda *refs: attention_kernel(parts, *refs), out_shape=ja...  9.07 us
    pallas_call x1, Pallas kernels, temporal_block(): pl.pallas_call(lambda *refs: temporal_kernel(positions, 4, *refs), out_sh...  7.62 us
    ppermute x15, starting transfers between devices, swap(): lax.ppermute(array, 'patch', [(rank, rank ^ offset) for rank in range(cou...  7.55 us
    unnamed x25, local copies, waits for them, and re-layouts  7.53 us
    all_to_all x1, waiting for transfers between devices, exchange(): pieces = lax.all_to_all(pieces, 'frame', 0, 0, tiled=True)  7.48 us
  transfers between devices with their start and end apart: 22, of which 5 were waited for; matrix products, arithmetic and copies ran while one was open for 0% of the time, Pallas kernels for 16%

profile of v2, /device:TPU:0, one launch (start us, length us, event | category | flops | bytes accessed | tf_op | source)
XLA Modules:
  0.0 98.8 jit_solution(16702043092740440303)
XLA Ops:
  0.0 0.5 collective-permute-start
  0.5 2.5 %collective-permute-start.1 = (bf16[256,1152]{1,0:T(8,128)(2,1)}, bf16[256,1152]{1,0:T(8,128)(2,1)S(1)}, u32[]{:S(2)}, u32[]{:S(2)}) collective-permute-start(bf16[256,1152]{1,0:T(8,128)(2,1)} %bitcast.16), channel_id=1, source_target_pairs={{0,2},{1,3},{2,0},{3,1},{4,6},{5,7},{6,4},{7,5},{8,10},{9,11},{10,... | collective-permute-start | bytes 1769480 | tf_op jit(solution)/shard_map/ppermute | solution.py:333
  2.9 1.2 %copy-done.5 = bf16[1152,432]{0,1:T(8,128)(2,1)S(1)} copy-done((bf16[1152,432]{0,1:T(8,128)(2,1)S(1)}, bf16[1152,432]{0,1:T(8,128)(2,1)}, u32[]{:S(2)}) %copy-start.5) | copy-done | bytes 995352
  4.2 1.0 copy-done.7
  5.1 0.1 pack.1
  5.2 1.6 %collective-permute-start.2 = (bf16[288,1152]{1,0:T(8,128)(2,1)S(1)}, bf16[288,1152]{1,0:T(8,128)(2,1)S(1)}, u32[]{:S(2)}, u32[]{:S(2)}) collective-permute-start(bf16[288,1152]{1,0:T(8,128)(2,1)S(1)} %get-tuple-element.95.refs_3_), channel_id=1, source_target_pairs={{0,8},{1,5},{2,10},{3,7},{8,16},{9,1},{10,18},{11,3},{16,24},{17,9... | collective-permute-start | bytes 1990664 | tf_op jit(solution)/shard_map/ppermute | solution.py:344
  6.9 0.0 collective-permute-start.4
  6.9 1.6 %collective-permute-start.5 = (bf16[288,1152]{1,0:T(8,128)(2,1)S(1)}, bf16[288,1152]{1,0:T(8,128)(2,1)S(1)}, u32[]{:S(2)}, u32[]{:S(2)}) collective-permute-start(bf16[288,1152]{1,0:T(8,128)(2,1)S(1)} %get-tuple-element.109.refs_4_), channel_id=1, source_target_pairs={{0,8},{1,5},{2,10},{3,7},{8,16},{9,1},{10,18},{11,3},{16,24},{17,9... | collective-permute-start | bytes 1990664 | tf_op jit(solution)/shard_map/ppermute | solution.py:344
  8.4 1.6 %copy-done = bf16[1152,864]{0,1:T(8,128)(2,1)S(1)} copy-done((bf16[1152,864]{0,1:T(8,128)(2,1)S(1)}, bf16[1152,864]{0,1:T(8,128)(2,1)}, u32[]{:S(2)}) %copy-start) | copy-done | bytes 1990680
  10.0 1.1 %copy-done.3 = bf16[1,256,1152]{2,1,0:T(8,128)(2,1)S(1)} copy-done((bf16[1,256,1152]{2,1,0:T(8,128)(2,1)S(1)}, bf16[1,256,1152]{2,1,0:T(8,128)(2,1)}, u32[]{:S(2)}) %copy-start.3) | copy-done | bytes 589848
  11.1 0.7 copy-done.8
  11.8 1.2 %spatial_qkv.4 = (bf16[8,80,256]{2,1,0:T(8,128)(2,1)S(1)}, bf16[4,256,80]{2,1,0:T(8,128)(2,1)S(1)}) custom-call(bf16[256,1152]{1,0:T(8,128)(2,1)S(1)} %bitcast.17, f32[3,1152]{1,0:T(4,128)S(1)} %copy-done.8, bf16[864,1152]{1,0:T(8,128)(2,1)S(1)} %bitcast.8), custom_call_target="tpu_custom_call" | custom-call | flops 1 | bytes 1 | tf_op jit(solution)/shard_map/spatial_qkv/pallas_call | solution.py:70
  13.0 0.4 copy-done.1
  13.3 1.2 %spatial_qkv.5 = (bf16[8,80,256]{2,1,0:T(8,128)(2,1)S(1)}, bf16[4,256,80]{2,1,0:T(8,128)(2,1)S(1)}) custom-call(bf16[256,1152]{1,0:T(8,128)(2,1)S(1)} %collective-permute-done.tokens_ref, f32[3,1152]{1,0:T(4,128)S(1)} %copy-done.8, bf16[864,1152]{1,0:T(8,128)(2,1)S(1)} %bitcast.9), custom_call_target="tpu_custom_call" | custom-call | flops 1 | bytes 1 | tf_op jit(solution)/shard_map/spatial_qkv/pallas_call | solution.py:70
  14.5 2.6 %collective-permute-done.1.tokens_ref = bf16[256,1152]{1,0:T(8,128)(2,1)S(1)} collective-permute-done((bf16[256,1152]{1,0:T(8,128)(2,1)}, bf16[256,1152]{1,0:T(8,128)(2,1)S(1)}, u32[]{:S(2)}, u32[]{:S(2)}) %collective-permute-start.1) | collective-permute-done | bytes 589856 | tf_op jit(solution)/shard_map/ppermute | solution.py:333
  17.2 0.0 collective-permute-start.3
  17.2 1.2 %spatial_qkv.6 = (bf16[8,80,256]{2,1,0:T(8,128)(2,1)S(1)}, bf16[4,256,80]{2,1,0:T(8,128)(2,1)S(1)}) custom-call(bf16[256,1152]{1,0:T(8,128)(2,1)S(1)} %collective-permute-done.1.tokens_ref, f32[3,1152]{1,0:T(4,128)S(1)} %copy-done.9, bf16[864,1152]{1,0:T(8,128)(2,1)S(1)} %bitcast.10), custom_call_target="tpu_custom_call" | custom-call | flops 1610612736 | bytes 1 | tf_op jit(solution)/shard_map/spatial_qkv/pallas_call | solution.py:70
  18.3 0.0 collective-permute-done.2.refs_5_
  18.3 1.9 %collective-permute-start.7 = (bf16[288,1152]{1,0:T(8,128)(2,1)S(1)}, bf16[288,1152]{1,0:T(8,128)(2,1)S(1)}, u32[]{:S(2)}, u32[]{:S(2)}) collective-permute-start(bf16[288,1152]{1,0:T(8,128)(2,1)S(1)} %collective-permute-done.2.refs_5_), channel_id=1, source_target_pairs={{0,8},{1,5},{2,10},{3,7},{8,16},{9,1},{10,18},{11,3},{16,24},{17,9... | collective-permute-start | bytes 1990664 | tf_op jit(solution)/shard_map/ppermute | solution.py:344
  20.2 1.2 %spatial_qkv.7 = (bf16[8,80,256]{2,1,0:T(8,128)(2,1)S(1)}, bf16[4,256,80]{2,1,0:T(8,128)(2,1)S(1)}) custom-call(bf16[256,1152]{1,0:T(8,128)(2,1)S(1)} %collective-permute-done.3.tokens_ref, f32[3,1152]{1,0:T(4,128)S(1)} %copy-done.9, bf16[864,1152]{1,0:T(8,128)(2,1)S(1)} %bitcast.11), custom_call_target="tpu_custom_call" | custom-call | flops 1 | bytes 1 | tf_op jit(solution)/shard_map/spatial_qkv/pallas_call | solution.py:70
  21.4 0.0 collective-permute-done.4.other_weight_ref
  21.4 2.3 %spatial_attention.4 = bf16[256,288]{1,0:T(8,128)(2,1)S(1)} custom-call(bf16[8,80,256]{2,1,0:T(8,128)(2,1)S(1)} %get-tuple-element.133.refs_0_.refs_4_, bf16[8,80,256]{2,1,0:T(8,128)(2,1)S(1)} %get-tuple-element.130.refs_1_.refs_0_, bf16[8,80,256]{2,1,0:T(8,128)(2,1)S(1)} %get-tuple-element.131.refs_2_.refs_0_, ...), custom_call_target="tpu_custom_call" | custom-call | flops 1 | bytes 1 | tf_op jit(solution)/shard_map/spatial_attention/pallas_call | solution.py:105
  23.7 0.0 copy-start.2
  23.7 0.0 collective-permute-done.5.refs_6_
  23.7 0.2 collective-permute-start.6
  23.9 2.3 %spatial_attention.5.heads_ref = bf16[256,288]{1,0:T(8,128)(2,1)S(1)} custom-call(bf16[8,80,256]{2,1,0:T(8,128)(2,1)S(1)} %get-tuple-element.132.refs_3_.refs_0_, bf16[8,80,256]{2,1,0:T(8,128)(2,1)S(1)} %get-tuple-element.130.refs_1_.refs_0_, bf16[8,80,256]{2,1,0:T(8,128)(2,1)S(1)} %get-tuple-element.131.refs_2_.refs_0_, ...), custom_call_target="tpu_custom_call" | custom-call | flops 1 | bytes 1 | tf_op jit(solution)/shard_map/spatial_attention/pallas_call | solution.py:105
  26.2 0.0 collective-permute-done.6.other_ref
  26.2 0.8 chip_partial.1
  27.1 1.6 %collective-permute-start.9 = (bf16[256,1152]{1,0:T(8,128)(2,1)S(1)}, bf16[256,1152]{1,0:T(8,128)(2,1)S(1)}, u32[]{:S(2)}, u32[]{:S(2)}) collective-permute-start(bf16[256,1152]{1,0:T(8,128)(2,1)S(1)} %chip_partial.1), channel_id=1, source_target_pairs={{0,2},{1,3},{2,0},{3,1},{4,6},{5,7},{6,4},{7,5},{8,10},{9,11},{10,... | collective-permute-start | bytes 1769480 | tf_op jit(solution)/shard_map/ppermute | solution.py:333
  28.6 2.3 %spatial_attention.6 = bf16[256,288]{1,0:T(8,128)(2,1)S(1)} custom-call(bf16[8,80,256]{2,1,0:T(8,128)(2,1)S(1)} %get-tuple-element.131.refs_2_.refs_0_, bf16[8,80,256]{2,1,0:T(8,128)(2,1)S(1)} %get-tuple-element.130.refs_1_.refs_0_, bf16[8,80,256]{2,1,0:T(8,128)(2,1)S(1)} %get-tuple-element.131.refs_2_.refs_0_, ...), custom_call_target="tpu_custom_call" | custom-call | flops 1 | bytes 1 | tf_op jit(solution)/shard_map/spatial_attention/pallas_call | solution.py:105
  30.9 0.0 copy-start.4
  30.9 1.6 %collective-permute-start.10 = (bf16[288,1152]{1,0:T(8,128)(2,1)S(1)}, bf16[288,1152]{1,0:T(8,128)(2,1)}, u32[]{:S(2)}, u32[]{:S(2)}) collective-permute-start(bf16[288,1152]{1,0:T(8,128)(2,1)S(1)} %collective-permute-done.7.refs_9_), channel_id=1, source_target_pairs={{0,8},{1,5},{2,10},{3,7},{8,16},{9,1},{10,18},{11,3},{16,24},{17,9... | collective-permute-start | bytes 1990664 | tf_op jit(solution)/shard_map/ppermute | solution.py:344
  32.6 2.3 %spatial_attention.7.heads_ref = bf16[256,288]{1,0:T(8,128)(2,1)S(1)} custom-call(bf16[8,80,256]{2,1,0:T(8,128)(2,1)S(1)} %get-tuple-element.130.refs_1_.refs_0_, bf16[8,80,256]{2,1,0:T(8,128)(2,1)S(1)} %get-tuple-element.130.refs_1_.refs_0_, bf16[8,80,256]{2,1,0:T(8,128)(2,1)S(1)} %get-tuple-element.131.refs_2_.refs_0_, ...), custom_call_target="tpu_custom_call" | custom-call | flops 1 | bytes 1 | tf_op jit(solution)/shard_map/spatial_attention/pallas_call | solution.py:105
  34.8 0.1 collective-permute-start.8
  34.9 1.6 %collective-permute-start.14 = (bf16[288,1152]{1,0:T(8,128)(2,1)S(1)}, bf16[288,1152]{1,0:T(8,128)(2,1)}, u32[]{:S(2)}, u32[]{:S(2)}) collective-permute-start(bf16[288,1152]{1,0:T(8,128)(2,1)S(1)} %collective-permute-done.5.refs_6_), channel_id=1, source_target_pairs={{0,8},{1,5},{2,10},{3,7},{8,16},{9,1},{10,18},{11,3},{16,24},{17,9... | collective-permute-start | bytes 1990664 | tf_op jit(solution)/shard_map/ppermute | solution.py:344
  36.6 0.0 collective-permute-done.8.other_ref
  36.6 0.8 spatial_base.1.base_ref
  37.4 0.0 copy-start.10
  37.4 0.1 collective-permute-start.11
  37.5 0.5 collective-permute-start.12
  38.0 4.7 %collective-permute-done.9.refs_0_ = bf16[256,1152]{1,0:T(8,128)(2,1)S(1)} collective-permute-done((bf16[256,1152]{1,0:T(8,128)(2,1)S(1)}, bf16[256,1152]{1,0:T(8,128)(2,1)S(1)}, u32[]{:S(2)}, u32[]{:S(2)}) %collective-permute-start.9) | collective-permute-done | bytes 589856 | tf_op jit(solution)/shard_map/ppermute | solution.py:333
  42.7 0.2 spatial_add.1
  42.9 0.0 copy-start.6
  42.9 0.8 copy-done.6
  43.7 0.0 collective-permute-done.10.refs_13_
  43.7 1.6 %collective-permute-start.19 = (bf16[288,1152]{1,0:T(8,128)(2,1)}, bf16[288,1152]{1,0:T(8,128)(2,1)}, u32[]{:S(2)}, u32[]{:S(2)}) collective-permute-start(bf16[288,1152]{1,0:T(8,128)(2,1)} %collective-permute-done.10.refs_13_), channel_id=1, source_target_pairs={{0,8},{1,5},{2,10},{3,7},{8,16},{9,1},{10,18},{11,3},{16,24},{17,9... | collective-permute-start | bytes 1990664 | tf_op jit(solution)/shard_map/ppermute | solution.py:344
  45.3 1.5 %collective-permute-start.17 = (bf16[288,1152]{1,0:T(8,128)(2,1)}, bf16[288,1152]{1,0:T(8,128)(2,1)}, u32[]{:S(2)}, u32[]{:S(2)}) collective-permute-start(bf16[288,1152]{1,0:T(8,128)(2,1)} %collective-permute-done.10.refs_13_), channel_id=1, source_target_pairs={{0,2},{1,3},{2,0},{3,1},{4,6},{5,7},{6,4},{7,5},{8,10},{9,11},{10,... | collective-permute-start | bytes 1990664 | tf_op jit(solution)/shard_map/ppermute | solution.py:333
  46.8 4.4 %all-to-all-start = ((bf16[8,32,1152]{2,1,0:T(8,128)(2,1)}), bf16[8,32,1152]{2,1,0:T(8,128)(2,1)S(1)}, u32[]{:S(2)}, u32[]{:S(2)}) async-start(bf16[8,32,1152]{2,1,0:T(8,128)(2,1)} %bitcast.20), calls=%async_computation | async-start | bytes 1179648 | tf_op jit(solution)/shard_map/all_to_all | solution.py:356
  51.2 0.1 collective-permute-start.13
  51.3 0.0 collective-permute-done.11.refs_7_
  51.3 0.5 collective-permute-start.16
  51.8 0.0 collective-permute-done.12.refs_8_
  51.8 0.1 collective-permute-start.15
  51.9 7.1 %collective-permute-done.19.refs_17_ = bf16[288,1152]{1,0:T(8,128)(2,1)} collective-permute-done((bf16[288,1152]{1,0:T(8,128)(2,1)}, bf16[288,1152]{1,0:T(8,128)(2,1)}, u32[]{:S(2)}, u32[]{:S(2)}) %collective-permute-start.19) | collective-permute-done | bytes 663584 | tf_op jit(solution)/shard_map/ppermute | solution.py:344
  58.9 0.0 collective-permute-start.20
  58.9 2.1 %collective-permute-done.17.refs_15_ = bf16[288,1152]{1,0:T(8,128)(2,1)} collective-permute-done((bf16[288,1152]{1,0:T(8,128)(2,1)}, bf16[288,1152]{1,0:T(8,128)(2,1)}, u32[]{:S(2)}, u32[]{:S(2)}) %collective-permute-start.17) | collective-permute-done | bytes 663584 | tf_op jit(solution)/shard_map/ppermute | solution.py:333
  61.1 0.0 collective-permute-start.18
  61.1 7.5 %all-to-all-done = bf16[8,32,1152]{2,1,0:T(8,128)(2,1)S(1)} async-done(((bf16[8,32,1152]{2,1,0:T(8,128)(2,1)}), bf16[8,32,1152]{2,1,0:T(8,128)(2,1)S(1)}, u32[]{:S(2)}, u32[]{:S(2)}) %all-to-all-start) | async-done | bytes 589856 | tf_op jit(solution)/shard_map/all_to_all | solution.py:356
  68.6 0.4 temporal_norm.1.refs_1_
  69.0 0.0 collective-permute-done.13.refs_10_
  69.0 0.0 collective-permute-done.20.refs_18_
  69.0 7.6 %temporal_block.1 = bf16[256,1152]{1,0:T(8,128)(2,1)S(1)} custom-call(bf16[256,1152]{1,0:T(8,128)(2,1)S(1)} %bitcast.13, bf16[256,1152]{1,0:T(8,128)(2,1)S(1)} %temporal_norm.1.refs_1_, f32[3,1152]{1,0:T(4,128)S(1)} %copy-done.10, bf16[288,1152]{1,0:T(8,128)(2,1)S(1)} %get-tuple-element.95.refs_3_, bf16[288,1152]{1,0:T(8,128)(2,1)S(1)} %get-tuple-element.109.refs_4_, ...), custom_call_target="tpu_custom_call" | custom-call | flops 1 | bytes 1 | tf_op jit(solution)/shard_map/temporal_block/pallas_call | solution.py:315
  76.7 21.3 %all_to_all.10 = bf16[8,32,1152]{2,1,0:T(8,128)(2,1)S(1)} all-to-all(bf16[8,32,1152]{2,1,0:T(8,128)(2,1)S(1)} %bitcast.14), channel_id=1, replica_groups=mesh['frame'=8,'patch'=4] {'frame'}, dimensions={0} | all-to-all | bytes 1179648 | tf_op jit(solution)/shard_map/all_to_all | solution.py:356
  97.9 0.8 copy.9
  (20 shorter events, 0.0 us)
Async XLA Ops:
  0.0 13.0 %collective-permute-start = (bf16[256,1152]{1,0:T(8,128)(2,1)}, bf16[256,1152]{1,0:T(8,128)(2,1)S(1)}, u32[]{:S(2)}, u32[]{:S(2)}) collective-permute-start(bf16[256,1152]{1,0:T(8,128)(2,1)} %bitcast.15), channel_id=1, source_target_pairs={{0,1},{1,0},{2,3},{3,2},{4,5},{5,4},{6,7},{7,6},{8,9},{9,8},{10,11... | collective-permute-start | bytes 1769480 | tf_op jit(solution)/shard_map/ppermute | solution.py:333
  0.5 16.7 %collective-permute-start.1 = (bf16[256,1152]{1,0:T(8,128)(2,1)}, bf16[256,1152]{1,0:T(8,128)(2,1)S(1)}, u32[]{:S(2)}, u32[]{:S(2)}) collective-permute-start(bf16[256,1152]{1,0:T(8,128)(2,1)} %bitcast.16), channel_id=1, source_target_pairs={{0,2},{1,3},{2,0},{3,1},{4,6},{5,7},{6,4},{7,5},{8,10},{9,11},{10,... | collective-permute-start | bytes 1769480 | tf_op jit(solution)/shard_map/ppermute | solution.py:333
  2.9 1.2 %copy-start.5 = (bf16[1152,432]{0,1:T(8,128)(2,1)S(1)}, bf16[1152,432]{0,1:T(8,128)(2,1)}, u32[]{:S(2)}) copy-start(bf16[1152,432]{0,1:T(8,128)(2,1)} %param.12) | copy-start | bytes 2985988
  4.1 1.0 copy-start.7
  5.2 13.1 %collective-permute-start.2 = (bf16[288,1152]{1,0:T(8,128)(2,1)S(1)}, bf16[288,1152]{1,0:T(8,128)(2,1)S(1)}, u32[]{:S(2)}, u32[]{:S(2)}) collective-permute-start(bf16[288,1152]{1,0:T(8,128)(2,1)S(1)} %get-tuple-element.95.refs_3_), channel_id=1, source_target_pairs={{0,8},{1,5},{2,10},{3,7},{8,16},{9,1},{10,18},{11,3},{16,24},{17,9... | collective-permute-start | bytes 1990664 | tf_op jit(solution)/shard_map/ppermute | solution.py:344
  6.9 14.5 %collective-permute-start.4 = (bf16[288,1152]{1,0:T(8,128)(2,1)}, bf16[288,1152]{1,0:T(8,128)(2,1)S(1)}, u32[]{:S(2)}, u32[]{:S(2)}) collective-permute-start(bf16[288,1152]{1,0:T(8,128)(2,1)} %weight_ref.3), channel_id=1, source_target_pairs={{0,1},{1,0},{2,3},{3,2},{4,5},{5,4},{6,7},{7,6},{8,9},{9,8},{10,11... | collective-permute-start | bytes 1990664 | tf_op jit(solution)/shard_map/ppermute | solution.py:333
  6.9 16.8 %collective-permute-start.5 = (bf16[288,1152]{1,0:T(8,128)(2,1)S(1)}, bf16[288,1152]{1,0:T(8,128)(2,1)S(1)}, u32[]{:S(2)}, u32[]{:S(2)}) collective-permute-start(bf16[288,1152]{1,0:T(8,128)(2,1)S(1)} %get-tuple-element.109.refs_4_), channel_id=1, source_target_pairs={{0,8},{1,5},{2,10},{3,7},{8,16},{9,1},{10,18},{11,3},{16,24},{17,9... | collective-permute-start | bytes 1990664 | tf_op jit(solution)/shard_map/ppermute | solution.py:344
  8.4 1.6 %copy-start = (bf16[1152,864]{0,1:T(8,128)(2,1)S(1)}, bf16[1152,864]{0,1:T(8,128)(2,1)}, u32[]{:S(2)}) copy-start(bf16[1152,864]{0,1:T(8,128)(2,1)} %param.9) | copy-start | bytes 5971972
  10.0 1.1 %copy-start.3 = (bf16[1,256,1152]{2,1,0:T(8,128)(2,1)S(1)}, bf16[1,256,1152]{2,1,0:T(8,128)(2,1)}, u32[]{:S(2)}) copy-start(bf16[1,256,1152]{2,1,0:T(8,128)(2,1)} %param.7) | copy-start | bytes 1769476
  11.1 0.7 copy-start.8
  11.8 1.6 %copy-start.1 = (bf16[1152,864]{0,1:T(8,128)(2,1)S(1)}, bf16[1152,864]{0,1:T(8,128)(2,1)}, u32[]{:S(2)}) copy-start(bf16[1152,864]{0,1:T(8,128)(2,1)} %param.9) | copy-start | bytes 5971972
  11.8 5.4 %copy-start.9 = (f32[3,1152]{1,0:T(4,128)S(1)}, f32[3,1152]{1,0:T(4,128)}, u32[]{:S(2)}) copy-start(f32[3,1152]{1,0:T(4,128)} %mod_ref.11) | copy-start | bytes 41476
  17.2 3.1 %collective-permute-start.3 = (bf16[256,1152]{1,0:T(8,128)(2,1)S(1)}, bf16[256,1152]{1,0:T(8,128)(2,1)S(1)}, u32[]{:S(2)}, u32[]{:S(2)}) collective-permute-start(bf16[256,1152]{1,0:T(8,128)(2,1)S(1)} %collective-permute-done.1.tokens_ref), channel_id=1, source_target_pairs={{0,1},{1,0},{2,3},{3,2},{4,5},{5,4},{6,7},{7,6},{8,9},{9,8},{10,11... | collective-permute-start | bytes 1769480 | tf_op jit(solution)/shard_map/ppermute | solution.py:333
  18.3 12.6 %collective-permute-start.7 = (bf16[288,1152]{1,0:T(8,128)(2,1)S(1)}, bf16[288,1152]{1,0:T(8,128)(2,1)S(1)}, u32[]{:S(2)}, u32[]{:S(2)}) collective-permute-start(bf16[288,1152]{1,0:T(8,128)(2,1)S(1)} %collective-permute-done.2.refs_5_), channel_id=1, source_target_pairs={{0,8},{1,5},{2,10},{3,7},{8,16},{9,1},{10,18},{11,3},{16,24},{17,9... | collective-permute-start | bytes 1990664 | tf_op jit(solution)/shard_map/ppermute | solution.py:344
  23.7 2.5 %copy-start.2 = (bf16[288,1152]{1,0:T(8,128)(2,1)S(1)}, bf16[288,1152]{1,0:T(8,128)(2,1)}, u32[]{:S(2)}) copy-start(bf16[288,1152]{1,0:T(8,128)(2,1)} %weight_ref.3) | copy-start | bytes 1990660
  23.7 2.5 %collective-permute-start.6 = (bf16[256,288]{1,0:T(8,128)(2,1)S(1)}, bf16[256,288]{1,0:T(8,128)(2,1)S(1)}, u32[]{:S(2)}, u32[]{:S(2)}) collective-permute-start(bf16[256,288]{1,0:T(8,128)(2,1)S(1)} %spatial_attention.4), channel_id=1, source_target_pairs={{0,1},{1,0},{2,3},{3,2},{4,5},{5,4},{6,7},{7,6},{8,9},{9,8},{10,11... | collective-permute-start | bytes 442376 | tf_op jit(solution)/shard_map/ppermute | solution.py:333
  27.1 15.6 %collective-permute-start.9 = (bf16[256,1152]{1,0:T(8,128)(2,1)S(1)}, bf16[256,1152]{1,0:T(8,128)(2,1)S(1)}, u32[]{:S(2)}, u32[]{:S(2)}) collective-permute-start(bf16[256,1152]{1,0:T(8,128)(2,1)S(1)} %chip_partial.1), channel_id=1, source_target_pairs={{0,2},{1,3},{2,0},{3,1},{4,6},{5,7},{6,4},{7,5},{8,10},{9,11},{10,... | collective-permute-start | bytes 1769480 | tf_op jit(solution)/shard_map/ppermute | solution.py:333
  30.9 5.6 %copy-start.4 = (bf16[1,256,1152]{2,1,0:T(8,128)(2,1)S(1)}, bf16[1,256,1152]{2,1,0:T(8,128)(2,1)}, u32[]{:S(2)}) copy-start(bf16[1,256,1152]{2,1,0:T(8,128)(2,1)} %param.7) | copy-start | bytes 1769476
  30.9 6.5 %copy-start.11 = (bf16[288,1152]{1,0:T(8,128)(2,1)}, bf16[288,1152]{1,0:T(8,128)(2,1)S(1)}, u32[]{:S(2)}) copy-start(bf16[288,1152]{1,0:T(8,128)(2,1)S(1)} %collective-permute-done.7.refs_9_) | copy-start | bytes 1990660
  30.9 12.8 %collective-permute-start.10 = (bf16[288,1152]{1,0:T(8,128)(2,1)S(1)}, bf16[288,1152]{1,0:T(8,128)(2,1)}, u32[]{:S(2)}, u32[]{:S(2)}) collective-permute-start(bf16[288,1152]{1,0:T(8,128)(2,1)S(1)} %collective-permute-done.7.refs_9_), channel_id=1, source_target_pairs={{0,8},{1,5},{2,10},{3,7},{8,16},{9,1},{10,18},{11,3},{16,24},{17,9... | collective-permute-start | bytes 1990664 | tf_op jit(solution)/shard_map/ppermute | solution.py:344
  34.8 1.7 %collective-permute-start.8 = (bf16[256,288]{1,0:T(8,128)(2,1)S(1)}, bf16[256,288]{1,0:T(8,128)(2,1)S(1)}, u32[]{:S(2)}, u32[]{:S(2)}) collective-permute-start(bf16[256,288]{1,0:T(8,128)(2,1)S(1)} %spatial_attention.6), channel_id=1, source_target_pairs={{0,1},{1,0},{2,3},{3,2},{4,5},{5,4},{6,7},{7,6},{8,9},{9,8},{10,11... | collective-permute-start | bytes 442376 | tf_op jit(solution)/shard_map/ppermute | solution.py:333
  34.9 16.3 %collective-permute-start.14 = (bf16[288,1152]{1,0:T(8,128)(2,1)S(1)}, bf16[288,1152]{1,0:T(8,128)(2,1)}, u32[]{:S(2)}, u32[]{:S(2)}) collective-permute-start(bf16[288,1152]{1,0:T(8,128)(2,1)S(1)} %collective-permute-done.5.refs_6_), channel_id=1, source_target_pairs={{0,8},{1,5},{2,10},{3,7},{8,16},{9,1},{10,18},{11,3},{16,24},{17,9... | collective-permute-start | bytes 1990664 | tf_op jit(solution)/shard_map/ppermute | solution.py:344
  37.4 31.1 %copy-start.10 = (f32[3,1152]{1,0:T(4,128)S(1)}, f32[3,1152]{1,0:T(4,128)}, u32[]{:S(2)}) copy-start(f32[3,1152]{1,0:T(4,128)} %refs_2_.1) | copy-start | bytes 41476
  37.4 13.9 %collective-permute-start.11 = (bf16[288,1152]{1,0:T(8,128)(2,1)S(1)}, bf16[288,1152]{1,0:T(8,128)(2,1)}, u32[]{:S(2)}, u32[]{:S(2)}) collective-permute-start(bf16[288,1152]{1,0:T(8,128)(2,1)S(1)} %collective-permute-done.2.refs_5_), channel_id=1, source_target_pairs={{0,1},{1,0},{2,3},{3,2},{4,5},{5,4},{6,7},{7,6},{8,9},{9,8},{10,11... | collective-permute-start | bytes 1990664 | tf_op jit(solution)/shard_map/ppermute | solution.py:333
  37.5 14.3 %collective-permute-start.12 = (bf16[288,1152]{1,0:T(8,128)(2,1)S(1)}, bf16[288,1152]{1,0:T(8,128)(2,1)}, u32[]{:S(2)}, u32[]{:S(2)}) collective-permute-start(bf16[288,1152]{1,0:T(8,128)(2,1)S(1)} %collective-permute-done.5.refs_6_), channel_id=1, source_target_pairs={{0,1},{1,0},{2,3},{3,2},{4,5},{5,4},{6,7},{7,6},{8,9},{9,8},{10,11... | collective-permute-start | bytes 1990664 | tf_op jit(solution)/shard_map/ppermute | solution.py:333
  42.9 0.8 copy-start.6
  43.7 15.2 %collective-permute-start.19 = (bf16[288,1152]{1,0:T(8,128)(2,1)}, bf16[288,1152]{1,0:T(8,128)(2,1)}, u32[]{:S(2)}, u32[]{:S(2)}) collective-permute-start(bf16[288,1152]{1,0:T(8,128)(2,1)} %collective-permute-done.10.refs_13_), channel_id=1, source_target_pairs={{0,8},{1,5},{2,10},{3,7},{8,16},{9,1},{10,18},{11,3},{16,24},{17,9... | collective-permute-start | bytes 1990664 | tf_op jit(solution)/shard_map/ppermute | solution.py:344
  45.3 15.8 %collective-permute-start.17 = (bf16[288,1152]{1,0:T(8,128)(2,1)}, bf16[288,1152]{1,0:T(8,128)(2,1)}, u32[]{:S(2)}, u32[]{:S(2)}) collective-permute-start(bf16[288,1152]{1,0:T(8,128)(2,1)} %collective-permute-done.10.refs_13_), channel_id=1, source_target_pairs={{0,2},{1,3},{2,0},{3,1},{4,6},{5,7},{6,4},{7,5},{8,10},{9,11},{10,... | collective-permute-start | bytes 1990664 | tf_op jit(solution)/shard_map/ppermute | solution.py:333
  46.8 21.8 %all-to-all-start = ((bf16[8,32,1152]{2,1,0:T(8,128)(2,1)}), bf16[8,32,1152]{2,1,0:T(8,128)(2,1)S(1)}, u32[]{:S(2)}, u32[]{:S(2)}) async-start(bf16[8,32,1152]{2,1,0:T(8,128)(2,1)} %bitcast.20), calls=%async_computation | async-start | bytes 1179648 | tf_op jit(solution)/shard_map/all_to_all | solution.py:356
  51.2 17.8 %collective-permute-start.13 = (bf16[288,1152]{1,0:T(8,128)(2,1)}, bf16[288,1152]{1,0:T(8,128)(2,1)}, u32[]{:S(2)}, u32[]{:S(2)}) collective-permute-start(bf16[288,1152]{1,0:T(8,128)(2,1)} %copy-done.11), channel_id=1, source_target_pairs={{0,1},{1,0},{2,3},{3,2},{4,5},{5,4},{6,7},{7,6},{8,9},{9,8},{10,11... | collective-permute-start | bytes 1990664 | tf_op jit(solution)/shard_map/ppermute | solution.py:333
  51.3 17.7 %collective-permute-start.16 = (bf16[288,1152]{1,0:T(8,128)(2,1)}, bf16[288,1152]{1,0:T(8,128)(2,1)}, u32[]{:S(2)}, u32[]{:S(2)}) collective-permute-start(bf16[288,1152]{1,0:T(8,128)(2,1)} %collective-permute-done.10.refs_13_), channel_id=1, source_target_pairs={{0,1},{1,0},{2,3},{3,2},{4,5},{5,4},{6,7},{7,6},{8,9},{9,8},{10,11... | collective-permute-start | bytes 1990664 | tf_op jit(solution)/shard_map/ppermute | solution.py:333
  51.8 17.2 %collective-permute-start.15 = (bf16[288,1152]{1,0:T(8,128)(2,1)}, bf16[288,1152]{1,0:T(8,128)(2,1)}, u32[]{:S(2)}, u32[]{:S(2)}) collective-permute-start(bf16[288,1152]{1,0:T(8,128)(2,1)} %collective-permute-done.14.refs_11_), channel_id=1, source_target_pairs={{0,1},{1,0},{2,3},{3,2},{4,5},{5,4},{6,7},{7,6},{8,9},{9,8},{10,11... | collective-permute-start | bytes 1990664 | tf_op jit(solution)/shard_map/ppermute | solution.py:333
  58.9 10.1 %collective-permute-start.20 = (bf16[288,1152]{1,0:T(8,128)(2,1)}, bf16[288,1152]{1,0:T(8,128)(2,1)}, u32[]{:S(2)}, u32[]{:S(2)}) collective-permute-start(bf16[288,1152]{1,0:T(8,128)(2,1)} %collective-permute-done.19.refs_17_), channel_id=1, source_target_pairs={{0,1},{1,0},{2,3},{3,2},{4,5},{5,4},{6,7},{7,6},{8,9},{9,8},{10,11... | collective-permute-start | bytes 1990664 | tf_op jit(solution)/shard_map/ppermute | solution.py:333
  61.1 8.0 %collective-permute-start.18 = (bf16[288,1152]{1,0:T(8,128)(2,1)}, bf16[288,1152]{1,0:T(8,128)(2,1)}, u32[]{:S(2)}, u32[]{:S(2)}) collective-permute-start(bf16[288,1152]{1,0:T(8,128)(2,1)} %collective-permute-done.17.refs_15_), channel_id=1, source_target_pairs={{0,1},{1,0},{2,3},{3,2},{4,5},{5,4},{6,7},{7,6},{8,9},{9,8},{10,11... | collective-permute-start | bytes 1990664 | tf_op jit(solution)/shard_map/ppermute | solution.py:333

commit v3 on v2

--- a/solution.py
+++ b/solution.py
@@ -191,9 +191,13 @@
     )(place, qkv, out)
 
 
-def temporal_kernel(positions, group, tokens_ref, moved_ref, mod_ref, *refs):
+def frame_start(frame_ref, offset, positions):
+    return pl.multiple_of((frame_ref[0] ^ offset) * positions, positions)
+
+
+def temporal_kernel(positions, group, frame_ref, tokens_ref, moved_ref, mod_ref, *refs):
     resident_refs, streamed_refs = refs[:RESIDENT], refs[RESIDENT:HEADS]
-    result_ref, heads_scratch, qkv_scratch, out_scratch, sems = refs[HEADS:]
+    *piece_refs, result_ref, heads_scratch, qkv_scratch, out_scratch, sems = refs[HEADS:]
     streamed = len(streamed_refs)
     copies = []
     for index, ref in enumerate(streamed_refs):
@@ -276,7 +280,10 @@
         result_ref[pl.ds(start, piece), :] = (
             tokens[start : start + piece].astype(jnp.float32)
             + mod_ref[2:3, :] * total[place : place + piece]
-        ).astype(jnp.bfloat16)
+        )
+    for offset, piece_ref in enumerate(piece_refs):
+        start = frame_start(frame_ref, offset, positions)
+        piece_ref[...] = result_ref[pl.ds(start, positions), :].astype(jnp.bfloat16)
 
 
 def halves_of(positions):
@@ -310,14 +317,16 @@
     )(tokens, mod)
 
 
-def temporal_block(tokens, moved, mod, weights, positions):
+def temporal_block(frame, tokens, moved, mod, weights, positions):
     count, width = tokens.shape
     return pl.pallas_call(
         lambda *refs: temporal_kernel(positions, 4, *refs),
-        out_shape=jax.ShapeDtypeStruct((count, width), jnp.bfloat16),
-        in_specs=[pl.BlockSpec(memory_space=pltpu.VMEM)] * (3 + RESIDENT)
+        out_shape=(jax.ShapeDtypeStruct((positions, width), jnp.bfloat16),) * (count // positions),
+        in_specs=[pl.BlockSpec(memory_space=pltpu.SMEM)]
+        + [pl.BlockSpec(memory_space=pltpu.VMEM)] * (3 + RESIDENT)
         + [pl.BlockSpec(memory_space=pl.ANY)] * (HEADS - RESIDENT),
         scratch_shapes=[
+            pltpu.VMEM((count, width), jnp.float32),
             pltpu.VMEM((HEADS * PAD_DIM, count), jnp.float32),
             pltpu.VMEM(((HEADS - RESIDENT) * QKV_ROWS, width), jnp.bfloat16),
             pltpu.VMEM((HEADS * PAD_DIM, width), jnp.bfloat16),
@@ -326,11 +335,34 @@
         compiler_params=pltpu.CompilerParams(vmem_limit_bytes=LARGE_VMEM_LIMIT),
         cost_estimate=SMALL,
         name="temporal_block",
-    )(tokens, moved, mod, *weights)
+    )(frame, tokens, moved, mod, *weights)
+
+
+def join_kernel(offsets, frame_ref, *refs):
+    positions = refs[0].shape[0]
+    for offset, ref in zip(offsets, refs[:-1]):
+        refs[-1][pl.ds(frame_start(frame_ref, offset, positions), positions), :] = ref[...]
+
+
+def join_frames(frame, pieces, offsets):
+    positions, width = pieces[0].shape
+    return pl.pallas_call(
+        lambda *refs: join_kernel(offsets, *refs),
+        out_shape=jax.ShapeDtypeStruct((positions * len(pieces), width), jnp.bfloat16),
+        in_specs=[pl.BlockSpec(memory_space=pltpu.SMEM)]
+        + [pl.BlockSpec(memory_space=pltpu.VMEM)] * len(pieces),
+        compiler_params=pltpu.CompilerParams(vmem_limit_bytes=VMEM_LIMIT),
+        cost_estimate=SMALL,
+        name="join_frames",
+    )(frame, *pieces)
 
 
 def swap(array, offset, count):
     return lax.ppermute(array, "patch", [(rank, rank ^ offset) for rank in range(count)])
+
+
+def frame_swap(array, offset, count):
+    return lax.ppermute(array, "frame", [(rank, rank ^ offset) for rank in range(count)])
 
 
 def ring_step(array, frame_count, patch_count):
@@ -371,7 +403,8 @@
         steps = frame_count // 2
         patch = lax.axis_index("patch").astype(jnp.int32)
         place = ((patch ^ (patch >> 1)) & 1).reshape(1)
-        place, hidden_states = barrier((place, hidden_states))
+        frame = lax.axis_index("frame").astype(jnp.int32).reshape(1)
+        place, frame, hidden_states = barrier((place, frame, hidden_states))
         tokens = hidden_states.reshape(patches, width)
         w_qkv = w_spatial_qkv.T
 
@@ -447,8 +480,15 @@
         for array in rest:
             others += [array, over_cores(array)]
         weights += others
-        result = temporal_block(arrived, moved, mod_temporal, weights, patches // frame_count)
-        return exchange(result).reshape(1, patches, width)
+        positions = patches // frame_count
+        pieces = list(temporal_block(frame, arrived, moved, mod_temporal, weights, positions))
+        middle = frame_count // 2
+        far = list(range(middle, frame_count))
+        order = [0, *far[:2], 1, *far[2:], *range(2, middle)]
+        for offset in order[1:]:
+            pieces[offset] = frame_swap(pieces[offset], offset, frame_count)
+        result = join_frames(frame, [pieces[offset] for offset in order], order)
+        return result.reshape(1, patches, width)
 
     return shards
 

time: 99.2 us -> 96.1 us (0.969)
  blocking collectives: 21.3 us -> 0 us
  starting transfers between devices: 21.9 us -> 32.3 us
  waiting for transfers between devices: 24.1 us -> 31.7 us
    all_to_all x1 -> x0, blocking collectives: 21.3 us -> none  [exchange(): pieces = lax.all_to_all(pieces, 'frame', 0, 0, tiled=True)]
    ppermute x0 -> x7, starting transfers between devices: none -> 10.4 us  [frame_swap(): lax.ppermute(array, 'frame', [(rank, rank ^ offset) for rank in range(cou...]
    ppermute x0 -> x7, waiting for transfers between devices: none -> 7.65 us  [frame_swap(): lax.ppermute(array, 'frame', [(rank, rank ^ offset) for rank in range(cou...]
    unnamed x25 -> x24, local copies, waits for them, and re-layouts: 7.53 us -> 6.72 us
  transfers between devices with their start and end apart: 22 -> 29, of which waited for: 5 -> 8; matrix products, arithmetic and copies ran while one was open for 0% -> 0% of each run, Pallas kernels for 16% -> 17%
where the time goes in v3:
time: 96.1 us; the launch traced here: 95.7 us
  starting transfers between devices  32.3 us (34%)
  waiting for transfers between devices  31.7 us (33%)
  Pallas kernels  24.6 us (26%)
  local copies, waits for them, and re-layouts  6.72 us (7%)
    ppermute x7, starting transfers between devices, frame_swap(): lax.ppermute(array, 'frame', [(rank, rank ^ offset) for rank in range(cou...  10.4 us
    ppermute x6, starting transfers between devices, ring_step(): return lax.ppermute(array, ('frame', 'patch'), pairs)  9.92 us
    ppermute x15, waiting for transfers between devices, swap(): lax.ppermute(array, 'patch', [(rank, rank ^ offset) for rank in range(cou...  9.51 us
    pallas_call x4, Pallas kernels, spatial_attention(): pl.pallas_call(lambda *refs: attention_kernel(parts, *refs), out_shape=ja...  9.07 us
    pallas_call x1, Pallas kernels, temporal_block(): pl.pallas_call(lambda *refs: temporal_kernel(positions, 4, *refs), out_sh...  7.7 us
    ppermute x7, waiting for transfers between devices, frame_swap(): lax.ppermute(array, 'frame', [(rank, rank ^ offset) for rank in range(cou...  7.65 us
    ppermute x15, starting transfers between devices, swap(): lax.ppermute(array, 'patch', [(rank, rank ^ offset) for rank in range(cou...  7.55 us
    all_to_all x1, waiting for transfers between devices, exchange(): pieces = lax.all_to_all(pieces, 'frame', 0, 0, tiled=True)  7.48 us
  transfers between devices with their start and end apart: 29, of which 8 were waited for; matrix products, arithmetic and copies ran while one was open for 0% of the time, Pallas kernels for 17%

profile of v3, /device:TPU:0, one launch (start us, length us, event | category | flops | bytes accessed | tf_op | source)
XLA Modules:
  0.0 95.7 jit_solution(6352307509843132398)
XLA Ops:
  0.0 0.5 collective-permute-start
  0.5 2.5 %collective-permute-start.1 = (bf16[256,1152]{1,0:T(8,128)(2,1)}, bf16[256,1152]{1,0:T(8,128)(2,1)S(1)}, u32[]{:S(2)}, u32[]{:S(2)}) collective-permute-start(bf16[256,1152]{1,0:T(8,128)(2,1)} %bitcast.15), channel_id=1, source_target_pairs={{0,2},{1,3},{2,0},{3,1},{4,6},{5,7},{6,4},{7,5},{8,10},{9,11},{10,... | collective-permute-start | bytes 1769480 | tf_op jit(solution)/shard_map/ppermute | solution.py:361
  2.9 1.2 %copy-done.5 = bf16[1152,432]{0,1:T(8,128)(2,1)S(1)} copy-done((bf16[1152,432]{0,1:T(8,128)(2,1)S(1)}, bf16[1152,432]{0,1:T(8,128)(2,1)}, u32[]{:S(2)}) %copy-start.5) | copy-done | bytes 995352
  4.2 1.0 %copy-done.7 = bf16[144,1152]{1,0:T(8,128)(2,1)S(1)} copy-done((bf16[144,1152]{1,0:T(8,128)(2,1)S(1)}, bf16[144,1152]{1,0:T(8,128)(2,1)}, u32[]{:S(2)}) %copy-start.7) | copy-done | bytes 331800
  5.1 0.1 pack.1
  5.2 1.6 %collective-permute-start.2 = (bf16[288,1152]{1,0:T(8,128)(2,1)S(1)}, bf16[288,1152]{1,0:T(8,128)(2,1)S(1)}, u32[]{:S(2)}, u32[]{:S(2)}) collective-permute-start(bf16[288,1152]{1,0:T(8,128)(2,1)S(1)} %get-tuple-element.105.refs_4_), channel_id=1, source_target_pairs={{0,8},{1,5},{2,10},{3,7},{8,16},{9,1},{10,18},{11,3},{16,24},{17,9... | collective-permute-start | bytes 1990664 | tf_op jit(solution)/shard_map/ppermute | solution.py:376
  6.9 1.6 %collective-permute-start.5 = (bf16[288,1152]{1,0:T(8,128)(2,1)S(1)}, bf16[288,1152]{1,0:T(8,128)(2,1)S(1)}, u32[]{:S(2)}, u32[]{:S(2)}) collective-permute-start(bf16[288,1152]{1,0:T(8,128)(2,1)S(1)} %get-tuple-element.119.refs_5_), channel_id=1, source_target_pairs={{0,8},{1,5},{2,10},{3,7},{8,16},{9,1},{10,18},{11,3},{16,24},{17,9... | collective-permute-start | bytes 1990664 | tf_op jit(solution)/shard_map/ppermute | solution.py:376
  8.4 1.6 %copy-done = bf16[1152,864]{0,1:T(8,128)(2,1)S(1)} copy-done((bf16[1152,864]{0,1:T(8,128)(2,1)S(1)}, bf16[1152,864]{0,1:T(8,128)(2,1)}, u32[]{:S(2)}) %copy-start) | copy-done | bytes 1990680
  10.0 1.1 %copy-done.3 = bf16[1,256,1152]{2,1,0:T(8,128)(2,1)S(1)} copy-done((bf16[1,256,1152]{2,1,0:T(8,128)(2,1)S(1)}, bf16[1,256,1152]{2,1,0:T(8,128)(2,1)}, u32[]{:S(2)}) %copy-start.3) | copy-done | bytes 589848
  11.1 0.7 copy-done.8
  11.8 1.2 %spatial_qkv.4 = (bf16[8,80,256]{2,1,0:T(8,128)(2,1)S(1)}, bf16[4,256,80]{2,1,0:T(8,128)(2,1)S(1)}) custom-call(bf16[256,1152]{1,0:T(8,128)(2,1)S(1)} %bitcast.16, f32[3,1152]{1,0:T(4,128)S(1)} %copy-done.8, bf16[864,1152]{1,0:T(8,128)(2,1)S(1)} %bitcast.8), custom_call_target="tpu_custom_call" | custom-call | flops 1 | bytes 1 | tf_op jit(solution)/shard_map/spatial_qkv/pallas_call | solution.py:70
  13.0 0.4 copy-done.1
  13.3 1.2 %spatial_qkv.5 = (bf16[8,80,256]{2,1,0:T(8,128)(2,1)S(1)}, bf16[4,256,80]{2,1,0:T(8,128)(2,1)S(1)}) custom-call(bf16[256,1152]{1,0:T(8,128)(2,1)S(1)} %collective-permute-done.tokens_ref, f32[3,1152]{1,0:T(4,128)S(1)} %copy-done.8, bf16[864,1152]{1,0:T(8,128)(2,1)S(1)} %bitcast.9), custom_call_target="tpu_custom_call" | custom-call | flops 1 | bytes 1 | tf_op jit(solution)/shard_map/spatial_qkv/pallas_call | solution.py:70
  14.5 2.6 %collective-permute-done.1.tokens_ref = bf16[256,1152]{1,0:T(8,128)(2,1)S(1)} collective-permute-done((bf16[256,1152]{1,0:T(8,128)(2,1)}, bf16[256,1152]{1,0:T(8,128)(2,1)S(1)}, u32[]{:S(2)}, u32[]{:S(2)}) %collective-permute-start.1) | collective-permute-done | bytes 589856 | tf_op jit(solution)/shard_map/ppermute | solution.py:361
  17.2 0.0 collective-permute-start.3
  17.2 1.2 %spatial_qkv.6 = (bf16[8,80,256]{2,1,0:T(8,128)(2,1)S(1)}, bf16[4,256,80]{2,1,0:T(8,128)(2,1)S(1)}) custom-call(bf16[256,1152]{1,0:T(8,128)(2,1)S(1)} %collective-permute-done.1.tokens_ref, f32[3,1152]{1,0:T(4,128)S(1)} %copy-done.9, bf16[864,1152]{1,0:T(8,128)(2,1)S(1)} %bitcast.10), custom_call_target="tpu_custom_call" | custom-call | flops 1610612736 | bytes 1 | tf_op jit(solution)/shard_map/spatial_qkv/pallas_call | solution.py:70
  18.3 0.0 collective-permute-done.2.refs_6_
  18.3 1.9 %collective-permute-start.7 = (bf16[288,1152]{1,0:T(8,128)(2,1)S(1)}, bf16[288,1152]{1,0:T(8,128)(2,1)S(1)}, u32[]{:S(2)}, u32[]{:S(2)}) collective-permute-start(bf16[288,1152]{1,0:T(8,128)(2,1)S(1)} %collective-permute-done.2.refs_6_), channel_id=1, source_target_pairs={{0,8},{1,5},{2,10},{3,7},{8,16},{9,1},{10,18},{11,3},{16,24},{17,9... | collective-permute-start | bytes 1990664 | tf_op jit(solution)/shard_map/ppermute | solution.py:376
  20.2 1.2 %spatial_qkv.7 = (bf16[8,80,256]{2,1,0:T(8,128)(2,1)S(1)}, bf16[4,256,80]{2,1,0:T(8,128)(2,1)S(1)}) custom-call(bf16[256,1152]{1,0:T(8,128)(2,1)S(1)} %collective-permute-done.3.tokens_ref, f32[3,1152]{1,0:T(4,128)S(1)} %copy-done.9, bf16[864,1152]{1,0:T(8,128)(2,1)S(1)} %bitcast.11), custom_call_target="tpu_custom_call" | custom-call | flops 1 | bytes 1 | tf_op jit(solution)/shard_map/spatial_qkv/pallas_call | solution.py:70
  21.4 2.3 %spatial_attention.4 = bf16[256,288]{1,0:T(8,128)(2,1)S(1)} custom-call(bf16[8,80,256]{2,1,0:T(8,128)(2,1)S(1)} %get-tuple-element.143.refs_0_.refs_4_, bf16[8,80,256]{2,1,0:T(8,128)(2,1)S(1)} %get-tuple-element.140.refs_1_.refs_0_, bf16[8,80,256]{2,1,0:T(8,128)(2,1)S(1)} %get-tuple-element.141.refs_2_.refs_0_, ...), custom_call_target="tpu_custom_call" | custom-call | flops 1 | bytes 1 | tf_op jit(solution)/shard_map/spatial_attention/pallas_call | solution.py:105
  23.7 0.0 copy-start.2
  23.7 0.0 collective-permute-done.5.refs_7_
  23.7 0.2 collective-permute-start.6
  23.9 2.3 %spatial_attention.5.heads_ref = bf16[256,288]{1,0:T(8,128)(2,1)S(1)} custom-call(bf16[8,80,256]{2,1,0:T(8,128)(2,1)S(1)} %get-tuple-element.142.refs_3_.refs_0_, bf16[8,80,256]{2,1,0:T(8,128)(2,1)S(1)} %get-tuple-element.140.refs_1_.refs_0_, bf16[8,80,256]{2,1,0:T(8,128)(2,1)S(1)} %get-tuple-element.141.refs_2_.refs_0_, ...), custom_call_target="tpu_custom_call" | custom-call | flops 1 | bytes 1 | tf_op jit(solution)/shard_map/spatial_attention/pallas_call | solution.py:105
  26.2 0.0 collective-permute-done.6.other_ref
  26.2 0.8 chip_partial.1
  27.1 1.6 %collective-permute-start.9 = (bf16[256,1152]{1,0:T(8,128)(2,1)S(1)}, bf16[256,1152]{1,0:T(8,128)(2,1)S(1)}, u32[]{:S(2)}, u32[]{:S(2)}) collective-permute-start(bf16[256,1152]{1,0:T(8,128)(2,1)S(1)} %chip_partial.1), channel_id=1, source_target_pairs={{0,2},{1,3},{2,0},{3,1},{4,6},{5,7},{6,4},{7,5},{8,10},{9,11},{10,... | collective-permute-start | bytes 1769480 | tf_op jit(solution)/shard_map/ppermute | solution.py:361
  28.6 2.3 %spatial_attention.6 = bf16[256,288]{1,0:T(8,128)(2,1)S(1)} custom-call(bf16[8,80,256]{2,1,0:T(8,128)(2,1)S(1)} %get-tuple-element.141.refs_2_.refs_0_, bf16[8,80,256]{2,1,0:T(8,128)(2,1)S(1)} %get-tuple-element.140.refs_1_.refs_0_, bf16[8,80,256]{2,1,0:T(8,128)(2,1)S(1)} %get-tuple-element.141.refs_2_.refs_0_, ...), custom_call_target="tpu_custom_call" | custom-call | flops 1 | bytes 1 | tf_op jit(solution)/shard_map/spatial_attention/pallas_call | solution.py:105
  30.9 0.0 copy-start.4
  30.9 1.6 %collective-permute-start.10 = (bf16[288,1152]{1,0:T(8,128)(2,1)S(1)}, bf16[288,1152]{1,0:T(8,128)(2,1)}, u32[]{:S(2)}, u32[]{:S(2)}) collective-permute-start(bf16[288,1152]{1,0:T(8,128)(2,1)S(1)} %collective-permute-done.7.refs_10_), channel_id=1, source_target_pairs={{0,8},{1,5},{2,10},{3,7},{8,16},{9,1},{10,18},{11,3},{16,24},{17,9... | collective-permute-start | bytes 1990664 | tf_op jit(solution)/shard_map/ppermute | solution.py:376
  32.6 2.3 %spatial_attention.7.heads_ref = bf16[256,288]{1,0:T(8,128)(2,1)S(1)} custom-call(bf16[8,80,256]{2,1,0:T(8,128)(2,1)S(1)} %get-tuple-element.140.refs_1_.refs_0_, bf16[8,80,256]{2,1,0:T(8,128)(2,1)S(1)} %get-tuple-element.140.refs_1_.refs_0_, bf16[8,80,256]{2,1,0:T(8,128)(2,1)S(1)} %get-tuple-element.141.refs_2_.refs_0_, ...), custom_call_target="tpu_custom_call" | custom-call | flops 1 | bytes 1 | tf_op jit(solution)/shard_map/spatial_attention/pallas_call | solution.py:105
  34.8 0.1 collective-permute-start.8
  34.9 1.6 %collective-permute-start.14 = (bf16[288,1152]{1,0:T(8,128)(2,1)S(1)}, bf16[288,1152]{1,0:T(8,128)(2,1)}, u32[]{:S(2)}, u32[]{:S(2)}) collective-permute-start(bf16[288,1152]{1,0:T(8,128)(2,1)S(1)} %collective-permute-done.5.refs_7_), channel_id=1, source_target_pairs={{0,8},{1,5},{2,10},{3,7},{8,16},{9,1},{10,18},{11,3},{16,24},{17,9... | collective-permute-start | bytes 1990664 | tf_op jit(solution)/shard_map/ppermute | solution.py:376
  36.6 0.0 collective-permute-done.8.other_ref
  36.6 0.8 spatial_base.1.base_ref
  37.4 0.0 copy-start.10
  37.4 0.1 collective-permute-start.11
  37.5 0.5 collective-permute-start.12
  38.0 4.7 %collective-permute-done.9.refs_0_ = bf16[256,1152]{1,0:T(8,128)(2,1)S(1)} collective-permute-done((bf16[256,1152]{1,0:T(8,128)(2,1)S(1)}, bf16[256,1152]{1,0:T(8,128)(2,1)S(1)}, u32[]{:S(2)}, u32[]{:S(2)}) %collective-permute-start.9) | collective-permute-done | bytes 589856 | tf_op jit(solution)/shard_map/ppermute | solution.py:361
  42.7 0.2 spatial_add.1
  42.9 0.0 copy-start.6
  42.9 0.8 copy-done.6
  43.7 0.0 collective-permute-done.10.refs_14_
  43.7 1.6 %collective-permute-start.19 = (bf16[288,1152]{1,0:T(8,128)(2,1)}, bf16[288,1152]{1,0:T(8,128)(2,1)}, u32[]{:S(2)}, u32[]{:S(2)}) collective-permute-start(bf16[288,1152]{1,0:T(8,128)(2,1)} %collective-permute-done.10.refs_14_), channel_id=1, source_target_pairs={{0,8},{1,5},{2,10},{3,7},{8,16},{9,1},{10,18},{11,3},{16,24},{17,9... | collective-permute-start | bytes 1990664 | tf_op jit(solution)/shard_map/ppermute | solution.py:376
  45.3 1.5 %collective-permute-start.17 = (bf16[288,1152]{1,0:T(8,128)(2,1)}, bf16[288,1152]{1,0:T(8,128)(2,1)}, u32[]{:S(2)}, u32[]{:S(2)}) collective-permute-start(bf16[288,1152]{1,0:T(8,128)(2,1)} %collective-permute-done.10.refs_14_), channel_id=1, source_target_pairs={{0,2},{1,3},{2,0},{3,1},{4,6},{5,7},{6,4},{7,5},{8,10},{9,11},{10,... | collective-permute-start | bytes 1990664 | tf_op jit(solution)/shard_map/ppermute | solution.py:361
  46.8 4.4 %all-to-all-start = ((bf16[8,32,1152]{2,1,0:T(8,128)(2,1)}), bf16[8,32,1152]{2,1,0:T(8,128)(2,1)S(1)}, u32[]{:S(2)}, u32[]{:S(2)}) async-start(bf16[8,32,1152]{2,1,0:T(8,128)(2,1)} %bitcast.19), calls=%async_computation | async-start | bytes 1179648 | tf_op jit(solution)/shard_map/all_to_all | solution.py:388
  51.2 0.1 collective-permute-start.13
  51.3 0.0 collective-permute-done.11.refs_8_
  51.3 0.5 collective-permute-start.16
  51.8 0.0 collective-permute-done.12.refs_9_
  51.8 0.1 collective-permute-start.15
  51.9 7.1 %collective-permute-done.19.refs_18_ = bf16[288,1152]{1,0:T(8,128)(2,1)} collective-permute-done((bf16[288,1152]{1,0:T(8,128)(2,1)}, bf16[288,1152]{1,0:T(8,128)(2,1)}, u32[]{:S(2)}, u32[]{:S(2)}) %collective-permute-start.19) | collective-permute-done | bytes 663584 | tf_op jit(solution)/shard_map/ppermute | solution.py:376
  58.9 2.1 %collective-permute-done.17.refs_16_ = bf16[288,1152]{1,0:T(8,128)(2,1)} collective-permute-done((bf16[288,1152]{1,0:T(8,128)(2,1)}, bf16[288,1152]{1,0:T(8,128)(2,1)}, u32[]{:S(2)}, u32[]{:S(2)}) %collective-permute-start.17) | collective-permute-done | bytes 663584 | tf_op jit(solution)/shard_map/ppermute | solution.py:361
  61.1 7.5 %all-to-all-done = bf16[8,32,1152]{2,1,0:T(8,128)(2,1)S(1)} async-done(((bf16[8,32,1152]{2,1,0:T(8,128)(2,1)}), bf16[8,32,1152]{2,1,0:T(8,128)(2,1)S(1)}, u32[]{:S(2)}, u32[]{:S(2)}) %all-to-all-start) | async-done | bytes 589856 | tf_op jit(solution)/shard_map/all_to_all | solution.py:388
  68.6 0.4 temporal_norm.1.refs_2_
  69.0 7.7 %temporal_block.1 = (bf16[32,1152]{1,0:T(8,128)(2,1)S(1)}, bf16[32,1152]{1,0:T(8,128)(2,1)S(1)}, bf16[32,1152]{1,0:T(8,128)(2,1)S(1)}, bf16[32,1152]{1,0:T(8,128...) custom-call(s32[1]{0:T(128)} %bitcast.1.refs_0_, ...), custom_call_target="tpu_custom_call" | custom-call | flops 1 | bytes 1 | tf_op jit(solution)/shard_map/temporal_block/pallas_call | solution.py:322
  76.7 1.0 %collective-permute-start.21 = (bf16[32,1152]{1,0:T(8,128)(2,1)S(1)}, bf16[32,1152]{1,0:T(8,128)(2,1)S(1)}, u32[]{:S(2)}, u32[]{:S(2)}) collective-permute-start(bf16[32,1152]{1,0:T(8,128)(2,1)S(1)} %get-tuple-element.162), channel_id=1, source_target_pairs={{0,16},{4,20},{8,24},{12,28},{16,0},{20,4},{24,8},{28,12},{1,17},{... | collective-permute-start | bytes 221192 | tf_op jit(solution)/shard_map/ppermute | solution.py:365
  77.8 4.1 %collective-permute-start.22 = (bf16[32,1152]{1,0:T(8,128)(2,1)S(1)}, bf16[32,1152]{1,0:T(8,128)(2,1)S(1)}, u32[]{:S(2)}, u32[]{:S(2)}) collective-permute-start(bf16[32,1152]{1,0:T(8,128)(2,1)S(1)} %get-tuple-element.163), channel_id=1, source_target_pairs={{0,20},{4,16},{8,28},{12,24},{16,4},{20,0},{24,12},{28,8},{1,21},{... | collective-permute-start | bytes 221192 | tf_op jit(solution)/shard_map/ppermute | solution.py:365
  81.9 2.8 %collective-permute-start.24 = (bf16[32,1152]{1,0:T(8,128)(2,1)S(1)}, bf16[32,1152]{1,0:T(8,128)(2,1)S(1)}, u32[]{:S(2)}, u32[]{:S(2)}) collective-permute-start(bf16[32,1152]{1,0:T(8,128)(2,1)S(1)} %get-tuple-element.165), channel_id=1, source_target_pairs={{0,24},{4,28},{8,16},{12,20},{16,8},{20,12},{24,0},{28,4},{1,25},{... | collective-permute-start | bytes 221192 | tf_op jit(solution)/shard_map/ppermute | solution.py:365
  84.7 2.5 %collective-permute-start.25 = (bf16[32,1152]{1,0:T(8,128)(2,1)S(1)}, bf16[32,1152]{1,0:T(8,128)(2,1)S(1)}, u32[]{:S(2)}, u32[]{:S(2)}) collective-permute-start(bf16[32,1152]{1,0:T(8,128)(2,1)S(1)} %get-tuple-element.166), channel_id=1, source_target_pairs={{0,28},{4,24},{8,20},{12,16},{16,12},{20,8},{24,4},{28,0},{1,29},{... | collective-permute-start | bytes 221192 | tf_op jit(solution)/shard_map/ppermute | solution.py:365
  87.2 2.4 %collective-permute-done.22.refs_3_ = bf16[32,1152]{1,0:T(8,128)(2,1)S(1)} collective-permute-done((bf16[32,1152]{1,0:T(8,128)(2,1)S(1)}, bf16[32,1152]{1,0:T(8,128)(2,1)S(1)}, u32[]{:S(2)}, u32[]{:S(2)}) %collective-permute-start.22) | collective-permute-done | bytes 73760 | tf_op jit(solution)/shard_map/ppermute | solution.py:365
  89.6 2.3 %collective-permute-done.25.refs_6_ = bf16[32,1152]{1,0:T(8,128)(2,1)S(1)} collective-permute-done((bf16[32,1152]{1,0:T(8,128)(2,1)S(1)}, bf16[32,1152]{1,0:T(8,128)(2,1)S(1)}, u32[]{:S(2)}, u32[]{:S(2)}) %collective-permute-start.25) | collective-permute-done | bytes 73760 | tf_op jit(solution)/shard_map/ppermute | solution.py:365
  91.9 2.9 %collective-permute-done.27.refs_8_ = bf16[32,1152]{1,0:T(8,128)(2,1)S(1)} collective-permute-done((bf16[32,1152]{1,0:T(8,128)(2,1)S(1)}, bf16[32,1152]{1,0:T(8,128)(2,1)S(1)}, u32[]{:S(2)}, u32[]{:S(2)}) %collective-permute-start.27) | collective-permute-done | bytes 73760 | tf_op jit(solution)/shard_map/ppermute | solution.py:365
  94.8 0.9 join_frames.1
  (33 shorter events, 0.1 us)
Async XLA Ops:
  0.0 13.0 %collective-permute-start = (bf16[256,1152]{1,0:T(8,128)(2,1)}, bf16[256,1152]{1,0:T(8,128)(2,1)S(1)}, u32[]{:S(2)}, u32[]{:S(2)}) collective-permute-start(bf16[256,1152]{1,0:T(8,128)(2,1)} %bitcast.14), channel_id=1, source_target_pairs={{0,1},{1,0},{2,3},{3,2},{4,5},{5,4},{6,7},{7,6},{8,9},{9,8},{10,11... | collective-permute-start | bytes 1769480 | tf_op jit(solution)/shard_map/ppermute | solution.py:361
  0.5 16.7 %collective-permute-start.1 = (bf16[256,1152]{1,0:T(8,128)(2,1)}, bf16[256,1152]{1,0:T(8,128)(2,1)S(1)}, u32[]{:S(2)}, u32[]{:S(2)}) collective-permute-start(bf16[256,1152]{1,0:T(8,128)(2,1)} %bitcast.15), channel_id=1, source_target_pairs={{0,2},{1,3},{2,0},{3,1},{4,6},{5,7},{6,4},{7,5},{8,10},{9,11},{10,... | collective-permute-start | bytes 1769480 | tf_op jit(solution)/shard_map/ppermute | solution.py:361
  2.9 1.2 %copy-start.5 = (bf16[1152,432]{0,1:T(8,128)(2,1)S(1)}, bf16[1152,432]{0,1:T(8,128)(2,1)}, u32[]{:S(2)}) copy-start(bf16[1152,432]{0,1:T(8,128)(2,1)} %param.12) | copy-start | bytes 2985988
  4.1 1.0 %copy-start.7 = (bf16[144,1152]{1,0:T(8,128)(2,1)S(1)}, bf16[144,1152]{1,0:T(8,128)(2,1)}, u32[]{:S(2)}) copy-start(bf16[144,1152]{1,0:T(8,128)(2,1)} %out_ref.1) | copy-start | bytes 995332
  5.2 13.1 %collective-permute-start.2 = (bf16[288,1152]{1,0:T(8,128)(2,1)S(1)}, bf16[288,1152]{1,0:T(8,128)(2,1)S(1)}, u32[]{:S(2)}, u32[]{:S(2)}) collective-permute-start(bf16[288,1152]{1,0:T(8,128)(2,1)S(1)} %get-tuple-element.105.refs_4_), channel_id=1, source_target_pairs={{0,8},{1,5},{2,10},{3,7},{8,16},{9,1},{10,18},{11,3},{16,24},{17,9... | collective-permute-start | bytes 1990664 | tf_op jit(solution)/shard_map/ppermute | solution.py:376
  6.9 14.5 %collective-permute-start.4 = (bf16[288,1152]{1,0:T(8,128)(2,1)}, bf16[288,1152]{1,0:T(8,128)(2,1)S(1)}, u32[]{:S(2)}, u32[]{:S(2)}) collective-permute-start(bf16[288,1152]{1,0:T(8,128)(2,1)} %weight_ref.3), channel_id=1, source_target_pairs={{0,1},{1,0},{2,3},{3,2},{4,5},{5,4},{6,7},{7,6},{8,9},{9,8},{10,11... | collective-permute-start | bytes 1990664 | tf_op jit(solution)/shard_map/ppermute | solution.py:361
  6.9 16.8 %collective-permute-start.5 = (bf16[288,1152]{1,0:T(8,128)(2,1)S(1)}, bf16[288,1152]{1,0:T(8,128)(2,1)S(1)}, u32[]{:S(2)}, u32[]{:S(2)}) collective-permute-start(bf16[288,1152]{1,0:T(8,128)(2,1)S(1)} %get-tuple-element.119.refs_5_), channel_id=1, source_target_pairs={{0,8},{1,5},{2,10},{3,7},{8,16},{9,1},{10,18},{11,3},{16,24},{17,9... | collective-permute-start | bytes 1990664 | tf_op jit(solution)/shard_map/ppermute | solution.py:376
  8.4 1.6 %copy-start = (bf16[1152,864]{0,1:T(8,128)(2,1)S(1)}, bf16[1152,864]{0,1:T(8,128)(2,1)}, u32[]{:S(2)}) copy-start(bf16[1152,864]{0,1:T(8,128)(2,1)} %param.9) | copy-start | bytes 5971972
  10.0 1.1 %copy-start.3 = (bf16[1,256,1152]{2,1,0:T(8,128)(2,1)S(1)}, bf16[1,256,1152]{2,1,0:T(8,128)(2,1)}, u32[]{:S(2)}) copy-start(bf16[1,256,1152]{2,1,0:T(8,128)(2,1)} %param.7) | copy-start | bytes 1769476
  11.1 0.7 copy-start.8
  11.8 1.6 %copy-start.1 = (bf16[1152,864]{0,1:T(8,128)(2,1)S(1)}, bf16[1152,864]{0,1:T(8,128)(2,1)}, u32[]{:S(2)}) copy-start(bf16[1152,864]{0,1:T(8,128)(2,1)} %param.9) | copy-start | bytes 5971972
  11.8 5.4 %copy-start.9 = (f32[3,1152]{1,0:T(4,128)S(1)}, f32[3,1152]{1,0:T(4,128)}, u32[]{:S(2)}) copy-start(f32[3,1152]{1,0:T(4,128)} %mod_ref.11) | copy-start | bytes 41476
  17.2 3.1 %collective-permute-start.3 = (bf16[256,1152]{1,0:T(8,128)(2,1)S(1)}, bf16[256,1152]{1,0:T(8,128)(2,1)S(1)}, u32[]{:S(2)}, u32[]{:S(2)}) collective-permute-start(bf16[256,1152]{1,0:T(8,128)(2,1)S(1)} %collective-permute-done.1.tokens_ref), channel_id=1, source_target_pairs={{0,1},{1,0},{2,3},{3,2},{4,5},{5,4},{6,7},{7,6},{8,9},{9,8},{10,11... | collective-permute-start | bytes 1769480 | tf_op jit(solution)/shard_map/ppermute | solution.py:361
  18.3 12.6 %collective-permute-start.7 = (bf16[288,1152]{1,0:T(8,128)(2,1)S(1)}, bf16[288,1152]{1,0:T(8,128)(2,1)S(1)}, u32[]{:S(2)}, u32[]{:S(2)}) collective-permute-start(bf16[288,1152]{1,0:T(8,128)(2,1)S(1)} %collective-permute-done.2.refs_6_), channel_id=1, source_target_pairs={{0,8},{1,5},{2,10},{3,7},{8,16},{9,1},{10,18},{11,3},{16,24},{17,9... | collective-permute-start | bytes 1990664 | tf_op jit(solution)/shard_map/ppermute | solution.py:376
  23.7 2.5 %copy-start.2 = (bf16[288,1152]{1,0:T(8,128)(2,1)S(1)}, bf16[288,1152]{1,0:T(8,128)(2,1)}, u32[]{:S(2)}) copy-start(bf16[288,1152]{1,0:T(8,128)(2,1)} %weight_ref.3) | copy-start | bytes 1990660
  23.7 2.5 %collective-permute-start.6 = (bf16[256,288]{1,0:T(8,128)(2,1)S(1)}, bf16[256,288]{1,0:T(8,128)(2,1)S(1)}, u32[]{:S(2)}, u32[]{:S(2)}) collective-permute-start(bf16[256,288]{1,0:T(8,128)(2,1)S(1)} %spatial_attention.4), channel_id=1, source_target_pairs={{0,1},{1,0},{2,3},{3,2},{4,5},{5,4},{6,7},{7,6},{8,9},{9,8},{10,11... | collective-permute-start | bytes 442376 | tf_op jit(solution)/shard_map/ppermute | solution.py:361
  27.1 15.6 %collective-permute-start.9 = (bf16[256,1152]{1,0:T(8,128)(2,1)S(1)}, bf16[256,1152]{1,0:T(8,128)(2,1)S(1)}, u32[]{:S(2)}, u32[]{:S(2)}) collective-permute-start(bf16[256,1152]{1,0:T(8,128)(2,1)S(1)} %chip_partial.1), channel_id=1, source_target_pairs={{0,2},{1,3},{2,0},{3,1},{4,6},{5,7},{6,4},{7,5},{8,10},{9,11},{10,... | collective-permute-start | bytes 1769480 | tf_op jit(solution)/shard_map/ppermute | solution.py:361
  30.9 5.6 %copy-start.4 = (bf16[1,256,1152]{2,1,0:T(8,128)(2,1)S(1)}, bf16[1,256,1152]{2,1,0:T(8,128)(2,1)}, u32[]{:S(2)}) copy-start(bf16[1,256,1152]{2,1,0:T(8,128)(2,1)} %param.7) | copy-start | bytes 1769476
  30.9 6.5 %copy-start.11 = (bf16[288,1152]{1,0:T(8,128)(2,1)}, bf16[288,1152]{1,0:T(8,128)(2,1)S(1)}, u32[]{:S(2)}) copy-start(bf16[288,1152]{1,0:T(8,128)(2,1)S(1)} %collective-permute-done.7.refs_10_) | copy-start | bytes 1990660
  30.9 12.8 %collective-permute-start.10 = (bf16[288,1152]{1,0:T(8,128)(2,1)S(1)}, bf16[288,1152]{1,0:T(8,128)(2,1)}, u32[]{:S(2)}, u32[]{:S(2)}) collective-permute-start(bf16[288,1152]{1,0:T(8,128)(2,1)S(1)} %collective-permute-done.7.refs_10_), channel_id=1, source_target_pairs={{0,8},{1,5},{2,10},{3,7},{8,16},{9,1},{10,18},{11,3},{16,24},{17,9... | collective-permute-start | bytes 1990664 | tf_op jit(solution)/shard_map/ppermute | solution.py:376
  34.8 1.7 %collective-permute-start.8 = (bf16[256,288]{1,0:T(8,128)(2,1)S(1)}, bf16[256,288]{1,0:T(8,128)(2,1)S(1)}, u32[]{:S(2)}, u32[]{:S(2)}) collective-permute-start(bf16[256,288]{1,0:T(8,128)(2,1)S(1)} %spatial_attention.6), channel_id=1, source_target_pairs={{0,1},{1,0},{2,3},{3,2},{4,5},{5,4},{6,7},{7,6},{8,9},{9,8},{10,11... | collective-permute-start | bytes 442376 | tf_op jit(solution)/shard_map/ppermute | solution.py:361
  34.9 16.3 %collective-permute-start.14 = (bf16[288,1152]{1,0:T(8,128)(2,1)S(1)}, bf16[288,1152]{1,0:T(8,128)(2,1)}, u32[]{:S(2)}, u32[]{:S(2)}) collective-permute-start(bf16[288,1152]{1,0:T(8,128)(2,1)S(1)} %collective-permute-done.5.refs_7_), channel_id=1, source_target_pairs={{0,8},{1,5},{2,10},{3,7},{8,16},{9,1},{10,18},{11,3},{16,24},{17,9... | collective-permute-start | bytes 1990664 | tf_op jit(solution)/shard_map/ppermute | solution.py:376
  37.4 31.1 %copy-start.10 = (f32[3,1152]{1,0:T(4,128)S(1)}, f32[3,1152]{1,0:T(4,128)}, u32[]{:S(2)}) copy-start(f32[3,1152]{1,0:T(4,128)} %refs_3_.1) | copy-start | bytes 41476
  37.4 13.9 %collective-permute-start.11 = (bf16[288,1152]{1,0:T(8,128)(2,1)S(1)}, bf16[288,1152]{1,0:T(8,128)(2,1)}, u32[]{:S(2)}, u32[]{:S(2)}) collective-permute-start(bf16[288,1152]{1,0:T(8,128)(2,1)S(1)} %collective-permute-done.2.refs_6_), channel_id=1, source_target_pairs={{0,1},{1,0},{2,3},{3,2},{4,5},{5,4},{6,7},{7,6},{8,9},{9,8},{10,11... | collective-permute-start | bytes 1990664 | tf_op jit(solution)/shard_map/ppermute | solution.py:361
  37.5 14.3 %collective-permute-start.12 = (bf16[288,1152]{1,0:T(8,128)(2,1)S(1)}, bf16[288,1152]{1,0:T(8,128)(2,1)}, u32[]{:S(2)}, u32[]{:S(2)}) collective-permute-start(bf16[288,1152]{1,0:T(8,128)(2,1)S(1)} %collective-permute-done.5.refs_7_), channel_id=1, source_target_pairs={{0,1},{1,0},{2,3},{3,2},{4,5},{5,4},{6,7},{7,6},{8,9},{9,8},{10,11... | collective-permute-start | bytes 1990664 | tf_op jit(solution)/shard_map/ppermute | solution.py:361
  42.9 0.8 copy-start.6
  43.7 15.2 %collective-permute-start.19 = (bf16[288,1152]{1,0:T(8,128)(2,1)}, bf16[288,1152]{1,0:T(8,128)(2,1)}, u32[]{:S(2)}, u32[]{:S(2)}) collective-permute-start(bf16[288,1152]{1,0:T(8,128)(2,1)} %collective-permute-done.10.refs_14_), channel_id=1, source_target_pairs={{0,8},{1,5},{2,10},{3,7},{8,16},{9,1},{10,18},{11,3},{16,24},{17,9... | collective-permute-start | bytes 1990664 | tf_op jit(solution)/shard_map/ppermute | solution.py:376
  45.3 15.8 %collective-permute-start.17 = (bf16[288,1152]{1,0:T(8,128)(2,1)}, bf16[288,1152]{1,0:T(8,128)(2,1)}, u32[]{:S(2)}, u32[]{:S(2)}) collective-permute-start(bf16[288,1152]{1,0:T(8,128)(2,1)} %collective-permute-done.10.refs_14_), channel_id=1, source_target_pairs={{0,2},{1,3},{2,0},{3,1},{4,6},{5,7},{6,4},{7,5},{8,10},{9,11},{10,... | collective-permute-start | bytes 1990664 | tf_op jit(solution)/shard_map/ppermute | solution.py:361
  46.8 21.8 %all-to-all-start = ((bf16[8,32,1152]{2,1,0:T(8,128)(2,1)}), bf16[8,32,1152]{2,1,0:T(8,128)(2,1)S(1)}, u32[]{:S(2)}, u32[]{:S(2)}) async-start(bf16[8,32,1152]{2,1,0:T(8,128)(2,1)} %bitcast.19), calls=%async_computation | async-start | bytes 1179648 | tf_op jit(solution)/shard_map/all_to_all | solution.py:388
  51.2 17.8 %collective-permute-start.13 = (bf16[288,1152]{1,0:T(8,128)(2,1)}, bf16[288,1152]{1,0:T(8,128)(2,1)}, u32[]{:S(2)}, u32[]{:S(2)}) collective-permute-start(bf16[288,1152]{1,0:T(8,128)(2,1)} %copy-done.11), channel_id=1, source_target_pairs={{0,1},{1,0},{2,3},{3,2},{4,5},{5,4},{6,7},{7,6},{8,9},{9,8},{10,11... | collective-permute-start | bytes 1990664 | tf_op jit(solution)/shard_map/ppermute | solution.py:361
  51.3 17.7 %collective-permute-start.16 = (bf16[288,1152]{1,0:T(8,128)(2,1)}, bf16[288,1152]{1,0:T(8,128)(2,1)}, u32[]{:S(2)}, u32[]{:S(2)}) collective-permute-start(bf16[288,1152]{1,0:T(8,128)(2,1)} %collective-permute-done.10.refs_14_), channel_id=1, source_target_pairs={{0,1},{1,0},{2,3},{3,2},{4,5},{5,4},{6,7},{7,6},{8,9},{9,8},{10,11... | collective-permute-start | bytes 1990664 | tf_op jit(solution)/shard_map/ppermute | solution.py:361
  51.8 17.2 %collective-permute-start.15 = (bf16[288,1152]{1,0:T(8,128)(2,1)}, bf16[288,1152]{1,0:T(8,128)(2,1)}, u32[]{:S(2)}, u32[]{:S(2)}) collective-permute-start(bf16[288,1152]{1,0:T(8,128)(2,1)} %collective-permute-done.14.refs_12_), channel_id=1, source_target_pairs={{0,1},{1,0},{2,3},{3,2},{4,5},{5,4},{6,7},{7,6},{8,9},{9,8},{10,11... | collective-permute-start | bytes 1990664 | tf_op jit(solution)/shard_map/ppermute | solution.py:361
  58.9 10.1 %collective-permute-start.20 = (bf16[288,1152]{1,0:T(8,128)(2,1)}, bf16[288,1152]{1,0:T(8,128)(2,1)}, u32[]{:S(2)}, u32[]{:S(2)}) collective-permute-start(bf16[288,1152]{1,0:T(8,128)(2,1)} %collective-permute-done.19.refs_18_), channel_id=1, source_target_pairs={{0,1},{1,0},{2,3},{3,2},{4,5},{5,4},{6,7},{7,6},{8,9},{9,8},{10,11... | collective-permute-start | bytes 1990664 | tf_op jit(solution)/shard_map/ppermute | solution.py:361
  61.1 8.0 %collective-permute-start.18 = (bf16[288,1152]{1,0:T(8,128)(2,1)}, bf16[288,1152]{1,0:T(8,128)(2,1)}, u32[]{:S(2)}, u32[]{:S(2)}) collective-permute-start(bf16[288,1152]{1,0:T(8,128)(2,1)} %collective-permute-done.17.refs_16_), channel_id=1, source_target_pairs={{0,1},{1,0},{2,3},{3,2},{4,5},{5,4},{6,7},{7,6},{8,9},{9,8},{10,11... | collective-permute-start | bytes 1990664 | tf_op jit(solution)/shard_map/ppermute | solution.py:361
  76.7 10.4 %collective-permute-start.21 = (bf16[32,1152]{1,0:T(8,128)(2,1)S(1)}, bf16[32,1152]{1,0:T(8,128)(2,1)S(1)}, u32[]{:S(2)}, u32[]{:S(2)}) collective-permute-start(bf16[32,1152]{1,0:T(8,128)(2,1)S(1)} %get-tuple-element.162), channel_id=1, source_target_pairs={{0,16},{4,20},{8,24},{12,28},{16,0},{20,4},{24,8},{28,12},{1,17},{... | collective-permute-start | bytes 221192 | tf_op jit(solution)/shard_map/ppermute | solution.py:365
  77.8 11.8 %collective-permute-start.22 = (bf16[32,1152]{1,0:T(8,128)(2,1)S(1)}, bf16[32,1152]{1,0:T(8,128)(2,1)S(1)}, u32[]{:S(2)}, u32[]{:S(2)}) collective-permute-start(bf16[32,1152]{1,0:T(8,128)(2,1)S(1)} %get-tuple-element.163), channel_id=1, source_target_pairs={{0,20},{4,16},{8,28},{12,24},{16,4},{20,0},{24,12},{28,8},{1,21},{... | collective-permute-start | bytes 221192 | tf_op jit(solution)/shard_map/ppermute | solution.py:365
  81.9 7.7 %collective-permute-start.23 = (bf16[32,1152]{1,0:T(8,128)(2,1)S(1)}, bf16[32,1152]{1,0:T(8,128)(2,1)S(1)}, u32[]{:S(2)}, u32[]{:S(2)}) collective-permute-start(bf16[32,1152]{1,0:T(8,128)(2,1)S(1)} %get-tuple-element.164), channel_id=1, source_target_pairs={{0,4},{4,0},{8,12},{12,8},{16,20},{20,16},{24,28},{28,24},{1,5},{5... | collective-permute-start | bytes 221192 | tf_op jit(solution)/shard_map/ppermute | solution.py:365
  81.9 7.7 %collective-permute-start.24 = (bf16[32,1152]{1,0:T(8,128)(2,1)S(1)}, bf16[32,1152]{1,0:T(8,128)(2,1)S(1)}, u32[]{:S(2)}, u32[]{:S(2)}) collective-permute-start(bf16[32,1152]{1,0:T(8,128)(2,1)S(1)} %get-tuple-element.165), channel_id=1, source_target_pairs={{0,24},{4,28},{8,16},{12,20},{16,8},{20,12},{24,0},{28,4},{1,25},{... | collective-permute-start | bytes 221192 | tf_op jit(solution)/shard_map/ppermute | solution.py:365
  84.7 7.3 %collective-permute-start.25 = (bf16[32,1152]{1,0:T(8,128)(2,1)S(1)}, bf16[32,1152]{1,0:T(8,128)(2,1)S(1)}, u32[]{:S(2)}, u32[]{:S(2)}) collective-permute-start(bf16[32,1152]{1,0:T(8,128)(2,1)S(1)} %get-tuple-element.166), channel_id=1, source_target_pairs={{0,28},{4,24},{8,20},{12,16},{16,12},{20,8},{24,4},{28,0},{1,29},{... | collective-permute-start | bytes 221192 | tf_op jit(solution)/shard_map/ppermute | solution.py:365
  87.2 4.7 %collective-permute-start.26 = (bf16[32,1152]{1,0:T(8,128)(2,1)S(1)}, bf16[32,1152]{1,0:T(8,128)(2,1)S(1)}, u32[]{:S(2)}, u32[]{:S(2)}) collective-permute-start(bf16[32,1152]{1,0:T(8,128)(2,1)S(1)} %get-tuple-element.167), channel_id=1, source_target_pairs={{0,8},{4,12},{8,0},{12,4},{16,24},{20,28},{24,16},{28,20},{1,9},{5... | collective-permute-start | bytes 221192 | tf_op jit(solution)/shard_map/ppermute | solution.py:365
  89.6 5.3 %collective-permute-start.27 = (bf16[32,1152]{1,0:T(8,128)(2,1)S(1)}, bf16[32,1152]{1,0:T(8,128)(2,1)S(1)}, u32[]{:S(2)}, u32[]{:S(2)}) collective-permute-start(bf16[32,1152]{1,0:T(8,128)(2,1)S(1)} %get-tuple-element.168), channel_id=1, source_target_pairs={{0,12},{4,8},{8,4},{12,0},{16,28},{20,24},{24,20},{28,16},{1,13},{... | collective-permute-start | bytes 221192 | tf_op jit(solution)/shard_map/ppermute | solution.py:365

commit v4 on v3

--- a/solution.py
+++ b/solution.py
@@ -483,8 +483,8 @@
         positions = patches // frame_count
         pieces = list(temporal_block(frame, arrived, moved, mod_temporal, weights, positions))
         middle = frame_count // 2
-        far = list(range(middle, frame_count))
-        order = [0, *far[:2], 1, *far[2:], *range(2, middle)]
+        far = [*range(middle * 3 // 2, frame_count), *range(middle, middle * 3 // 2)]
+        order = [0, 1, far[0], 2, *far[1:], *range(3, middle)]
         for offset in order[1:]:
             pieces[offset] = frame_swap(pieces[offset], offset, frame_count)
         result = join_frames(frame, [pieces[offset] for offset in order], order)

time: 96.1 us -> 96.4 us (level)
  transfers between devices with their start and end apart: 29 -> 29, of which waited for: 8 -> 9; matrix products, arithmetic and copies ran while one was open for 0% -> 0% of each run, Pallas kernels for 17% -> 17%
where the time goes in v4:
time: 96.4 us; the launch traced here: 95.9 us
  starting transfers between devices  33 us (34%)
  waiting for transfers between devices  31.3 us (32%)
  Pallas kernels  24.6 us (26%)
  local copies, waits for them, and re-layouts  6.72 us (7%)
    ppermute x7, starting transfers between devices, frame_swap(): lax.ppermute(array, 'frame', [(rank, rank ^ offset) for rank in range(cou...  11.1 us
    ppermute x6, starting transfers between devices, ring_step(): return lax.ppermute(array, ('frame', 'patch'), pairs)  9.92 us
    ppermute x15, waiting for transfers between devices, swap(): lax.ppermute(array, 'patch', [(rank, rank ^ offset) for rank in range(cou...  9.51 us
    pallas_call x4, Pallas kernels, spatial_attention(): pl.pallas_call(lambda *refs: attention_kernel(parts, *refs), out_shape=ja...  9.07 us
    pallas_call x1, Pallas kernels, temporal_block(): pl.pallas_call(lambda *refs: temporal_kernel(positions, 4, *refs), out_sh...  7.7 us
    ppermute x15, starting transfers between devices, swap(): lax.ppermute(array, 'patch', [(rank, rank ^ offset) for rank in range(cou...  7.55 us
    all_to_all x1, waiting for transfers between devices, exchange(): pieces = lax.all_to_all(pieces, 'frame', 0, 0, tiled=True)  7.48 us
    ppermute x7, waiting for transfers between devices, frame_swap(): lax.ppermute(array, 'frame', [(rank, rank ^ offset) for rank in range(cou...  7.25 us
  transfers between devices with their start and end apart: 29, of which 9 were waited for; matrix products, arithmetic and copies ran while one was open for 0% of the time, Pallas kernels for 17%

profile of v4, /device:TPU:0, one launch (start us, length us, event | category | flops | bytes accessed | tf_op | source)
XLA Modules:
  0.0 95.9 jit_solution(6055157184788894513)
XLA Ops:
  0.0 0.5 collective-permute-start
  0.5 2.5 %collective-permute-start.1 = (bf16[256,1152]{1,0:T(8,128)(2,1)}, bf16[256,1152]{1,0:T(8,128)(2,1)S(1)}, u32[]{:S(2)}, u32[]{:S(2)}) collective-permute-start(bf16[256,1152]{1,0:T(8,128)(2,1)} %bitcast.15), channel_id=1, source_target_pairs={{0,2},{1,3},{2,0},{3,1},{4,6},{5,7},{6,4},{7,5},{8,10},{9,11},{10,... | collective-permute-start | bytes 1769480 | tf_op jit(solution)/shard_map/ppermute | solution.py:361
  2.9 1.2 %copy-done.5 = bf16[1152,432]{0,1:T(8,128)(2,1)S(1)} copy-done((bf16[1152,432]{0,1:T(8,128)(2,1)S(1)}, bf16[1152,432]{0,1:T(8,128)(2,1)}, u32[]{:S(2)}) %copy-start.5) | copy-done | bytes 995352
  4.2 1.0 %copy-done.7 = bf16[144,1152]{1,0:T(8,128)(2,1)S(1)} copy-done((bf16[144,1152]{1,0:T(8,128)(2,1)S(1)}, bf16[144,1152]{1,0:T(8,128)(2,1)}, u32[]{:S(2)}) %copy-start.7) | copy-done | bytes 331800
  5.1 0.1 pack.1
  5.2 1.6 %collective-permute-start.2 = (bf16[288,1152]{1,0:T(8,128)(2,1)S(1)}, bf16[288,1152]{1,0:T(8,128)(2,1)S(1)}, u32[]{:S(2)}, u32[]{:S(2)}) collective-permute-start(bf16[288,1152]{1,0:T(8,128)(2,1)S(1)} %get-tuple-element.105.refs_4_), channel_id=1, source_target_pairs={{0,8},{1,5},{2,10},{3,7},{8,16},{9,1},{10,18},{11,3},{16,24},{17,9... | collective-permute-start | bytes 1990664 | tf_op jit(solution)/shard_map/ppermute | solution.py:376
  6.9 1.6 %collective-permute-start.5 = (bf16[288,1152]{1,0:T(8,128)(2,1)S(1)}, bf16[288,1152]{1,0:T(8,128)(2,1)S(1)}, u32[]{:S(2)}, u32[]{:S(2)}) collective-permute-start(bf16[288,1152]{1,0:T(8,128)(2,1)S(1)} %get-tuple-element.119.refs_5_), channel_id=1, source_target_pairs={{0,8},{1,5},{2,10},{3,7},{8,16},{9,1},{10,18},{11,3},{16,24},{17,9... | collective-permute-start | bytes 1990664 | tf_op jit(solution)/shard_map/ppermute | solution.py:376
  8.4 1.6 %copy-done = bf16[1152,864]{0,1:T(8,128)(2,1)S(1)} copy-done((bf16[1152,864]{0,1:T(8,128)(2,1)S(1)}, bf16[1152,864]{0,1:T(8,128)(2,1)}, u32[]{:S(2)}) %copy-start) | copy-done | bytes 1990680
  10.0 1.1 %copy-done.3 = bf16[1,256,1152]{2,1,0:T(8,128)(2,1)S(1)} copy-done((bf16[1,256,1152]{2,1,0:T(8,128)(2,1)S(1)}, bf16[1,256,1152]{2,1,0:T(8,128)(2,1)}, u32[]{:S(2)}) %copy-start.3) | copy-done | bytes 589848
  11.1 0.7 copy-done.8
  11.8 1.2 %spatial_qkv.4 = (bf16[8,80,256]{2,1,0:T(8,128)(2,1)S(1)}, bf16[4,256,80]{2,1,0:T(8,128)(2,1)S(1)}) custom-call(bf16[256,1152]{1,0:T(8,128)(2,1)S(1)} %bitcast.16, f32[3,1152]{1,0:T(4,128)S(1)} %copy-done.8, bf16[864,1152]{1,0:T(8,128)(2,1)S(1)} %bitcast.8), custom_call_target="tpu_custom_call" | custom-call | flops 1 | bytes 1 | tf_op jit(solution)/shard_map/spatial_qkv/pallas_call | solution.py:70
  13.0 0.4 copy-done.1
  13.3 1.2 %spatial_qkv.5 = (bf16[8,80,256]{2,1,0:T(8,128)(2,1)S(1)}, bf16[4,256,80]{2,1,0:T(8,128)(2,1)S(1)}) custom-call(bf16[256,1152]{1,0:T(8,128)(2,1)S(1)} %collective-permute-done.tokens_ref, f32[3,1152]{1,0:T(4,128)S(1)} %copy-done.8, bf16[864,1152]{1,0:T(8,128)(2,1)S(1)} %bitcast.9), custom_call_target="tpu_custom_call" | custom-call | flops 1 | bytes 1 | tf_op jit(solution)/shard_map/spatial_qkv/pallas_call | solution.py:70
  14.5 2.6 %collective-permute-done.1.tokens_ref = bf16[256,1152]{1,0:T(8,128)(2,1)S(1)} collective-permute-done((bf16[256,1152]{1,0:T(8,128)(2,1)}, bf16[256,1152]{1,0:T(8,128)(2,1)S(1)}, u32[]{:S(2)}, u32[]{:S(2)}) %collective-permute-start.1) | collective-permute-done | bytes 589856 | tf_op jit(solution)/shard_map/ppermute | solution.py:361
  17.2 0.0 collective-permute-start.3
  17.2 1.2 %spatial_qkv.6 = (bf16[8,80,256]{2,1,0:T(8,128)(2,1)S(1)}, bf16[4,256,80]{2,1,0:T(8,128)(2,1)S(1)}) custom-call(bf16[256,1152]{1,0:T(8,128)(2,1)S(1)} %collective-permute-done.1.tokens_ref, f32[3,1152]{1,0:T(4,128)S(1)} %copy-done.9, bf16[864,1152]{1,0:T(8,128)(2,1)S(1)} %bitcast.10), custom_call_target="tpu_custom_call" | custom-call | flops 1610612736 | bytes 1 | tf_op jit(solution)/shard_map/spatial_qkv/pallas_call | solution.py:70
  18.3 0.0 collective-permute-done.2.refs_6_
  18.3 1.9 %collective-permute-start.7 = (bf16[288,1152]{1,0:T(8,128)(2,1)S(1)}, bf16[288,1152]{1,0:T(8,128)(2,1)S(1)}, u32[]{:S(2)}, u32[]{:S(2)}) collective-permute-start(bf16[288,1152]{1,0:T(8,128)(2,1)S(1)} %collective-permute-done.2.refs_6_), channel_id=1, source_target_pairs={{0,8},{1,5},{2,10},{3,7},{8,16},{9,1},{10,18},{11,3},{16,24},{17,9... | collective-permute-start | bytes 1990664 | tf_op jit(solution)/shard_map/ppermute | solution.py:376
  20.2 1.2 %spatial_qkv.7 = (bf16[8,80,256]{2,1,0:T(8,128)(2,1)S(1)}, bf16[4,256,80]{2,1,0:T(8,128)(2,1)S(1)}) custom-call(bf16[256,1152]{1,0:T(8,128)(2,1)S(1)} %collective-permute-done.3.tokens_ref, f32[3,1152]{1,0:T(4,128)S(1)} %copy-done.9, bf16[864,1152]{1,0:T(8,128)(2,1)S(1)} %bitcast.11), custom_call_target="tpu_custom_call" | custom-call | flops 1 | bytes 1 | tf_op jit(solution)/shard_map/spatial_qkv/pallas_call | solution.py:70
  21.4 0.0 collective-permute-done.4.other_weight_ref
  21.4 2.3 %spatial_attention.4 = bf16[256,288]{1,0:T(8,128)(2,1)S(1)} custom-call(bf16[8,80,256]{2,1,0:T(8,128)(2,1)S(1)} %get-tuple-element.143.refs_0_.refs_4_, bf16[8,80,256]{2,1,0:T(8,128)(2,1)S(1)} %get-tuple-element.140.refs_1_.refs_0_, bf16[8,80,256]{2,1,0:T(8,128)(2,1)S(1)} %get-tuple-element.141.refs_2_.refs_0_, ...), custom_call_target="tpu_custom_call" | custom-call | flops 1 | bytes 1 | tf_op jit(solution)/shard_map/spatial_attention/pallas_call | solution.py:105
  23.7 0.0 copy-start.2
  23.7 0.0 collective-permute-done.5.refs_7_
  23.7 0.2 collective-permute-start.6
  23.9 2.3 %spatial_attention.5.heads_ref = bf16[256,288]{1,0:T(8,128)(2,1)S(1)} custom-call(bf16[8,80,256]{2,1,0:T(8,128)(2,1)S(1)} %get-tuple-element.142.refs_3_.refs_0_, bf16[8,80,256]{2,1,0:T(8,128)(2,1)S(1)} %get-tuple-element.140.refs_1_.refs_0_, bf16[8,80,256]{2,1,0:T(8,128)(2,1)S(1)} %get-tuple-element.141.refs_2_.refs_0_, ...), custom_call_target="tpu_custom_call" | custom-call | flops 1 | bytes 1 | tf_op jit(solution)/shard_map/spatial_attention/pallas_call | solution.py:105
  26.2 0.0 collective-permute-done.6.other_ref
  26.2 0.8 chip_partial.1
  27.1 1.6 %collective-permute-start.9 = (bf16[256,1152]{1,0:T(8,128)(2,1)S(1)}, bf16[256,1152]{1,0:T(8,128)(2,1)S(1)}, u32[]{:S(2)}, u32[]{:S(2)}) collective-permute-start(bf16[256,1152]{1,0:T(8,128)(2,1)S(1)} %chip_partial.1), channel_id=1, source_target_pairs={{0,2},{1,3},{2,0},{3,1},{4,6},{5,7},{6,4},{7,5},{8,10},{9,11},{10,... | collective-permute-start | bytes 1769480 | tf_op jit(solution)/shard_map/ppermute | solution.py:361
  28.6 2.3 %spatial_attention.6 = bf16[256,288]{1,0:T(8,128)(2,1)S(1)} custom-call(bf16[8,80,256]{2,1,0:T(8,128)(2,1)S(1)} %get-tuple-element.141.refs_2_.refs_0_, bf16[8,80,256]{2,1,0:T(8,128)(2,1)S(1)} %get-tuple-element.140.refs_1_.refs_0_, bf16[8,80,256]{2,1,0:T(8,128)(2,1)S(1)} %get-tuple-element.141.refs_2_.refs_0_, ...), custom_call_target="tpu_custom_call" | custom-call | flops 1 | bytes 1 | tf_op jit(solution)/shard_map/spatial_attention/pallas_call | solution.py:105
  30.9 0.0 copy-start.4
  30.9 1.6 %collective-permute-start.10 = (bf16[288,1152]{1,0:T(8,128)(2,1)S(1)}, bf16[288,1152]{1,0:T(8,128)(2,1)}, u32[]{:S(2)}, u32[]{:S(2)}) collective-permute-start(bf16[288,1152]{1,0:T(8,128)(2,1)S(1)} %collective-permute-done.7.refs_10_), channel_id=1, source_target_pairs={{0,8},{1,5},{2,10},{3,7},{8,16},{9,1},{10,18},{11,3},{16,24},{17,9... | collective-permute-start | bytes 1990664 | tf_op jit(solution)/shard_map/ppermute | solution.py:376
  32.6 2.3 %spatial_attention.7.heads_ref = bf16[256,288]{1,0:T(8,128)(2,1)S(1)} custom-call(bf16[8,80,256]{2,1,0:T(8,128)(2,1)S(1)} %get-tuple-element.140.refs_1_.refs_0_, bf16[8,80,256]{2,1,0:T(8,128)(2,1)S(1)} %get-tuple-element.140.refs_1_.refs_0_, bf16[8,80,256]{2,1,0:T(8,128)(2,1)S(1)} %get-tuple-element.141.refs_2_.refs_0_, ...), custom_call_target="tpu_custom_call" | custom-call | flops 1 | bytes 1 | tf_op jit(solution)/shard_map/spatial_attention/pallas_call | solution.py:105
  34.8 0.1 collective-permute-start.8
  34.9 1.6 %collective-permute-start.14 = (bf16[288,1152]{1,0:T(8,128)(2,1)S(1)}, bf16[288,1152]{1,0:T(8,128)(2,1)}, u32[]{:S(2)}, u32[]{:S(2)}) collective-permute-start(bf16[288,1152]{1,0:T(8,128)(2,1)S(1)} %collective-permute-done.5.refs_7_), channel_id=1, source_target_pairs={{0,8},{1,5},{2,10},{3,7},{8,16},{9,1},{10,18},{11,3},{16,24},{17,9... | collective-permute-start | bytes 1990664 | tf_op jit(solution)/shard_map/ppermute | solution.py:376
  36.6 0.8 spatial_base.1.base_ref
  37.4 0.0 copy-start.10
  37.4 0.1 collective-permute-start.11
  37.5 0.5 collective-permute-start.12
  38.0 4.7 %collective-permute-done.9.refs_0_ = bf16[256,1152]{1,0:T(8,128)(2,1)S(1)} collective-permute-done((bf16[256,1152]{1,0:T(8,128)(2,1)S(1)}, bf16[256,1152]{1,0:T(8,128)(2,1)S(1)}, u32[]{:S(2)}, u32[]{:S(2)}) %collective-permute-start.9) | collective-permute-done | bytes 589856 | tf_op jit(solution)/shard_map/ppermute | solution.py:361
  42.7 0.2 spatial_add.1
  42.9 0.0 copy-start.6
  42.9 0.8 copy-done.6
  43.7 1.6 %collective-permute-start.19 = (bf16[288,1152]{1,0:T(8,128)(2,1)}, bf16[288,1152]{1,0:T(8,128)(2,1)}, u32[]{:S(2)}, u32[]{:S(2)}) collective-permute-start(bf16[288,1152]{1,0:T(8,128)(2,1)} %collective-permute-done.10.refs_14_), channel_id=1, source_target_pairs={{0,8},{1,5},{2,10},{3,7},{8,16},{9,1},{10,18},{11,3},{16,24},{17,9... | collective-permute-start | bytes 1990664 | tf_op jit(solution)/shard_map/ppermute | solution.py:376
  45.3 1.5 %collective-permute-start.17 = (bf16[288,1152]{1,0:T(8,128)(2,1)}, bf16[288,1152]{1,0:T(8,128)(2,1)}, u32[]{:S(2)}, u32[]{:S(2)}) collective-permute-start(bf16[288,1152]{1,0:T(8,128)(2,1)} %collective-permute-done.10.refs_14_), channel_id=1, source_target_pairs={{0,2},{1,3},{2,0},{3,1},{4,6},{5,7},{6,4},{7,5},{8,10},{9,11},{10,... | collective-permute-start | bytes 1990664 | tf_op jit(solution)/shard_map/ppermute | solution.py:361
  46.8 4.4 %all-to-all-start = ((bf16[8,32,1152]{2,1,0:T(8,128)(2,1)}), bf16[8,32,1152]{2,1,0:T(8,128)(2,1)S(1)}, u32[]{:S(2)}, u32[]{:S(2)}) async-start(bf16[8,32,1152]{2,1,0:T(8,128)(2,1)} %bitcast.19), calls=%async_computation | async-start | bytes 1179648 | tf_op jit(solution)/shard_map/all_to_all | solution.py:388
  51.2 0.1 collective-permute-start.13
  51.3 0.5 collective-permute-start.16
  51.8 0.1 collective-permute-start.15
  51.9 7.1 %collective-permute-done.19.refs_18_ = bf16[288,1152]{1,0:T(8,128)(2,1)} collective-permute-done((bf16[288,1152]{1,0:T(8,128)(2,1)}, bf16[288,1152]{1,0:T(8,128)(2,1)}, u32[]{:S(2)}, u32[]{:S(2)}) %collective-permute-start.19) | collective-permute-done | bytes 663584 | tf_op jit(solution)/shard_map/ppermute | solution.py:376
  58.9 2.1 %collective-permute-done.17.refs_16_ = bf16[288,1152]{1,0:T(8,128)(2,1)} collective-permute-done((bf16[288,1152]{1,0:T(8,128)(2,1)}, bf16[288,1152]{1,0:T(8,128)(2,1)}, u32[]{:S(2)}, u32[]{:S(2)}) %collective-permute-start.17) | collective-permute-done | bytes 663584 | tf_op jit(solution)/shard_map/ppermute | solution.py:361
  61.1 7.5 %all-to-all-done = bf16[8,32,1152]{2,1,0:T(8,128)(2,1)S(1)} async-done(((bf16[8,32,1152]{2,1,0:T(8,128)(2,1)}), bf16[8,32,1152]{2,1,0:T(8,128)(2,1)S(1)}, u32[]{:S(2)}, u32[]{:S(2)}) %all-to-all-start) | async-done | bytes 589856 | tf_op jit(solution)/shard_map/all_to_all | solution.py:388
  68.6 0.4 temporal_norm.1.refs_2_
  69.0 7.7 %temporal_block.1 = (bf16[32,1152]{1,0:T(8,128)(2,1)S(1)}, bf16[32,1152]{1,0:T(8,128)(2,1)S(1)}, bf16[32,1152]{1,0:T(8,128)(2,1)S(1)}, bf16[32,1152]{1,0:T(8,128...) custom-call(s32[1]{0:T(128)} %bitcast.1.refs_0_, ...), custom_call_target="tpu_custom_call" | custom-call | flops 1 | bytes 1 | tf_op jit(solution)/shard_map/temporal_block/pallas_call | solution.py:322
  76.7 2.8 %collective-permute-start.21 = (bf16[32,1152]{1,0:T(8,128)(2,1)S(1)}, bf16[32,1152]{1,0:T(8,128)(2,1)S(1)}, u32[]{:S(2)}, u32[]{:S(2)}) collective-permute-start(bf16[32,1152]{1,0:T(8,128)(2,1)S(1)} %get-tuple-element.162), channel_id=1, source_target_pairs={{0,4},{4,0},{8,12},{12,8},{16,20},{20,16},{24,28},{28,24},{1,5},{5... | collective-permute-start | bytes 221192 | tf_op jit(solution)/shard_map/ppermute | solution.py:365
  79.5 1.4 %collective-permute-start.22 = (bf16[32,1152]{1,0:T(8,128)(2,1)S(1)}, bf16[32,1152]{1,0:T(8,128)(2,1)S(1)}, u32[]{:S(2)}, u32[]{:S(2)}) collective-permute-start(bf16[32,1152]{1,0:T(8,128)(2,1)S(1)} %get-tuple-element.163), channel_id=1, source_target_pairs={{0,24},{4,28},{8,16},{12,20},{16,8},{20,12},{24,0},{28,4},{1,25},{... | collective-permute-start | bytes 221192 | tf_op jit(solution)/shard_map/ppermute | solution.py:365
  81.0 2.2 %collective-permute-start.24 = (bf16[32,1152]{1,0:T(8,128)(2,1)S(1)}, bf16[32,1152]{1,0:T(8,128)(2,1)S(1)}, u32[]{:S(2)}, u32[]{:S(2)}) collective-permute-start(bf16[32,1152]{1,0:T(8,128)(2,1)S(1)} %get-tuple-element.165), channel_id=1, source_target_pairs={{0,28},{4,24},{8,20},{12,16},{16,12},{20,8},{24,4},{28,0},{1,29},{... | collective-permute-start | bytes 221192 | tf_op jit(solution)/shard_map/ppermute | solution.py:365
  83.1 2.1 %collective-permute-start.25 = (bf16[32,1152]{1,0:T(8,128)(2,1)S(1)}, bf16[32,1152]{1,0:T(8,128)(2,1)S(1)}, u32[]{:S(2)}, u32[]{:S(2)}) collective-permute-start(bf16[32,1152]{1,0:T(8,128)(2,1)S(1)} %get-tuple-element.166), channel_id=1, source_target_pairs={{0,16},{4,20},{8,24},{12,28},{16,0},{20,4},{24,8},{28,12},{1,17},{... | collective-permute-start | bytes 221192 | tf_op jit(solution)/shard_map/ppermute | solution.py:365
  85.2 2.0 %collective-permute-start.26 = (bf16[32,1152]{1,0:T(8,128)(2,1)S(1)}, bf16[32,1152]{1,0:T(8,128)(2,1)S(1)}, u32[]{:S(2)}, u32[]{:S(2)}) collective-permute-start(bf16[32,1152]{1,0:T(8,128)(2,1)S(1)} %get-tuple-element.167), channel_id=1, source_target_pairs={{0,20},{4,16},{8,28},{12,24},{16,4},{20,0},{24,12},{28,8},{1,21},{... | collective-permute-start | bytes 221192 | tf_op jit(solution)/shard_map/ppermute | solution.py:365
  87.2 0.6 collective-permute-start.27
  87.8 1.0 %collective-permute-done.24.refs_5_ = bf16[32,1152]{1,0:T(8,128)(2,1)S(1)} collective-permute-done((bf16[32,1152]{1,0:T(8,128)(2,1)S(1)}, bf16[32,1152]{1,0:T(8,128)(2,1)S(1)}, u32[]{:S(2)}, u32[]{:S(2)}) %collective-permute-start.24) | collective-permute-done | bytes 73760 | tf_op jit(solution)/shard_map/ppermute | solution.py:365
  88.9 4.5 %collective-permute-done.25.refs_6_ = bf16[32,1152]{1,0:T(8,128)(2,1)S(1)} collective-permute-done((bf16[32,1152]{1,0:T(8,128)(2,1)S(1)}, bf16[32,1152]{1,0:T(8,128)(2,1)S(1)}, u32[]{:S(2)}, u32[]{:S(2)}) %collective-permute-start.25) | collective-permute-done | bytes 73760 | tf_op jit(solution)/shard_map/ppermute | solution.py:365
  93.4 1.4 %collective-permute-done.26.refs_7_ = bf16[32,1152]{1,0:T(8,128)(2,1)S(1)} collective-permute-done((bf16[32,1152]{1,0:T(8,128)(2,1)S(1)}, bf16[32,1152]{1,0:T(8,128)(2,1)S(1)}, u32[]{:S(2)}, u32[]{:S(2)}) %collective-permute-start.26) | collective-permute-done | bytes 73760 | tf_op jit(solution)/shard_map/ppermute | solution.py:365
  94.8 0.3 collective-permute-done.27.refs_8_
  95.1 0.9 join_frames.1
  (33 shorter events, 0.1 us)
Async XLA Ops:
  0.0 13.0 %collective-permute-start = (bf16[256,1152]{1,0:T(8,128)(2,1)}, bf16[256,1152]{1,0:T(8,128)(2,1)S(1)}, u32[]{:S(2)}, u32[]{:S(2)}) collective-permute-start(bf16[256,1152]{1,0:T(8,128)(2,1)} %bitcast.14), channel_id=1, source_target_pairs={{0,1},{1,0},{2,3},{3,2},{4,5},{5,4},{6,7},{7,6},{8,9},{9,8},{10,11... | collective-permute-start | bytes 1769480 | tf_op jit(solution)/shard_map/ppermute | solution.py:361
  0.5 16.7 %collective-permute-start.1 = (bf16[256,1152]{1,0:T(8,128)(2,1)}, bf16[256,1152]{1,0:T(8,128)(2,1)S(1)}, u32[]{:S(2)}, u32[]{:S(2)}) collective-permute-start(bf16[256,1152]{1,0:T(8,128)(2,1)} %bitcast.15), channel_id=1, source_target_pairs={{0,2},{1,3},{2,0},{3,1},{4,6},{5,7},{6,4},{7,5},{8,10},{9,11},{10,... | collective-permute-start | bytes 1769480 | tf_op jit(solution)/shard_map/ppermute | solution.py:361
  2.9 1.2 %copy-start.5 = (bf16[1152,432]{0,1:T(8,128)(2,1)S(1)}, bf16[1152,432]{0,1:T(8,128)(2,1)}, u32[]{:S(2)}) copy-start(bf16[1152,432]{0,1:T(8,128)(2,1)} %param.12) | copy-start | bytes 2985988
  4.1 1.0 %copy-start.7 = (bf16[144,1152]{1,0:T(8,128)(2,1)S(1)}, bf16[144,1152]{1,0:T(8,128)(2,1)}, u32[]{:S(2)}) copy-start(bf16[144,1152]{1,0:T(8,128)(2,1)} %out_ref.1) | copy-start | bytes 995332
  5.2 13.1 %collective-permute-start.2 = (bf16[288,1152]{1,0:T(8,128)(2,1)S(1)}, bf16[288,1152]{1,0:T(8,128)(2,1)S(1)}, u32[]{:S(2)}, u32[]{:S(2)}) collective-permute-start(bf16[288,1152]{1,0:T(8,128)(2,1)S(1)} %get-tuple-element.105.refs_4_), channel_id=1, source_target_pairs={{0,8},{1,5},{2,10},{3,7},{8,16},{9,1},{10,18},{11,3},{16,24},{17,9... | collective-permute-start | bytes 1990664 | tf_op jit(solution)/shard_map/ppermute | solution.py:376
  6.9 14.5 %collective-permute-start.4 = (bf16[288,1152]{1,0:T(8,128)(2,1)}, bf16[288,1152]{1,0:T(8,128)(2,1)S(1)}, u32[]{:S(2)}, u32[]{:S(2)}) collective-permute-start(bf16[288,1152]{1,0:T(8,128)(2,1)} %weight_ref.3), channel_id=1, source_target_pairs={{0,1},{1,0},{2,3},{3,2},{4,5},{5,4},{6,7},{7,6},{8,9},{9,8},{10,11... | collective-permute-start | bytes 1990664 | tf_op jit(solution)/shard_map/ppermute | solution.py:361
  6.9 16.8 %collective-permute-start.5 = (bf16[288,1152]{1,0:T(8,128)(2,1)S(1)}, bf16[288,1152]{1,0:T(8,128)(2,1)S(1)}, u32[]{:S(2)}, u32[]{:S(2)}) collective-permute-start(bf16[288,1152]{1,0:T(8,128)(2,1)S(1)} %get-tuple-element.119.refs_5_), channel_id=1, source_target_pairs={{0,8},{1,5},{2,10},{3,7},{8,16},{9,1},{10,18},{11,3},{16,24},{17,9... | collective-permute-start | bytes 1990664 | tf_op jit(solution)/shard_map/ppermute | solution.py:376
  8.4 1.6 %copy-start = (bf16[1152,864]{0,1:T(8,128)(2,1)S(1)}, bf16[1152,864]{0,1:T(8,128)(2,1)}, u32[]{:S(2)}) copy-start(bf16[1152,864]{0,1:T(8,128)(2,1)} %param.9) | copy-start | bytes 5971972
  10.0 1.1 %copy-start.3 = (bf16[1,256,1152]{2,1,0:T(8,128)(2,1)S(1)}, bf16[1,256,1152]{2,1,0:T(8,128)(2,1)}, u32[]{:S(2)}) copy-start(bf16[1,256,1152]{2,1,0:T(8,128)(2,1)} %param.7) | copy-start | bytes 1769476
  11.1 0.7 copy-start.8
  11.8 1.6 %copy-start.1 = (bf16[1152,864]{0,1:T(8,128)(2,1)S(1)}, bf16[1152,864]{0,1:T(8,128)(2,1)}, u32[]{:S(2)}) copy-start(bf16[1152,864]{0,1:T(8,128)(2,1)} %param.9) | copy-start | bytes 5971972
  11.8 5.4 %copy-start.9 = (f32[3,1152]{1,0:T(4,128)S(1)}, f32[3,1152]{1,0:T(4,128)}, u32[]{:S(2)}) copy-start(f32[3,1152]{1,0:T(4,128)} %mod_ref.11) | copy-start | bytes 41476
  17.2 3.1 %collective-permute-start.3 = (bf16[256,1152]{1,0:T(8,128)(2,1)S(1)}, bf16[256,1152]{1,0:T(8,128)(2,1)S(1)}, u32[]{:S(2)}, u32[]{:S(2)}) collective-permute-start(bf16[256,1152]{1,0:T(8,128)(2,1)S(1)} %collective-permute-done.1.tokens_ref), channel_id=1, source_target_pairs={{0,1},{1,0},{2,3},{3,2},{4,5},{5,4},{6,7},{7,6},{8,9},{9,8},{10,11... | collective-permute-start | bytes 1769480 | tf_op jit(solution)/shard_map/ppermute | solution.py:361
  18.3 12.6 %collective-permute-start.7 = (bf16[288,1152]{1,0:T(8,128)(2,1)S(1)}, bf16[288,1152]{1,0:T(8,128)(2,1)S(1)}, u32[]{:S(2)}, u32[]{:S(2)}) collective-permute-start(bf16[288,1152]{1,0:T(8,128)(2,1)S(1)} %collective-permute-done.2.refs_6_), channel_id=1, source_target_pairs={{0,8},{1,5},{2,10},{3,7},{8,16},{9,1},{10,18},{11,3},{16,24},{17,9... | collective-permute-start | bytes 1990664 | tf_op jit(solution)/shard_map/ppermute | solution.py:376
  23.7 2.5 %copy-start.2 = (bf16[288,1152]{1,0:T(8,128)(2,1)S(1)}, bf16[288,1152]{1,0:T(8,128)(2,1)}, u32[]{:S(2)}) copy-start(bf16[288,1152]{1,0:T(8,128)(2,1)} %weight_ref.3) | copy-start | bytes 1990660
  23.7 2.5 %collective-permute-start.6 = (bf16[256,288]{1,0:T(8,128)(2,1)S(1)}, bf16[256,288]{1,0:T(8,128)(2,1)S(1)}, u32[]{:S(2)}, u32[]{:S(2)}) collective-permute-start(bf16[256,288]{1,0:T(8,128)(2,1)S(1)} %spatial_attention.4), channel_id=1, source_target_pairs={{0,1},{1,0},{2,3},{3,2},{4,5},{5,4},{6,7},{7,6},{8,9},{9,8},{10,11... | collective-permute-start | bytes 442376 | tf_op jit(solution)/shard_map/ppermute | solution.py:361
  27.1 15.6 %collective-permute-start.9 = (bf16[256,1152]{1,0:T(8,128)(2,1)S(1)}, bf16[256,1152]{1,0:T(8,128)(2,1)S(1)}, u32[]{:S(2)}, u32[]{:S(2)}) collective-permute-start(bf16[256,1152]{1,0:T(8,128)(2,1)S(1)} %chip_partial.1), channel_id=1, source_target_pairs={{0,2},{1,3},{2,0},{3,1},{4,6},{5,7},{6,4},{7,5},{8,10},{9,11},{10,... | collective-permute-start | bytes 1769480 | tf_op jit(solution)/shard_map/ppermute | solution.py:361
  30.9 5.6 %copy-start.4 = (bf16[1,256,1152]{2,1,0:T(8,128)(2,1)S(1)}, bf16[1,256,1152]{2,1,0:T(8,128)(2,1)}, u32[]{:S(2)}) copy-start(bf16[1,256,1152]{2,1,0:T(8,128)(2,1)} %param.7) | copy-start | bytes 1769476
  30.9 6.5 %copy-start.11 = (bf16[288,1152]{1,0:T(8,128)(2,1)}, bf16[288,1152]{1,0:T(8,128)(2,1)S(1)}, u32[]{:S(2)}) copy-start(bf16[288,1152]{1,0:T(8,128)(2,1)S(1)} %collective-permute-done.7.refs_10_) | copy-start | bytes 1990660
  30.9 12.8 %collective-permute-start.10 = (bf16[288,1152]{1,0:T(8,128)(2,1)S(1)}, bf16[288,1152]{1,0:T(8,128)(2,1)}, u32[]{:S(2)}, u32[]{:S(2)}) collective-permute-start(bf16[288,1152]{1,0:T(8,128)(2,1)S(1)} %collective-permute-done.7.refs_10_), channel_id=1, source_target_pairs={{0,8},{1,5},{2,10},{3,7},{8,16},{9,1},{10,18},{11,3},{16,24},{17,9... | collective-permute-start | bytes 1990664 | tf_op jit(solution)/shard_map/ppermute | solution.py:376
  34.8 1.7 %collective-permute-start.8 = (bf16[256,288]{1,0:T(8,128)(2,1)S(1)}, bf16[256,288]{1,0:T(8,128)(2,1)S(1)}, u32[]{:S(2)}, u32[]{:S(2)}) collective-permute-start(bf16[256,288]{1,0:T(8,128)(2,1)S(1)} %spatial_attention.6), channel_id=1, source_target_pairs={{0,1},{1,0},{2,3},{3,2},{4,5},{5,4},{6,7},{7,6},{8,9},{9,8},{10,11... | collective-permute-start | bytes 442376 | tf_op jit(solution)/shard_map/ppermute | solution.py:361
  34.9 16.3 %collective-permute-start.14 = (bf16[288,1152]{1,0:T(8,128)(2,1)S(1)}, bf16[288,1152]{1,0:T(8,128)(2,1)}, u32[]{:S(2)}, u32[]{:S(2)}) collective-permute-start(bf16[288,1152]{1,0:T(8,128)(2,1)S(1)} %collective-permute-done.5.refs_7_), channel_id=1, source_target_pairs={{0,8},{1,5},{2,10},{3,7},{8,16},{9,1},{10,18},{11,3},{16,24},{17,9... | collective-permute-start | bytes 1990664 | tf_op jit(solution)/shard_map/ppermute | solution.py:376
  37.4 31.1 %copy-start.10 = (f32[3,1152]{1,0:T(4,128)S(1)}, f32[3,1152]{1,0:T(4,128)}, u32[]{:S(2)}) copy-start(f32[3,1152]{1,0:T(4,128)} %refs_3_.1) | copy-start | bytes 41476
  37.4 13.9 %collective-permute-start.11 = (bf16[288,1152]{1,0:T(8,128)(2,1)S(1)}, bf16[288,1152]{1,0:T(8,128)(2,1)}, u32[]{:S(2)}, u32[]{:S(2)}) collective-permute-start(bf16[288,1152]{1,0:T(8,128)(2,1)S(1)} %collective-permute-done.2.refs_6_), channel_id=1, source_target_pairs={{0,1},{1,0},{2,3},{3,2},{4,5},{5,4},{6,7},{7,6},{8,9},{9,8},{10,11... | collective-permute-start | bytes 1990664 | tf_op jit(solution)/shard_map/ppermute | solution.py:361
  37.5 14.3 %collective-permute-start.12 = (bf16[288,1152]{1,0:T(8,128)(2,1)S(1)}, bf16[288,1152]{1,0:T(8,128)(2,1)}, u32[]{:S(2)}, u32[]{:S(2)}) collective-permute-start(bf16[288,1152]{1,0:T(8,128)(2,1)S(1)} %collective-permute-done.5.refs_7_), channel_id=1, source_target_pairs={{0,1},{1,0},{2,3},{3,2},{4,5},{5,4},{6,7},{7,6},{8,9},{9,8},{10,11... | collective-permute-start | bytes 1990664 | tf_op jit(solution)/shard_map/ppermute | solution.py:361
  42.9 0.8 copy-start.6
  43.7 15.2 %collective-permute-start.19 = (bf16[288,1152]{1,0:T(8,128)(2,1)}, bf16[288,1152]{1,0:T(8,128)(2,1)}, u32[]{:S(2)}, u32[]{:S(2)}) collective-permute-start(bf16[288,1152]{1,0:T(8,128)(2,1)} %collective-permute-done.10.refs_14_), channel_id=1, source_target_pairs={{0,8},{1,5},{2,10},{3,7},{8,16},{9,1},{10,18},{11,3},{16,24},{17,9... | collective-permute-start | bytes 1990664 | tf_op jit(solution)/shard_map/ppermute | solution.py:376
  45.3 15.8 %collective-permute-start.17 = (bf16[288,1152]{1,0:T(8,128)(2,1)}, bf16[288,1152]{1,0:T(8,128)(2,1)}, u32[]{:S(2)}, u32[]{:S(2)}) collective-permute-start(bf16[288,1152]{1,0:T(8,128)(2,1)} %collective-permute-done.10.refs_14_), channel_id=1, source_target_pairs={{0,2},{1,3},{2,0},{3,1},{4,6},{5,7},{6,4},{7,5},{8,10},{9,11},{10,... | collective-permute-start | bytes 1990664 | tf_op jit(solution)/shard_map/ppermute | solution.py:361
  46.8 21.8 %all-to-all-start = ((bf16[8,32,1152]{2,1,0:T(8,128)(2,1)}), bf16[8,32,1152]{2,1,0:T(8,128)(2,1)S(1)}, u32[]{:S(2)}, u32[]{:S(2)}) async-start(bf16[8,32,1152]{2,1,0:T(8,128)(2,1)} %bitcast.19), calls=%async_computation | async-start | bytes 1179648 | tf_op jit(solution)/shard_map/all_to_all | solution.py:388
  51.2 17.8 %collective-permute-start.13 = (bf16[288,1152]{1,0:T(8,128)(2,1)}, bf16[288,1152]{1,0:T(8,128)(2,1)}, u32[]{:S(2)}, u32[]{:S(2)}) collective-permute-start(bf16[288,1152]{1,0:T(8,128)(2,1)} %copy-done.11), channel_id=1, source_target_pairs={{0,1},{1,0},{2,3},{3,2},{4,5},{5,4},{6,7},{7,6},{8,9},{9,8},{10,11... | collective-permute-start | bytes 1990664 | tf_op jit(solution)/shard_map/ppermute | solution.py:361
  51.3 17.7 %collective-permute-start.16 = (bf16[288,1152]{1,0:T(8,128)(2,1)}, bf16[288,1152]{1,0:T(8,128)(2,1)}, u32[]{:S(2)}, u32[]{:S(2)}) collective-permute-start(bf16[288,1152]{1,0:T(8,128)(2,1)} %collective-permute-done.10.refs_14_), channel_id=1, source_target_pairs={{0,1},{1,0},{2,3},{3,2},{4,5},{5,4},{6,7},{7,6},{8,9},{9,8},{10,11... | collective-permute-start | bytes 1990664 | tf_op jit(solution)/shard_map/ppermute | solution.py:361
  51.8 17.2 %collective-permute-start.15 = (bf16[288,1152]{1,0:T(8,128)(2,1)}, bf16[288,1152]{1,0:T(8,128)(2,1)}, u32[]{:S(2)}, u32[]{:S(2)}) collective-permute-start(bf16[288,1152]{1,0:T(8,128)(2,1)} %collective-permute-done.14.refs_12_), channel_id=1, source_target_pairs={{0,1},{1,0},{2,3},{3,2},{4,5},{5,4},{6,7},{7,6},{8,9},{9,8},{10,11... | collective-permute-start | bytes 1990664 | tf_op jit(solution)/shard_map/ppermute | solution.py:361
  58.9 10.1 %collective-permute-start.20 = (bf16[288,1152]{1,0:T(8,128)(2,1)}, bf16[288,1152]{1,0:T(8,128)(2,1)}, u32[]{:S(2)}, u32[]{:S(2)}) collective-permute-start(bf16[288,1152]{1,0:T(8,128)(2,1)} %collective-permute-done.19.refs_18_), channel_id=1, source_target_pairs={{0,1},{1,0},{2,3},{3,2},{4,5},{5,4},{6,7},{7,6},{8,9},{9,8},{10,11... | collective-permute-start | bytes 1990664 | tf_op jit(solution)/shard_map/ppermute | solution.py:361
  61.1 8.0 %collective-permute-start.18 = (bf16[288,1152]{1,0:T(8,128)(2,1)}, bf16[288,1152]{1,0:T(8,128)(2,1)}, u32[]{:S(2)}, u32[]{:S(2)}) collective-permute-start(bf16[288,1152]{1,0:T(8,128)(2,1)} %collective-permute-done.17.refs_16_), channel_id=1, source_target_pairs={{0,1},{1,0},{2,3},{3,2},{4,5},{5,4},{6,7},{7,6},{8,9},{9,8},{10,11... | collective-permute-start | bytes 1990664 | tf_op jit(solution)/shard_map/ppermute | solution.py:361
  76.7 8.5 %collective-permute-start.21 = (bf16[32,1152]{1,0:T(8,128)(2,1)S(1)}, bf16[32,1152]{1,0:T(8,128)(2,1)S(1)}, u32[]{:S(2)}, u32[]{:S(2)}) collective-permute-start(bf16[32,1152]{1,0:T(8,128)(2,1)S(1)} %get-tuple-element.162), channel_id=1, source_target_pairs={{0,4},{4,0},{8,12},{12,8},{16,20},{20,16},{24,28},{28,24},{1,5},{5... | collective-permute-start | bytes 221192 | tf_op jit(solution)/shard_map/ppermute | solution.py:365
  79.5 7.7 %collective-permute-start.22 = (bf16[32,1152]{1,0:T(8,128)(2,1)S(1)}, bf16[32,1152]{1,0:T(8,128)(2,1)S(1)}, u32[]{:S(2)}, u32[]{:S(2)}) collective-permute-start(bf16[32,1152]{1,0:T(8,128)(2,1)S(1)} %get-tuple-element.163), channel_id=1, source_target_pairs={{0,24},{4,28},{8,16},{12,20},{16,8},{20,12},{24,0},{28,4},{1,25},{... | collective-permute-start | bytes 221192 | tf_op jit(solution)/shard_map/ppermute | solution.py:365
  81.0 6.9 %collective-permute-start.23 = (bf16[32,1152]{1,0:T(8,128)(2,1)S(1)}, bf16[32,1152]{1,0:T(8,128)(2,1)S(1)}, u32[]{:S(2)}, u32[]{:S(2)}) collective-permute-start(bf16[32,1152]{1,0:T(8,128)(2,1)S(1)} %get-tuple-element.164), channel_id=1, source_target_pairs={{0,8},{4,12},{8,0},{12,4},{16,24},{20,28},{24,16},{28,20},{1,9},{5... | collective-permute-start | bytes 221192 | tf_op jit(solution)/shard_map/ppermute | solution.py:365
  81.0 7.9 %collective-permute-start.24 = (bf16[32,1152]{1,0:T(8,128)(2,1)S(1)}, bf16[32,1152]{1,0:T(8,128)(2,1)S(1)}, u32[]{:S(2)}, u32[]{:S(2)}) collective-permute-start(bf16[32,1152]{1,0:T(8,128)(2,1)S(1)} %get-tuple-element.165), channel_id=1, source_target_pairs={{0,28},{4,24},{8,20},{12,16},{16,12},{20,8},{24,4},{28,0},{1,29},{... | collective-permute-start | bytes 221192 | tf_op jit(solution)/shard_map/ppermute | solution.py:365
  83.1 10.2 %collective-permute-start.25 = (bf16[32,1152]{1,0:T(8,128)(2,1)S(1)}, bf16[32,1152]{1,0:T(8,128)(2,1)S(1)}, u32[]{:S(2)}, u32[]{:S(2)}) collective-permute-start(bf16[32,1152]{1,0:T(8,128)(2,1)S(1)} %get-tuple-element.166), channel_id=1, source_target_pairs={{0,16},{4,20},{8,24},{12,28},{16,0},{20,4},{24,8},{28,12},{1,17},{... | collective-permute-start | bytes 221192 | tf_op jit(solution)/shard_map/ppermute | solution.py:365
  85.2 9.6 %collective-permute-start.26 = (bf16[32,1152]{1,0:T(8,128)(2,1)S(1)}, bf16[32,1152]{1,0:T(8,128)(2,1)S(1)}, u32[]{:S(2)}, u32[]{:S(2)}) collective-permute-start(bf16[32,1152]{1,0:T(8,128)(2,1)S(1)} %get-tuple-element.167), channel_id=1, source_target_pairs={{0,20},{4,16},{8,28},{12,24},{16,4},{20,0},{24,12},{28,8},{1,21},{... | collective-permute-start | bytes 221192 | tf_op jit(solution)/shard_map/ppermute | solution.py:365
  87.2 7.9 %collective-permute-start.27 = (bf16[32,1152]{1,0:T(8,128)(2,1)S(1)}, bf16[32,1152]{1,0:T(8,128)(2,1)S(1)}, u32[]{:S(2)}, u32[]{:S(2)}) collective-permute-start(bf16[32,1152]{1,0:T(8,128)(2,1)S(1)} %get-tuple-element.168), channel_id=1, source_target_pairs={{0,12},{4,8},{8,4},{12,0},{16,28},{20,24},{24,20},{28,16},{1,13},{... | collective-permute-start | bytes 221192 | tf_op jit(solution)/shard_map/ppermute | solution.py:365

commit v5 on v4

--- a/solution.py
+++ b/solution.py
@@ -436,6 +436,7 @@
         for offset in near:
             heads[offset + 1] = spatial_attention(qv[offset + 1], qv, keys)
         heads, qv, keys, first = barrier((heads, qv, keys, first))
+        second += [hop(array) for array in first[1:]]
 
         for offset in near:
             heads[offset + 1] = over_cores(heads[offset + 1])
@@ -451,7 +452,6 @@
         heads[1], qv, keys, second[0], first = barrier((heads[1], qv, keys, second[0], first))
 
         third = hop(second[0])
-        second += [hop(array) for array in first[1:]]
         heads[0] = spatial_attention(qv[0], qv, keys)
         heads[:2] = barrier(heads[:2])
 
@@ -483,8 +483,8 @@
         positions = patches // frame_count
         pieces = list(temporal_block(frame, arrived, moved, mod_temporal, weights, positions))
         middle = frame_count // 2
-        far = [*range(middle * 3 // 2, frame_count), *range(middle, middle * 3 // 2)]
-        order = [0, 1, far[0], 2, *far[1:], *range(3, middle)]
+        order = [1, middle, 2, *range(middle + 1, frame_count), *range(3, middle)]
+        order = [0, *dict.fromkeys(order)]
         for offset in order[1:]:
             pieces[offset] = frame_swap(pieces[offset], offset, frame_count)
         result = join_frames(frame, [pieces[offset] for offset in order], order)

time: 96.4 us -> 94.5 us (0.980)
  waiting for transfers between devices: 31.3 us -> 30.1 us
    ppermute x7, waiting for transfers between devices: 7.25 us -> 5.99 us  [frame_swap(): lax.ppermute(array, 'frame', [(rank, rank ^ offset) for rank in range(cou...]
  transfers between devices with their start and end apart: 29 -> 29, of which waited for: 9 -> 8; matrix products, arithmetic and copies ran while one was open for 0% -> 0% of each run, Pallas kernels for 17% -> 17%
where the time goes in v5:
time: 94.5 us; the launch traced here: 94.1 us
  starting transfers between devices  32.3 us (34%)
  waiting for transfers between devices  30.1 us (32%)
  Pallas kernels  24.6 us (26%)
  local copies, waits for them, and re-layouts  6.72 us (7%)
    ppermute x7, starting transfers between devices, frame_swap(): lax.ppermute(array, 'frame', [(rank, rank ^ offset) for rank in range(cou...  10.4 us
    ppermute x6, starting transfers between devices, ring_step(): return lax.ppermute(array, ('frame', 'patch'), pairs)  9.92 us
    ppermute x15, waiting for transfers between devices, swap(): lax.ppermute(array, 'patch', [(rank, rank ^ offset) for rank in range(cou...  9.51 us
    pallas_call x4, Pallas kernels, spatial_attention(): pl.pallas_call(lambda *refs: attention_kernel(parts, *refs), out_shape=ja...  9.07 us
    pallas_call x1, Pallas kernels, temporal_block(): pl.pallas_call(lambda *refs: temporal_kernel(positions, 4, *refs), out_sh...  7.7 us
    ppermute x15, starting transfers between devices, swap(): lax.ppermute(array, 'patch', [(rank, rank ^ offset) for rank in range(cou...  7.55 us
    all_to_all x1, waiting for transfers between devices, exchange(): pieces = lax.all_to_all(pieces, 'frame', 0, 0, tiled=True)  7.48 us
    ppermute x6, waiting for transfers between devices, ring_step(): return lax.ppermute(array, ('frame', 'patch'), pairs)  7.09 us
  transfers between devices with their start and end apart: 29, of which 8 were waited for; matrix products, arithmetic and copies ran while one was open for 0% of the time, Pallas kernels for 17%

profile of v5, /device:TPU:0, one launch (start us, length us, event | category | flops | bytes accessed | tf_op | source)
XLA Modules:
  0.0 94.1 jit_solution(10886089267778508461)
XLA Ops:
  0.0 0.5 collective-permute-start
  0.5 2.5 %collective-permute-start.1 = (bf16[256,1152]{1,0:T(8,128)(2,1)}, bf16[256,1152]{1,0:T(8,128)(2,1)S(1)}, u32[]{:S(2)}, u32[]{:S(2)}) collective-permute-start(bf16[256,1152]{1,0:T(8,128)(2,1)} %bitcast.15), channel_id=1, source_target_pairs={{0,2},{1,3},{2,0},{3,1},{4,6},{5,7},{6,4},{7,5},{8,10},{9,11},{10,... | collective-permute-start | bytes 1769480 | tf_op jit(solution)/shard_map/ppermute | solution.py:361
  2.9 1.2 %copy-done.5 = bf16[1152,432]{0,1:T(8,128)(2,1)S(1)} copy-done((bf16[1152,432]{0,1:T(8,128)(2,1)S(1)}, bf16[1152,432]{0,1:T(8,128)(2,1)}, u32[]{:S(2)}) %copy-start.5) | copy-done | bytes 995352
  4.2 1.0 %copy-done.7 = bf16[144,1152]{1,0:T(8,128)(2,1)S(1)} copy-done((bf16[144,1152]{1,0:T(8,128)(2,1)S(1)}, bf16[144,1152]{1,0:T(8,128)(2,1)}, u32[]{:S(2)}) %copy-start.7) | copy-done | bytes 331800
  5.1 0.1 pack.1
  5.2 1.6 %collective-permute-start.2 = (bf16[288,1152]{1,0:T(8,128)(2,1)S(1)}, bf16[288,1152]{1,0:T(8,128)(2,1)S(1)}, u32[]{:S(2)}, u32[]{:S(2)}) collective-permute-start(bf16[288,1152]{1,0:T(8,128)(2,1)S(1)} %get-tuple-element.105.refs_4_), channel_id=1, source_target_pairs={{0,8},{1,5},{2,10},{3,7},{8,16},{9,1},{10,18},{11,3},{16,24},{17,9... | collective-permute-start | bytes 1990664 | tf_op jit(solution)/shard_map/ppermute | solution.py:376
  6.9 1.6 %collective-permute-start.5 = (bf16[288,1152]{1,0:T(8,128)(2,1)S(1)}, bf16[288,1152]{1,0:T(8,128)(2,1)S(1)}, u32[]{:S(2)}, u32[]{:S(2)}) collective-permute-start(bf16[288,1152]{1,0:T(8,128)(2,1)S(1)} %get-tuple-element.119.refs_5_), channel_id=1, source_target_pairs={{0,8},{1,5},{2,10},{3,7},{8,16},{9,1},{10,18},{11,3},{16,24},{17,9... | collective-permute-start | bytes 1990664 | tf_op jit(solution)/shard_map/ppermute | solution.py:376
  8.4 1.6 %copy-done = bf16[1152,864]{0,1:T(8,128)(2,1)S(1)} copy-done((bf16[1152,864]{0,1:T(8,128)(2,1)S(1)}, bf16[1152,864]{0,1:T(8,128)(2,1)}, u32[]{:S(2)}) %copy-start) | copy-done | bytes 1990680
  10.0 1.1 %copy-done.3 = bf16[1,256,1152]{2,1,0:T(8,128)(2,1)S(1)} copy-done((bf16[1,256,1152]{2,1,0:T(8,128)(2,1)S(1)}, bf16[1,256,1152]{2,1,0:T(8,128)(2,1)}, u32[]{:S(2)}) %copy-start.3) | copy-done | bytes 589848
  11.1 0.7 copy-done.8
  11.8 1.2 %spatial_qkv.4 = (bf16[8,80,256]{2,1,0:T(8,128)(2,1)S(1)}, bf16[4,256,80]{2,1,0:T(8,128)(2,1)S(1)}) custom-call(bf16[256,1152]{1,0:T(8,128)(2,1)S(1)} %bitcast.16, f32[3,1152]{1,0:T(4,128)S(1)} %copy-done.8, bf16[864,1152]{1,0:T(8,128)(2,1)S(1)} %bitcast.8), custom_call_target="tpu_custom_call" | custom-call | flops 1 | bytes 1 | tf_op jit(solution)/shard_map/spatial_qkv/pallas_call | solution.py:70
  13.0 0.4 copy-done.1
  13.3 1.2 %spatial_qkv.5 = (bf16[8,80,256]{2,1,0:T(8,128)(2,1)S(1)}, bf16[4,256,80]{2,1,0:T(8,128)(2,1)S(1)}) custom-call(bf16[256,1152]{1,0:T(8,128)(2,1)S(1)} %collective-permute-done.tokens_ref, f32[3,1152]{1,0:T(4,128)S(1)} %copy-done.8, bf16[864,1152]{1,0:T(8,128)(2,1)S(1)} %bitcast.9), custom_call_target="tpu_custom_call" | custom-call | flops 1 | bytes 1 | tf_op jit(solution)/shard_map/spatial_qkv/pallas_call | solution.py:70
  14.5 2.6 %collective-permute-done.1.tokens_ref = bf16[256,1152]{1,0:T(8,128)(2,1)S(1)} collective-permute-done((bf16[256,1152]{1,0:T(8,128)(2,1)}, bf16[256,1152]{1,0:T(8,128)(2,1)S(1)}, u32[]{:S(2)}, u32[]{:S(2)}) %collective-permute-start.1) | collective-permute-done | bytes 589856 | tf_op jit(solution)/shard_map/ppermute | solution.py:361
  17.2 0.0 collective-permute-start.3
  17.2 1.2 %spatial_qkv.6 = (bf16[8,80,256]{2,1,0:T(8,128)(2,1)S(1)}, bf16[4,256,80]{2,1,0:T(8,128)(2,1)S(1)}) custom-call(bf16[256,1152]{1,0:T(8,128)(2,1)S(1)} %collective-permute-done.1.tokens_ref, f32[3,1152]{1,0:T(4,128)S(1)} %copy-done.9, bf16[864,1152]{1,0:T(8,128)(2,1)S(1)} %bitcast.10), custom_call_target="tpu_custom_call" | custom-call | flops 1610612736 | bytes 1 | tf_op jit(solution)/shard_map/spatial_qkv/pallas_call | solution.py:70
  18.3 0.0 collective-permute-done.2.refs_6_
  18.3 1.9 %collective-permute-start.7 = (bf16[288,1152]{1,0:T(8,128)(2,1)S(1)}, bf16[288,1152]{1,0:T(8,128)(2,1)S(1)}, u32[]{:S(2)}, u32[]{:S(2)}) collective-permute-start(bf16[288,1152]{1,0:T(8,128)(2,1)S(1)} %collective-permute-done.2.refs_6_), channel_id=1, source_target_pairs={{0,8},{1,5},{2,10},{3,7},{8,16},{9,1},{10,18},{11,3},{16,24},{17,9... | collective-permute-start | bytes 1990664 | tf_op jit(solution)/shard_map/ppermute | solution.py:376
  20.2 1.2 %spatial_qkv.7 = (bf16[8,80,256]{2,1,0:T(8,128)(2,1)S(1)}, bf16[4,256,80]{2,1,0:T(8,128)(2,1)S(1)}) custom-call(bf16[256,1152]{1,0:T(8,128)(2,1)S(1)} %collective-permute-done.3.tokens_ref, f32[3,1152]{1,0:T(4,128)S(1)} %copy-done.9, bf16[864,1152]{1,0:T(8,128)(2,1)S(1)} %bitcast.11), custom_call_target="tpu_custom_call" | custom-call | flops 1 | bytes 1 | tf_op jit(solution)/shard_map/spatial_qkv/pallas_call | solution.py:70
  21.4 0.0 collective-permute-done.4.other_weight_ref
  21.4 2.3 %spatial_attention.4 = bf16[256,288]{1,0:T(8,128)(2,1)S(1)} custom-call(bf16[8,80,256]{2,1,0:T(8,128)(2,1)S(1)} %get-tuple-element.143.refs_0_.refs_4_, bf16[8,80,256]{2,1,0:T(8,128)(2,1)S(1)} %get-tuple-element.140.refs_1_.refs_0_, bf16[8,80,256]{2,1,0:T(8,128)(2,1)S(1)} %get-tuple-element.141.refs_2_.refs_0_, ...), custom_call_target="tpu_custom_call" | custom-call | flops 1 | bytes 1 | tf_op jit(solution)/shard_map/spatial_attention/pallas_call | solution.py:105
  23.7 0.0 copy-start.2
  23.7 0.0 collective-permute-done.5.refs_7_
  23.7 0.2 collective-permute-start.6
  23.9 2.3 %spatial_attention.5.heads_ref = bf16[256,288]{1,0:T(8,128)(2,1)S(1)} custom-call(bf16[8,80,256]{2,1,0:T(8,128)(2,1)S(1)} %get-tuple-element.142.refs_3_.refs_0_, bf16[8,80,256]{2,1,0:T(8,128)(2,1)S(1)} %get-tuple-element.140.refs_1_.refs_0_, bf16[8,80,256]{2,1,0:T(8,128)(2,1)S(1)} %get-tuple-element.141.refs_2_.refs_0_, ...), custom_call_target="tpu_custom_call" | custom-call | flops 1 | bytes 1 | tf_op jit(solution)/shard_map/spatial_attention/pallas_call | solution.py:105
  26.2 0.0 collective-permute-done.6.other_ref
  26.2 0.8 chip_partial.1
  27.1 1.6 %collective-permute-start.9 = (bf16[256,1152]{1,0:T(8,128)(2,1)S(1)}, bf16[256,1152]{1,0:T(8,128)(2,1)S(1)}, u32[]{:S(2)}, u32[]{:S(2)}) collective-permute-start(bf16[256,1152]{1,0:T(8,128)(2,1)S(1)} %chip_partial.1), channel_id=1, source_target_pairs={{0,2},{1,3},{2,0},{3,1},{4,6},{5,7},{6,4},{7,5},{8,10},{9,11},{10,... | collective-permute-start | bytes 1769480 | tf_op jit(solution)/shard_map/ppermute | solution.py:361
  28.6 2.3 %spatial_attention.6 = bf16[256,288]{1,0:T(8,128)(2,1)S(1)} custom-call(bf16[8,80,256]{2,1,0:T(8,128)(2,1)S(1)} %get-tuple-element.141.refs_2_.refs_0_, bf16[8,80,256]{2,1,0:T(8,128)(2,1)S(1)} %get-tuple-element.140.refs_1_.refs_0_, bf16[8,80,256]{2,1,0:T(8,128)(2,1)S(1)} %get-tuple-element.141.refs_2_.refs_0_, ...), custom_call_target="tpu_custom_call" | custom-call | flops 1 | bytes 1 | tf_op jit(solution)/shard_map/spatial_attention/pallas_call | solution.py:105
  30.9 0.0 copy-start.4
  30.9 1.6 %collective-permute-start.10 = (bf16[288,1152]{1,0:T(8,128)(2,1)S(1)}, bf16[288,1152]{1,0:T(8,128)(2,1)}, u32[]{:S(2)}, u32[]{:S(2)}) collective-permute-start(bf16[288,1152]{1,0:T(8,128)(2,1)S(1)} %collective-permute-done.7.refs_10_), channel_id=1, source_target_pairs={{0,8},{1,5},{2,10},{3,7},{8,16},{9,1},{10,18},{11,3},{16,24},{17,9... | collective-permute-start | bytes 1990664 | tf_op jit(solution)/shard_map/ppermute | solution.py:376
  32.6 2.3 %spatial_attention.7.heads_ref = bf16[256,288]{1,0:T(8,128)(2,1)S(1)} custom-call(bf16[8,80,256]{2,1,0:T(8,128)(2,1)S(1)} %get-tuple-element.140.refs_1_.refs_0_, bf16[8,80,256]{2,1,0:T(8,128)(2,1)S(1)} %get-tuple-element.140.refs_1_.refs_0_, bf16[8,80,256]{2,1,0:T(8,128)(2,1)S(1)} %get-tuple-element.141.refs_2_.refs_0_, ...), custom_call_target="tpu_custom_call" | custom-call | flops 1 | bytes 1 | tf_op jit(solution)/shard_map/spatial_attention/pallas_call | solution.py:105
  34.8 0.1 collective-permute-start.8
  34.9 1.6 %collective-permute-start.14 = (bf16[288,1152]{1,0:T(8,128)(2,1)S(1)}, bf16[288,1152]{1,0:T(8,128)(2,1)}, u32[]{:S(2)}, u32[]{:S(2)}) collective-permute-start(bf16[288,1152]{1,0:T(8,128)(2,1)S(1)} %collective-permute-done.5.refs_7_), channel_id=1, source_target_pairs={{0,8},{1,5},{2,10},{3,7},{8,16},{9,1},{10,18},{11,3},{16,24},{17,9... | collective-permute-start | bytes 1990664 | tf_op jit(solution)/shard_map/ppermute | solution.py:376
  36.6 0.0 collective-permute-done.8.other_ref
  36.6 0.8 spatial_base.1.base_ref
  37.4 0.0 copy-start.10
  37.4 0.1 collective-permute-start.11
  37.5 0.5 collective-permute-start.12
  38.0 4.7 %collective-permute-done.9.refs_0_ = bf16[256,1152]{1,0:T(8,128)(2,1)S(1)} collective-permute-done((bf16[256,1152]{1,0:T(8,128)(2,1)S(1)}, bf16[256,1152]{1,0:T(8,128)(2,1)S(1)}, u32[]{:S(2)}, u32[]{:S(2)}) %collective-permute-start.9) | collective-permute-done | bytes 589856 | tf_op jit(solution)/shard_map/ppermute | solution.py:361
  42.7 0.2 spatial_add.1
  42.9 0.0 copy-start.6
  42.9 0.8 copy-done.6
  43.7 0.0 collective-permute-done.10.refs_14_
  43.7 1.6 %collective-permute-start.19 = (bf16[288,1152]{1,0:T(8,128)(2,1)}, bf16[288,1152]{1,0:T(8,128)(2,1)}, u32[]{:S(2)}, u32[]{:S(2)}) collective-permute-start(bf16[288,1152]{1,0:T(8,128)(2,1)} %collective-permute-done.10.refs_14_), channel_id=1, source_target_pairs={{0,8},{1,5},{2,10},{3,7},{8,16},{9,1},{10,18},{11,3},{16,24},{17,9... | collective-permute-start | bytes 1990664 | tf_op jit(solution)/shard_map/ppermute | solution.py:376
  45.3 1.5 %collective-permute-start.17 = (bf16[288,1152]{1,0:T(8,128)(2,1)}, bf16[288,1152]{1,0:T(8,128)(2,1)}, u32[]{:S(2)}, u32[]{:S(2)}) collective-permute-start(bf16[288,1152]{1,0:T(8,128)(2,1)} %collective-permute-done.10.refs_14_), channel_id=1, source_target_pairs={{0,2},{1,3},{2,0},{3,1},{4,6},{5,7},{6,4},{7,5},{8,10},{9,11},{10,... | collective-permute-start | bytes 1990664 | tf_op jit(solution)/shard_map/ppermute | solution.py:361
  46.8 4.4 %all-to-all-start = ((bf16[8,32,1152]{2,1,0:T(8,128)(2,1)}), bf16[8,32,1152]{2,1,0:T(8,128)(2,1)S(1)}, u32[]{:S(2)}, u32[]{:S(2)}) async-start(bf16[8,32,1152]{2,1,0:T(8,128)(2,1)} %bitcast.19), calls=%async_computation | async-start | bytes 1179648 | tf_op jit(solution)/shard_map/all_to_all | solution.py:388
  51.2 0.1 collective-permute-start.13
  51.3 0.5 collective-permute-start.15
  51.8 0.1 collective-permute-start.16
  51.9 7.1 %collective-permute-done.19.refs_18_ = bf16[288,1152]{1,0:T(8,128)(2,1)} collective-permute-done((bf16[288,1152]{1,0:T(8,128)(2,1)}, bf16[288,1152]{1,0:T(8,128)(2,1)}, u32[]{:S(2)}, u32[]{:S(2)}) %collective-permute-start.19) | collective-permute-done | bytes 663584 | tf_op jit(solution)/shard_map/ppermute | solution.py:376
  58.9 2.1 %collective-permute-done.17.refs_16_ = bf16[288,1152]{1,0:T(8,128)(2,1)} collective-permute-done((bf16[288,1152]{1,0:T(8,128)(2,1)}, bf16[288,1152]{1,0:T(8,128)(2,1)}, u32[]{:S(2)}, u32[]{:S(2)}) %collective-permute-start.17) | collective-permute-done | bytes 663584 | tf_op jit(solution)/shard_map/ppermute | solution.py:361
  61.1 7.5 %all-to-all-done = bf16[8,32,1152]{2,1,0:T(8,128)(2,1)S(1)} async-done(((bf16[8,32,1152]{2,1,0:T(8,128)(2,1)}), bf16[8,32,1152]{2,1,0:T(8,128)(2,1)S(1)}, u32[]{:S(2)}, u32[]{:S(2)}) %all-to-all-start) | async-done | bytes 589856 | tf_op jit(solution)/shard_map/all_to_all | solution.py:388
  68.6 0.4 temporal_norm.1.refs_2_
  69.0 7.7 %temporal_block.1 = (bf16[32,1152]{1,0:T(8,128)(2,1)S(1)}, bf16[32,1152]{1,0:T(8,128)(2,1)S(1)}, bf16[32,1152]{1,0:T(8,128)(2,1)S(1)}, bf16[32,1152]{1,0:T(8,128...) custom-call(s32[1]{0:T(128)} %bitcast.1.refs_0_, ...), custom_call_target="tpu_custom_call" | custom-call | flops 1 | bytes 1 | tf_op jit(solution)/shard_map/temporal_block/pallas_call | solution.py:322
  76.7 2.8 %collective-permute-start.21 = (bf16[32,1152]{1,0:T(8,128)(2,1)S(1)}, bf16[32,1152]{1,0:T(8,128)(2,1)S(1)}, u32[]{:S(2)}, u32[]{:S(2)}) collective-permute-start(bf16[32,1152]{1,0:T(8,128)(2,1)S(1)} %get-tuple-element.162), channel_id=1, source_target_pairs={{0,4},{4,0},{8,12},{12,8},{16,20},{20,16},{24,28},{28,24},{1,5},{5... | collective-permute-start | bytes 221192 | tf_op jit(solution)/shard_map/ppermute | solution.py:365
  79.5 2.0 %collective-permute-start.23 = (bf16[32,1152]{1,0:T(8,128)(2,1)S(1)}, bf16[32,1152]{1,0:T(8,128)(2,1)S(1)}, u32[]{:S(2)}, u32[]{:S(2)}) collective-permute-start(bf16[32,1152]{1,0:T(8,128)(2,1)S(1)} %get-tuple-element.164), channel_id=1, source_target_pairs={{0,8},{4,12},{8,0},{12,4},{16,24},{20,28},{24,16},{28,20},{1,9},{5... | collective-permute-start | bytes 221192 | tf_op jit(solution)/shard_map/ppermute | solution.py:365
  81.5 1.6 %collective-permute-start.24 = (bf16[32,1152]{1,0:T(8,128)(2,1)S(1)}, bf16[32,1152]{1,0:T(8,128)(2,1)S(1)}, u32[]{:S(2)}, u32[]{:S(2)}) collective-permute-start(bf16[32,1152]{1,0:T(8,128)(2,1)S(1)} %get-tuple-element.165), channel_id=1, source_target_pairs={{0,20},{4,16},{8,28},{12,24},{16,4},{20,0},{24,12},{28,8},{1,21},{... | collective-permute-start | bytes 221192 | tf_op jit(solution)/shard_map/ppermute | solution.py:365
  83.1 1.5 %collective-permute-start.25 = (bf16[32,1152]{1,0:T(8,128)(2,1)S(1)}, bf16[32,1152]{1,0:T(8,128)(2,1)S(1)}, u32[]{:S(2)}, u32[]{:S(2)}) collective-permute-start(bf16[32,1152]{1,0:T(8,128)(2,1)S(1)} %get-tuple-element.166), channel_id=1, source_target_pairs={{0,24},{4,28},{8,16},{12,20},{16,8},{20,12},{24,0},{28,4},{1,25},{... | collective-permute-start | bytes 221192 | tf_op jit(solution)/shard_map/ppermute | solution.py:365
  84.7 2.5 %collective-permute-start.26 = (bf16[32,1152]{1,0:T(8,128)(2,1)S(1)}, bf16[32,1152]{1,0:T(8,128)(2,1)S(1)}, u32[]{:S(2)}, u32[]{:S(2)}) collective-permute-start(bf16[32,1152]{1,0:T(8,128)(2,1)S(1)} %get-tuple-element.167), channel_id=1, source_target_pairs={{0,28},{4,24},{8,20},{12,16},{16,12},{20,8},{24,4},{28,0},{1,29},{... | collective-permute-start | bytes 221192 | tf_op jit(solution)/shard_map/ppermute | solution.py:365
  87.2 0.7 collective-permute-done.22.refs_3_
  87.9 4.2 %collective-permute-done.24.refs_5_ = bf16[32,1152]{1,0:T(8,128)(2,1)S(1)} collective-permute-done((bf16[32,1152]{1,0:T(8,128)(2,1)S(1)}, bf16[32,1152]{1,0:T(8,128)(2,1)S(1)}, u32[]{:S(2)}, u32[]{:S(2)}) %collective-permute-start.24) | collective-permute-done | bytes 73760 | tf_op jit(solution)/shard_map/ppermute | solution.py:365
  92.1 1.1 %collective-permute-done.27.refs_8_ = bf16[32,1152]{1,0:T(8,128)(2,1)S(1)} collective-permute-done((bf16[32,1152]{1,0:T(8,128)(2,1)S(1)}, bf16[32,1152]{1,0:T(8,128)(2,1)S(1)}, u32[]{:S(2)}, u32[]{:S(2)}) %collective-permute-start.27) | collective-permute-done | bytes 73760 | tf_op jit(solution)/shard_map/ppermute | solution.py:365
  93.2 0.9 join_frames.1
  (33 shorter events, 0.1 us)
Async XLA Ops:
  0.0 13.0 %collective-permute-start = (bf16[256,1152]{1,0:T(8,128)(2,1)}, bf16[256,1152]{1,0:T(8,128)(2,1)S(1)}, u32[]{:S(2)}, u32[]{:S(2)}) collective-permute-start(bf16[256,1152]{1,0:T(8,128)(2,1)} %bitcast.14), channel_id=1, source_target_pairs={{0,1},{1,0},{2,3},{3,2},{4,5},{5,4},{6,7},{7,6},{8,9},{9,8},{10,11... | collective-permute-start | bytes 1769480 | tf_op jit(solution)/shard_map/ppermute | solution.py:361
  0.5 16.7 %collective-permute-start.1 = (bf16[256,1152]{1,0:T(8,128)(2,1)}, bf16[256,1152]{1,0:T(8,128)(2,1)S(1)}, u32[]{:S(2)}, u32[]{:S(2)}) collective-permute-start(bf16[256,1152]{1,0:T(8,128)(2,1)} %bitcast.15), channel_id=1, source_target_pairs={{0,2},{1,3},{2,0},{3,1},{4,6},{5,7},{6,4},{7,5},{8,10},{9,11},{10,... | collective-permute-start | bytes 1769480 | tf_op jit(solution)/shard_map/ppermute | solution.py:361
  2.9 1.2 %copy-start.5 = (bf16[1152,432]{0,1:T(8,128)(2,1)S(1)}, bf16[1152,432]{0,1:T(8,128)(2,1)}, u32[]{:S(2)}) copy-start(bf16[1152,432]{0,1:T(8,128)(2,1)} %param.12) | copy-start | bytes 2985988
  4.1 1.0 %copy-start.7 = (bf16[144,1152]{1,0:T(8,128)(2,1)S(1)}, bf16[144,1152]{1,0:T(8,128)(2,1)}, u32[]{:S(2)}) copy-start(bf16[144,1152]{1,0:T(8,128)(2,1)} %out_ref.1) | copy-start | bytes 995332
  5.2 13.1 %collective-permute-start.2 = (bf16[288,1152]{1,0:T(8,128)(2,1)S(1)}, bf16[288,1152]{1,0:T(8,128)(2,1)S(1)}, u32[]{:S(2)}, u32[]{:S(2)}) collective-permute-start(bf16[288,1152]{1,0:T(8,128)(2,1)S(1)} %get-tuple-element.105.refs_4_), channel_id=1, source_target_pairs={{0,8},{1,5},{2,10},{3,7},{8,16},{9,1},{10,18},{11,3},{16,24},{17,9... | collective-permute-start | bytes 1990664 | tf_op jit(solution)/shard_map/ppermute | solution.py:376
  6.9 14.5 %collective-permute-start.4 = (bf16[288,1152]{1,0:T(8,128)(2,1)}, bf16[288,1152]{1,0:T(8,128)(2,1)S(1)}, u32[]{:S(2)}, u32[]{:S(2)}) collective-permute-start(bf16[288,1152]{1,0:T(8,128)(2,1)} %weight_ref.3), channel_id=1, source_target_pairs={{0,1},{1,0},{2,3},{3,2},{4,5},{5,4},{6,7},{7,6},{8,9},{9,8},{10,11... | collective-permute-start | bytes 1990664 | tf_op jit(solution)/shard_map/ppermute | solution.py:361
  6.9 16.8 %collective-permute-start.5 = (bf16[288,1152]{1,0:T(8,128)(2,1)S(1)}, bf16[288,1152]{1,0:T(8,128)(2,1)S(1)}, u32[]{:S(2)}, u32[]{:S(2)}) collective-permute-start(bf16[288,1152]{1,0:T(8,128)(2,1)S(1)} %get-tuple-element.119.refs_5_), channel_id=1, source_target_pairs={{0,8},{1,5},{2,10},{3,7},{8,16},{9,1},{10,18},{11,3},{16,24},{17,9... | collective-permute-start | bytes 1990664 | tf_op jit(solution)/shard_map/ppermute | solution.py:376
  8.4 1.6 %copy-start = (bf16[1152,864]{0,1:T(8,128)(2,1)S(1)}, bf16[1152,864]{0,1:T(8,128)(2,1)}, u32[]{:S(2)}) copy-start(bf16[1152,864]{0,1:T(8,128)(2,1)} %param.9) | copy-start | bytes 5971972
  10.0 1.1 %copy-start.3 = (bf16[1,256,1152]{2,1,0:T(8,128)(2,1)S(1)}, bf16[1,256,1152]{2,1,0:T(8,128)(2,1)}, u32[]{:S(2)}) copy-start(bf16[1,256,1152]{2,1,0:T(8,128)(2,1)} %param.7) | copy-start | bytes 1769476
  11.1 0.7 copy-start.8
  11.8 1.6 %copy-start.1 = (bf16[1152,864]{0,1:T(8,128)(2,1)S(1)}, bf16[1152,864]{0,1:T(8,128)(2,1)}, u32[]{:S(2)}) copy-start(bf16[1152,864]{0,1:T(8,128)(2,1)} %param.9) | copy-start | bytes 5971972
  11.8 5.4 %copy-start.9 = (f32[3,1152]{1,0:T(4,128)S(1)}, f32[3,1152]{1,0:T(4,128)}, u32[]{:S(2)}) copy-start(f32[3,1152]{1,0:T(4,128)} %mod_ref.11) | copy-start | bytes 41476
  17.2 3.1 %collective-permute-start.3 = (bf16[256,1152]{1,0:T(8,128)(2,1)S(1)}, bf16[256,1152]{1,0:T(8,128)(2,1)S(1)}, u32[]{:S(2)}, u32[]{:S(2)}) collective-permute-start(bf16[256,1152]{1,0:T(8,128)(2,1)S(1)} %collective-permute-done.1.tokens_ref), channel_id=1, source_target_pairs={{0,1},{1,0},{2,3},{3,2},{4,5},{5,4},{6,7},{7,6},{8,9},{9,8},{10,11... | collective-permute-start | bytes 1769480 | tf_op jit(solution)/shard_map/ppermute | solution.py:361
  18.3 12.6 %collective-permute-start.7 = (bf16[288,1152]{1,0:T(8,128)(2,1)S(1)}, bf16[288,1152]{1,0:T(8,128)(2,1)S(1)}, u32[]{:S(2)}, u32[]{:S(2)}) collective-permute-start(bf16[288,1152]{1,0:T(8,128)(2,1)S(1)} %collective-permute-done.2.refs_6_), channel_id=1, source_target_pairs={{0,8},{1,5},{2,10},{3,7},{8,16},{9,1},{10,18},{11,3},{16,24},{17,9... | collective-permute-start | bytes 1990664 | tf_op jit(solution)/shard_map/ppermute | solution.py:376
  23.7 2.5 %copy-start.2 = (bf16[288,1152]{1,0:T(8,128)(2,1)S(1)}, bf16[288,1152]{1,0:T(8,128)(2,1)}, u32[]{:S(2)}) copy-start(bf16[288,1152]{1,0:T(8,128)(2,1)} %weight_ref.3) | copy-start | bytes 1990660
  23.7 2.5 %collective-permute-start.6 = (bf16[256,288]{1,0:T(8,128)(2,1)S(1)}, bf16[256,288]{1,0:T(8,128)(2,1)S(1)}, u32[]{:S(2)}, u32[]{:S(2)}) collective-permute-start(bf16[256,288]{1,0:T(8,128)(2,1)S(1)} %spatial_attention.4), channel_id=1, source_target_pairs={{0,1},{1,0},{2,3},{3,2},{4,5},{5,4},{6,7},{7,6},{8,9},{9,8},{10,11... | collective-permute-start | bytes 442376 | tf_op jit(solution)/shard_map/ppermute | solution.py:361
  27.1 15.6 %collective-permute-start.9 = (bf16[256,1152]{1,0:T(8,128)(2,1)S(1)}, bf16[256,1152]{1,0:T(8,128)(2,1)S(1)}, u32[]{:S(2)}, u32[]{:S(2)}) collective-permute-start(bf16[256,1152]{1,0:T(8,128)(2,1)S(1)} %chip_partial.1), channel_id=1, source_target_pairs={{0,2},{1,3},{2,0},{3,1},{4,6},{5,7},{6,4},{7,5},{8,10},{9,11},{10,... | collective-permute-start | bytes 1769480 | tf_op jit(solution)/shard_map/ppermute | solution.py:361
  30.9 5.6 %copy-start.4 = (bf16[1,256,1152]{2,1,0:T(8,128)(2,1)S(1)}, bf16[1,256,1152]{2,1,0:T(8,128)(2,1)}, u32[]{:S(2)}) copy-start(bf16[1,256,1152]{2,1,0:T(8,128)(2,1)} %param.7) | copy-start | bytes 1769476
  30.9 6.5 %copy-start.11 = (bf16[288,1152]{1,0:T(8,128)(2,1)}, bf16[288,1152]{1,0:T(8,128)(2,1)S(1)}, u32[]{:S(2)}) copy-start(bf16[288,1152]{1,0:T(8,128)(2,1)S(1)} %collective-permute-done.7.refs_10_) | copy-start | bytes 1990660
  30.9 12.8 %collective-permute-start.10 = (bf16[288,1152]{1,0:T(8,128)(2,1)S(1)}, bf16[288,1152]{1,0:T(8,128)(2,1)}, u32[]{:S(2)}, u32[]{:S(2)}) collective-permute-start(bf16[288,1152]{1,0:T(8,128)(2,1)S(1)} %collective-permute-done.7.refs_10_), channel_id=1, source_target_pairs={{0,8},{1,5},{2,10},{3,7},{8,16},{9,1},{10,18},{11,3},{16,24},{17,9... | collective-permute-start | bytes 1990664 | tf_op jit(solution)/shard_map/ppermute | solution.py:376
  34.8 1.7 %collective-permute-start.8 = (bf16[256,288]{1,0:T(8,128)(2,1)S(1)}, bf16[256,288]{1,0:T(8,128)(2,1)S(1)}, u32[]{:S(2)}, u32[]{:S(2)}) collective-permute-start(bf16[256,288]{1,0:T(8,128)(2,1)S(1)} %spatial_attention.6), channel_id=1, source_target_pairs={{0,1},{1,0},{2,3},{3,2},{4,5},{5,4},{6,7},{7,6},{8,9},{9,8},{10,11... | collective-permute-start | bytes 442376 | tf_op jit(solution)/shard_map/ppermute | solution.py:361
  34.9 16.3 %collective-permute-start.14 = (bf16[288,1152]{1,0:T(8,128)(2,1)S(1)}, bf16[288,1152]{1,0:T(8,128)(2,1)}, u32[]{:S(2)}, u32[]{:S(2)}) collective-permute-start(bf16[288,1152]{1,0:T(8,128)(2,1)S(1)} %collective-permute-done.5.refs_7_), channel_id=1, source_target_pairs={{0,8},{1,5},{2,10},{3,7},{8,16},{9,1},{10,18},{11,3},{16,24},{17,9... | collective-permute-start | bytes 1990664 | tf_op jit(solution)/shard_map/ppermute | solution.py:376
  37.4 31.1 %copy-start.10 = (f32[3,1152]{1,0:T(4,128)S(1)}, f32[3,1152]{1,0:T(4,128)}, u32[]{:S(2)}) copy-start(f32[3,1152]{1,0:T(4,128)} %refs_3_.1) | copy-start | bytes 41476
  37.4 13.9 %collective-permute-start.11 = (bf16[288,1152]{1,0:T(8,128)(2,1)S(1)}, bf16[288,1152]{1,0:T(8,128)(2,1)}, u32[]{:S(2)}, u32[]{:S(2)}) collective-permute-start(bf16[288,1152]{1,0:T(8,128)(2,1)S(1)} %collective-permute-done.2.refs_6_), channel_id=1, source_target_pairs={{0,1},{1,0},{2,3},{3,2},{4,5},{5,4},{6,7},{7,6},{8,9},{9,8},{10,11... | collective-permute-start | bytes 1990664 | tf_op jit(solution)/shard_map/ppermute | solution.py:361
  37.5 14.3 %collective-permute-start.12 = (bf16[288,1152]{1,0:T(8,128)(2,1)S(1)}, bf16[288,1152]{1,0:T(8,128)(2,1)}, u32[]{:S(2)}, u32[]{:S(2)}) collective-permute-start(bf16[288,1152]{1,0:T(8,128)(2,1)S(1)} %collective-permute-done.5.refs_7_), channel_id=1, source_target_pairs={{0,1},{1,0},{2,3},{3,2},{4,5},{5,4},{6,7},{7,6},{8,9},{9,8},{10,11... | collective-permute-start | bytes 1990664 | tf_op jit(solution)/shard_map/ppermute | solution.py:361
  42.9 0.8 copy-start.6
  43.7 15.2 %collective-permute-start.19 = (bf16[288,1152]{1,0:T(8,128)(2,1)}, bf16[288,1152]{1,0:T(8,128)(2,1)}, u32[]{:S(2)}, u32[]{:S(2)}) collective-permute-start(bf16[288,1152]{1,0:T(8,128)(2,1)} %collective-permute-done.10.refs_14_), channel_id=1, source_target_pairs={{0,8},{1,5},{2,10},{3,7},{8,16},{9,1},{10,18},{11,3},{16,24},{17,9... | collective-permute-start | bytes 1990664 | tf_op jit(solution)/shard_map/ppermute | solution.py:376
  45.3 15.8 %collective-permute-start.17 = (bf16[288,1152]{1,0:T(8,128)(2,1)}, bf16[288,1152]{1,0:T(8,128)(2,1)}, u32[]{:S(2)}, u32[]{:S(2)}) collective-permute-start(bf16[288,1152]{1,0:T(8,128)(2,1)} %collective-permute-done.10.refs_14_), channel_id=1, source_target_pairs={{0,2},{1,3},{2,0},{3,1},{4,6},{5,7},{6,4},{7,5},{8,10},{9,11},{10,... | collective-permute-start | bytes 1990664 | tf_op jit(solution)/shard_map/ppermute | solution.py:361
  46.8 21.8 %all-to-all-start = ((bf16[8,32,1152]{2,1,0:T(8,128)(2,1)}), bf16[8,32,1152]{2,1,0:T(8,128)(2,1)S(1)}, u32[]{:S(2)}, u32[]{:S(2)}) async-start(bf16[8,32,1152]{2,1,0:T(8,128)(2,1)} %bitcast.19), calls=%async_computation | async-start | bytes 1179648 | tf_op jit(solution)/shard_map/all_to_all | solution.py:388
  51.2 17.8 %collective-permute-start.13 = (bf16[288,1152]{1,0:T(8,128)(2,1)}, bf16[288,1152]{1,0:T(8,128)(2,1)}, u32[]{:S(2)}, u32[]{:S(2)}) collective-permute-start(bf16[288,1152]{1,0:T(8,128)(2,1)} %copy-done.11), channel_id=1, source_target_pairs={{0,1},{1,0},{2,3},{3,2},{4,5},{5,4},{6,7},{7,6},{8,9},{9,8},{10,11... | collective-permute-start | bytes 1990664 | tf_op jit(solution)/shard_map/ppermute | solution.py:361
  51.3 17.7 %collective-permute-start.15 = (bf16[288,1152]{1,0:T(8,128)(2,1)}, bf16[288,1152]{1,0:T(8,128)(2,1)}, u32[]{:S(2)}, u32[]{:S(2)}) collective-permute-start(bf16[288,1152]{1,0:T(8,128)(2,1)} %collective-permute-done.14.refs_12_), channel_id=1, source_target_pairs={{0,1},{1,0},{2,3},{3,2},{4,5},{5,4},{6,7},{7,6},{8,9},{9,8},{10,11... | collective-permute-start | bytes 1990664 | tf_op jit(solution)/shard_map/ppermute | solution.py:361
  51.8 17.2 %collective-permute-start.16 = (bf16[288,1152]{1,0:T(8,128)(2,1)}, bf16[288,1152]{1,0:T(8,128)(2,1)}, u32[]{:S(2)}, u32[]{:S(2)}) collective-permute-start(bf16[288,1152]{1,0:T(8,128)(2,1)} %collective-permute-done.10.refs_14_), channel_id=1, source_target_pairs={{0,1},{1,0},{2,3},{3,2},{4,5},{5,4},{6,7},{7,6},{8,9},{9,8},{10,11... | collective-permute-start | bytes 1990664 | tf_op jit(solution)/shard_map/ppermute | solution.py:361
  58.9 10.1 %collective-permute-start.20 = (bf16[288,1152]{1,0:T(8,128)(2,1)}, bf16[288,1152]{1,0:T(8,128)(2,1)}, u32[]{:S(2)}, u32[]{:S(2)}) collective-permute-start(bf16[288,1152]{1,0:T(8,128)(2,1)} %collective-permute-done.19.refs_18_), channel_id=1, source_target_pairs={{0,1},{1,0},{2,3},{3,2},{4,5},{5,4},{6,7},{7,6},{8,9},{9,8},{10,11... | collective-permute-start | bytes 1990664 | tf_op jit(solution)/shard_map/ppermute | solution.py:361
  61.1 8.0 %collective-permute-start.18 = (bf16[288,1152]{1,0:T(8,128)(2,1)}, bf16[288,1152]{1,0:T(8,128)(2,1)}, u32[]{:S(2)}, u32[]{:S(2)}) collective-permute-start(bf16[288,1152]{1,0:T(8,128)(2,1)} %collective-permute-done.17.refs_16_), channel_id=1, source_target_pairs={{0,1},{1,0},{2,3},{3,2},{4,5},{5,4},{6,7},{7,6},{8,9},{9,8},{10,11... | collective-permute-start | bytes 1990664 | tf_op jit(solution)/shard_map/ppermute | solution.py:361
  76.7 7.9 %collective-permute-start.21 = (bf16[32,1152]{1,0:T(8,128)(2,1)S(1)}, bf16[32,1152]{1,0:T(8,128)(2,1)S(1)}, u32[]{:S(2)}, u32[]{:S(2)}) collective-permute-start(bf16[32,1152]{1,0:T(8,128)(2,1)S(1)} %get-tuple-element.162), channel_id=1, source_target_pairs={{0,4},{4,0},{8,12},{12,8},{16,20},{20,16},{24,28},{28,24},{1,5},{5... | collective-permute-start | bytes 221192 | tf_op jit(solution)/shard_map/ppermute | solution.py:365
  79.5 8.4 %collective-permute-start.22 = (bf16[32,1152]{1,0:T(8,128)(2,1)S(1)}, bf16[32,1152]{1,0:T(8,128)(2,1)S(1)}, u32[]{:S(2)}, u32[]{:S(2)}) collective-permute-start(bf16[32,1152]{1,0:T(8,128)(2,1)S(1)} %get-tuple-element.163), channel_id=1, source_target_pairs={{0,16},{4,20},{8,24},{12,28},{16,0},{20,4},{24,8},{28,12},{1,17},{... | collective-permute-start | bytes 221192 | tf_op jit(solution)/shard_map/ppermute | solution.py:365
  79.5 8.4 %collective-permute-start.23 = (bf16[32,1152]{1,0:T(8,128)(2,1)S(1)}, bf16[32,1152]{1,0:T(8,128)(2,1)S(1)}, u32[]{:S(2)}, u32[]{:S(2)}) collective-permute-start(bf16[32,1152]{1,0:T(8,128)(2,1)S(1)} %get-tuple-element.164), channel_id=1, source_target_pairs={{0,8},{4,12},{8,0},{12,4},{16,24},{20,28},{24,16},{28,20},{1,9},{5... | collective-permute-start | bytes 221192 | tf_op jit(solution)/shard_map/ppermute | solution.py:365
  81.5 10.6 %collective-permute-start.24 = (bf16[32,1152]{1,0:T(8,128)(2,1)S(1)}, bf16[32,1152]{1,0:T(8,128)(2,1)S(1)}, u32[]{:S(2)}, u32[]{:S(2)}) collective-permute-start(bf16[32,1152]{1,0:T(8,128)(2,1)S(1)} %get-tuple-element.165), channel_id=1, source_target_pairs={{0,20},{4,16},{8,28},{12,24},{16,4},{20,0},{24,12},{28,8},{1,21},{... | collective-permute-start | bytes 221192 | tf_op jit(solution)/shard_map/ppermute | solution.py:365
  83.1 9.0 %collective-permute-start.25 = (bf16[32,1152]{1,0:T(8,128)(2,1)S(1)}, bf16[32,1152]{1,0:T(8,128)(2,1)S(1)}, u32[]{:S(2)}, u32[]{:S(2)}) collective-permute-start(bf16[32,1152]{1,0:T(8,128)(2,1)S(1)} %get-tuple-element.166), channel_id=1, source_target_pairs={{0,24},{4,28},{8,16},{12,20},{16,8},{20,12},{24,0},{28,4},{1,25},{... | collective-permute-start | bytes 221192 | tf_op jit(solution)/shard_map/ppermute | solution.py:365
  84.7 7.4 %collective-permute-start.26 = (bf16[32,1152]{1,0:T(8,128)(2,1)S(1)}, bf16[32,1152]{1,0:T(8,128)(2,1)S(1)}, u32[]{:S(2)}, u32[]{:S(2)}) collective-permute-start(bf16[32,1152]{1,0:T(8,128)(2,1)S(1)} %get-tuple-element.167), channel_id=1, source_target_pairs={{0,28},{4,24},{8,20},{12,16},{16,12},{20,8},{24,4},{28,0},{1,29},{... | collective-permute-start | bytes 221192 | tf_op jit(solution)/shard_map/ppermute | solution.py:365
  87.9 5.3 %collective-permute-start.27 = (bf16[32,1152]{1,0:T(8,128)(2,1)S(1)}, bf16[32,1152]{1,0:T(8,128)(2,1)S(1)}, u32[]{:S(2)}, u32[]{:S(2)}) collective-permute-start(bf16[32,1152]{1,0:T(8,128)(2,1)S(1)} %get-tuple-element.168), channel_id=1, source_target_pairs={{0,12},{4,8},{8,4},{12,0},{16,28},{20,24},{24,20},{28,16},{1,13},{... | collective-permute-start | bytes 221192 | tf_op jit(solution)/shard_map/ppermute | solution.py:365
